TPU v7x, 32 devices: a whole 2x2x4 slice. The times are simulated.
32 devices in a mesh: seq: 8 (over y, x, core), fsdp: 4 (over z).
Axes of the slice: x: 2, y: 2, z: 4, core: 2. Of those that a mesh axis runs over, the one named last changes fastest.
Arguments:
- tokens: bfloat16 [4, 2048, 1152], P('fsdp', 'seq'), may hold values from -6 to 6
- cotangent: bfloat16 [4, 2048, 1152], P('fsdp', 'seq'), may hold values from -6 to 6
- doc_lengths: int32 [4, 3], P('fsdp'), may hold values from 682 to 684, as said below
- true_counts: int32 [4, 3], P('fsdp'), may hold values from 512 to 684, as said below
- w_query: bfloat16 [1152, 1024], P(('seq', 'fsdp')), may hold values from -0.1875 to 0.1875
- w_key: bfloat16 [1152, 256], P(('seq', 'fsdp')), may hold values from -0.1875 to 0.1875
- w_value: bfloat16 [1152, 256], P(('seq', 'fsdp')), may hold values from -0.1875 to 0.1875
- w_out: bfloat16 [1152, 1024], P(('seq', 'fsdp')), may hold values from -0.1875 to 0.1875
- w_gate: bfloat16 [1152, 6912], P('seq', 'fsdp'), may hold values from -0.1875 to 0.1875
- w_up: bfloat16 [1152, 6912], P('seq', 'fsdp'), may hold values from -0.1875 to 0.1875
- w_down: bfloat16 [1152, 6912], P('seq', 'fsdp'), may hold values from -0.078125 to 0.078125
- attn_norm_gain: bfloat16 [1152], P(('seq', 'fsdp')), may hold values from 0.5 to 1.5
- query_gain: bfloat16 [256], P(('seq', 'fsdp')), may hold values from 0.5 to 1.5
- key_gain: bfloat16 [256], P(('seq', 'fsdp')), may hold values from 0.5 to 1.5
- attn_post_gain: bfloat16 [1152], P(('seq', 'fsdp')), may hold values from 0.5 to 1.5
- ffn_norm_gain: bfloat16 [1152], P(('seq', 'fsdp')), may hold values from 0.5 to 1.5
- ffn_post_gain: bfloat16 [1152], P(('seq', 'fsdp')), may hold values from 0.5 to 1.5
Outputs:
- output: bfloat16 [4, 2048, 1152], P('fsdp', 'seq')
- input_grad: float32 [4, 2048, 1152], P('fsdp', 'seq')
- grad_query: float32 [1152, 1024], P(('seq', 'fsdp'))
- grad_key: float32 [1152, 256], P(('seq', 'fsdp'))
- grad_value: float32 [1152, 256], P(('seq', 'fsdp'))
- grad_out: float32 [1152, 1024], P(('seq', 'fsdp'))
- grad_gate: float32 [1152, 6912], P('seq', 'fsdp')
- grad_up: float32 [1152, 6912], P('seq', 'fsdp')
- grad_down: float32 [1152, 6912], P('seq', 'fsdp')
- grad_attn_norm: float32 [1152], P(('seq', 'fsdp'))
- grad_query_gain: float32 [256], P(('seq', 'fsdp'))
- grad_key_gain: float32 [256], P(('seq', 'fsdp'))
- grad_attn_post: float32 [1152], P(('seq', 'fsdp'))
- grad_ffn_norm: float32 [1152], P(('seq', 'fsdp'))
- grad_ffn_post: float32 [1152], P(('seq', 'fsdp'))
Inputs may be any that keep to these rules, and one draw needn't show every extreme that they name: `doc_lengths`: row g gives the slot lengths of the 3 documents of group g, laid end to end in order; each row sums to 2048. In each group one document has the least length and one has the greatest. true_counts[g, k] is the number of real tokens of document k of group g; its first doc_lengths[g, k] - true_counts[g, k] slots are padding, at most min(doc_lengths[g, k] // 4, 256) of them.
All inputs are finite; a program needn't handle non-finite values.
Results may differ from a plain program's by a relative error of at most 0.02.
Values may be sent and summed in bfloat16 or wider, within the bound.
No kernel may reach another device: no remote copies, remote signals or barrier semaphores. Data moves between devices by JAX's collectives and lax.ppermute only.
A program may use at most 128 MiB of HBM per device.

v0:
```python
import jax
import jax.numpy as jnp
from jax import lax
from jax.sharding import PartitionSpec as P

WINDOW = 512


NORM_EPS = 1e-06
ROPE_BASE = 10000.0
NEGATIVE = -1e30


def from_behind(value, axis, steps):
    count = lax.axis_size(axis)
    first, last = (max(0, -steps), min(count, count - steps))
    return lax.ppermute(value, axis, [(source, source + steps) for source in range(first, last)])


def matmul(left_side, right_side):
    return jnp.dot(left_side, right_side, preferred_element_type=jnp.float32)


def matmul_t(left_side, right_side):
    return lax.dot_general(
        left_side, right_side, (((1,), (1,)), ((), ())), preferred_element_type=jnp.float32
    )


def matmul_tn(left_side, right_side):
    return lax.dot_general(
        left_side, right_side, (((0,), (0,)), ((), ())), preferred_element_type=jnp.float32
    )


def scaled_norm(values, gain_vec):
    return (
        values * lax.rsqrt(jnp.mean(values * values, axis=-1, keepdims=True) + NORM_EPS) * gain_vec
    )


def rotate(values, position):
    half_dim = values.shape[-1] // 2
    frequency = ROPE_BASE ** (-2.0 * jnp.arange(half_dim, dtype=jnp.float32) / values.shape[-1])
    angles = position.astype(jnp.float32)[..., None] * frequency
    first_half = values[..., :half_dim]
    second_half = values[..., half_dim:]
    cosine = jnp.cos(angles)
    sine_part = jnp.sin(angles)
    return jnp.concatenate(
        [
            first_half * cosine - second_half * sine_part,
            second_half * cosine + first_half * sine_part,
        ],
        axis=-1,
    )


def layout(lengths, counts, first_slot, row_count):
    starts = jnp.cumsum(lengths) - lengths
    slot_index = first_slot + jnp.arange(row_count, dtype=jnp.int32)
    member = (slot_index[:, None] >= starts[None, :]).astype(jnp.int32)
    document = jnp.sum(member, axis=1) - 1
    onehot = (document[:, None] == jnp.arange(lengths.shape[0], dtype=jnp.int32)[None, :]).astype(
        jnp.int32
    )
    position = slot_index - jnp.sum(onehot * starts[None, :], axis=1)
    padded = jnp.sum(onehot * (lengths - counts)[None, :], axis=1)
    return (position, padded)


def visible(position, padded, distance):
    query_pos = position[:, None]
    return (
        (distance >= 0)
        & (distance < WINDOW)
        & (distance <= query_pos)
        & ((query_pos - distance >= padded[:, None]) | (distance == 0))
    )


def block_scores(query_block, key_block, row_pos, row_pad, distance, score_scale):
    raw_scores = jnp.einsum(
        "qhd,kd->hqk", query_block, key_block, preferred_element_type=jnp.float32
    )
    return jnp.where(visible(row_pos, row_pad, distance)[None], raw_scores * score_scale, NEGATIVE)


def on_device(
    tokens,
    cotangent,
    doc_lengths,
    true_counts,
    w_query,
    w_key,
    w_value,
    w_out,
    w_gate,
    w_up,
    w_down,
    attn_norm_gain,
    query_gain,
    key_gain,
    attn_post_gain,
    ffn_norm_gain,
    ffn_post_gain,
):
    row_count = tokens.shape[1]
    head_dim = w_key.shape[1]
    heads_width = w_query.shape[1]
    head_count = heads_width // head_dim
    score_scale = head_dim ** (-0.5)
    hop_count = (WINDOW + row_count - 1) // row_count
    block_rows = min(512, row_count)
    inputs = tokens[0].astype(jnp.float32)
    upstream = cotangent[0].astype(jnp.float32)
    position, padded = layout(
        doc_lengths[0], true_counts[0], lax.axis_index("seq") * row_count, row_count
    )
    gathered = (
        lax.all_gather(w_query, ("seq", "fsdp"), axis=0, tiled=True),
        lax.all_gather(w_key, ("seq", "fsdp"), axis=0, tiled=True),
        lax.all_gather(w_value, ("seq", "fsdp"), axis=0, tiled=True),
        lax.all_gather(w_out, ("seq", "fsdp"), axis=0, tiled=True),
        lax.all_gather(attn_norm_gain, ("seq", "fsdp"), axis=0, tiled=True),
        lax.all_gather(query_gain, ("seq", "fsdp"), axis=0, tiled=True),
        lax.all_gather(key_gain, ("seq", "fsdp"), axis=0, tiled=True),
        lax.all_gather(attn_post_gain, ("seq", "fsdp"), axis=0, tiled=True),
        lax.all_gather(ffn_norm_gain, ("seq", "fsdp"), axis=0, tiled=True),
        lax.all_gather(ffn_post_gain, ("seq", "fsdp"), axis=0, tiled=True),
    )
    wq_full, wk_full, wv_full, wo_full = (gathered[0], gathered[1], gathered[2], gathered[3])
    gain_an = gathered[4].astype(jnp.float32)
    gain_q = gathered[5].astype(jnp.float32)
    gain_k = gathered[6].astype(jnp.float32)
    gain_ap = gathered[7].astype(jnp.float32)
    gain_fn = gathered[8].astype(jnp.float32)
    gain_fp = gathered[9].astype(jnp.float32)
    gate_part, up_part, down_part = (w_gate, w_up, w_down)
    wg_full, wu_full, wd_full = (
        lax.all_gather(gate_part, "seq", axis=0, tiled=True),
        lax.all_gather(up_part, "seq", axis=0, tiled=True),
        lax.all_gather(down_part, "seq", axis=0, tiled=True),
    )
    attn_in_f, an_pull = jax.vjp(scaled_norm, inputs, gain_an)
    attn_in = attn_in_f.astype(jnp.bfloat16)
    query_lin = matmul(attn_in, wq_full).reshape(row_count, head_count, head_dim)
    key_lin = matmul(attn_in, wk_full)
    values = matmul(attn_in, wv_full).astype(jnp.bfloat16)
    query_rot, q_pull = jax.vjp(
        lambda lin_part, gain_vec: rotate(scaled_norm(lin_part, gain_vec), position[:, None]),
        query_lin,
        gain_q,
    )
    key_rot, k_pull = jax.vjp(
        lambda lin_part, gain_vec: rotate(scaled_norm(lin_part, gain_vec), position),
        key_lin,
        gain_k,
    )
    queries = query_rot.astype(jnp.bfloat16)
    key_rows = key_rot.astype(jnp.bfloat16)
    kv_stack = jnp.stack([key_rows, values], axis=0)
    far_parts = []
    for step_back in range(hop_count, 0, -1):
        far_parts.append(from_behind(kv_stack, "seq", step_back))
    extended = jnp.concatenate(far_parts + [kv_stack], axis=1)
    key_ext = extended[0]
    value_ext = extended[1]
    distance = (
        WINDOW
        + jnp.arange(block_rows, dtype=jnp.int32)[:, None]
        - jnp.arange(block_rows + WINDOW, dtype=jnp.int32)[None, :]
    )
    scores = block_scores(queries, key_ext, position, padded, distance, score_scale)
    row_peak = jnp.max(scores, axis=-1, keepdims=True)
    exp_scores = jnp.exp(scores - row_peak)
    row_total = jnp.sum(exp_scores, axis=-1, keepdims=True)
    attn_probs = exp_scores / row_total
    log_parts = row_peak + jnp.log(row_total)
    attended_parts = jnp.einsum(
        "hqk,kd->qhd",
        attn_probs.astype(jnp.bfloat16),
        value_ext,
        preferred_element_type=jnp.float32,
    )
    attended = attended_parts.reshape(row_count, heads_width)
    attended_low = attended.astype(jnp.bfloat16)
    attn_out = matmul_t(attended_low, wo_full)
    post_attn, ap_pull = jax.vjp(scaled_norm, attn_out, gain_ap)
    middle = inputs + post_attn
    ffn_in_f, fn_pull = jax.vjp(scaled_norm, middle, gain_fn)
    ffn_in = ffn_in_f.astype(jnp.bfloat16)
    ffn_rows_in = lax.all_gather(ffn_in, "fsdp", axis=0, tiled=True)
    gate_proj = matmul(ffn_rows_in, wg_full)
    up_proj = matmul(ffn_rows_in, wu_full)
    act_f, act_pull = jax.vjp(
        lambda gate_in, up_in: jax.nn.gelu(gate_in, approximate=True) * up_in, gate_proj, up_proj
    )
    act_low = act_f.astype(jnp.bfloat16)
    ffn_out = lax.psum_scatter(
        matmul_t(act_low, wd_full).astype(jnp.bfloat16), "fsdp", scatter_dimension=0, tiled=True
    ).astype(jnp.float32)
    post_ffn, fp_pull = jax.vjp(scaled_norm, ffn_out, gain_fp)
    output = (middle + post_ffn).astype(jnp.bfloat16)[None]
    d_ffn_out, grad_fp = fp_pull(upstream)
    d_ffn_low = d_ffn_out.astype(jnp.bfloat16)
    d_rows = lax.all_gather(d_ffn_low, "fsdp", axis=0, tiled=True)
    d_act = matmul(d_rows, wd_full)
    grad_down = matmul_tn(d_rows, act_low)
    d_gate, d_up = act_pull(d_act)
    d_gate_low = d_gate.astype(jnp.bfloat16)
    d_up_low = d_up.astype(jnp.bfloat16)
    grad_gate = matmul_tn(ffn_rows_in, d_gate_low)
    grad_up = matmul_tn(ffn_rows_in, d_up_low)
    d_ffn_in = lax.psum_scatter(
        (matmul_t(d_gate_low, wg_full) + matmul_t(d_up_low, wu_full)).astype(jnp.bfloat16),
        "fsdp",
        scatter_dimension=0,
        tiled=True,
    ).astype(jnp.float32)
    d_mid_part, grad_fn = fn_pull(d_ffn_in)
    d_middle = upstream + d_mid_part
    d_attn_out, grad_ap = ap_pull(d_middle)
    d_attn_low = d_attn_out.astype(jnp.bfloat16)
    grad_out = matmul_tn(d_attn_low, attended_low)
    d_attended = (
        matmul(d_attn_low, wo_full).astype(jnp.bfloat16).reshape(row_count, head_count, head_dim)
    )
    d_key_ext = jnp.zeros((WINDOW + row_count, head_dim), jnp.float32)
    d_value_ext = jnp.zeros((WINDOW + row_count, head_dim), jnp.float32)
    scores = block_scores(queries, key_ext, position, padded, distance, score_scale)
    attn_probs = jnp.exp(scores - log_parts)
    probs_low = attn_probs.astype(jnp.bfloat16)
    d_probs = jnp.einsum("qhd,kd->hqk", d_attended, value_ext, preferred_element_type=jnp.float32)
    row_delta = jnp.sum(attn_probs * d_probs, axis=-1, keepdims=True)
    d_scores = (attn_probs * (d_probs - row_delta) * score_scale).astype(jnp.bfloat16)
    query_grad_parts = jnp.einsum(
        "hqk,kd->qhd", d_scores, key_ext, preferred_element_type=jnp.float32
    )
    d_key_ext = d_key_ext.at[0 : block_rows + WINDOW].add(
        jnp.einsum("hqk,qhd->kd", d_scores, queries, preferred_element_type=jnp.float32)
    )
    d_value_ext = d_value_ext.at[0 : block_rows + WINDOW].add(
        jnp.einsum("hqk,qhd->kd", probs_low, d_attended, preferred_element_type=jnp.float32)
    )
    grad_stack = jnp.stack([d_key_ext, d_value_ext], axis=0)
    halo_part = jnp.concatenate(
        [
            jnp.zeros((2, hop_count * row_count - WINDOW, head_dim), jnp.float32),
            grad_stack[:, :WINDOW],
        ],
        axis=1,
    )
    local_part = grad_stack[:, WINDOW:]
    for step_back in range(hop_count, 0, -1):
        piece_start = (hop_count - step_back) * row_count
        local_part = local_part + from_behind(
            halo_part[:, piece_start : piece_start + row_count].astype(jnp.bfloat16),
            "seq",
            -step_back,
        ).astype(jnp.float32)
    d_query_lin, grad_q = q_pull(query_grad_parts)
    d_key_lin, grad_k = k_pull(local_part[0])
    d_query_low = d_query_lin.reshape(row_count, heads_width).astype(jnp.bfloat16)
    d_key_low = d_key_lin.astype(jnp.bfloat16)
    d_value_low = local_part[1].astype(jnp.bfloat16)
    grad_query = matmul_tn(attn_in, d_query_low)
    grad_key = matmul_tn(attn_in, d_key_low)
    grad_value = matmul_tn(attn_in, d_value_low)
    d_attn_in = (
        matmul_t(d_query_low, wq_full)
        + matmul_t(d_key_low, wk_full)
        + matmul_t(d_value_low, wv_full)
    )
    d_in_part, grad_an = an_pull(d_attn_in)
    input_grad = (d_middle + d_in_part)[None]
    reduced = (
        lax.psum_scatter(grad_query, ("seq", "fsdp"), scatter_dimension=0, tiled=True),
        lax.psum_scatter(grad_key, ("seq", "fsdp"), scatter_dimension=0, tiled=True),
        lax.psum_scatter(grad_value, ("seq", "fsdp"), scatter_dimension=0, tiled=True),
        lax.psum_scatter(grad_out, ("seq", "fsdp"), scatter_dimension=0, tiled=True),
        lax.psum_scatter(grad_an, ("seq", "fsdp"), scatter_dimension=0, tiled=True),
        lax.psum_scatter(grad_q, ("seq", "fsdp"), scatter_dimension=0, tiled=True),
        lax.psum_scatter(grad_k, ("seq", "fsdp"), scatter_dimension=0, tiled=True),
        lax.psum_scatter(grad_ap, ("seq", "fsdp"), scatter_dimension=0, tiled=True),
        lax.psum_scatter(grad_fn, ("seq", "fsdp"), scatter_dimension=0, tiled=True),
        lax.psum_scatter(grad_fp, ("seq", "fsdp"), scatter_dimension=0, tiled=True),
    )
    ffn_grads = (
        lax.psum_scatter(
            grad_gate.astype(jnp.bfloat16), "seq", scatter_dimension=0, tiled=True
        ).astype(jnp.float32),
        lax.psum_scatter(
            grad_up.astype(jnp.bfloat16), "seq", scatter_dimension=0, tiled=True
        ).astype(jnp.float32),
        lax.psum_scatter(
            grad_down.astype(jnp.bfloat16), "seq", scatter_dimension=0, tiled=True
        ).astype(jnp.float32),
    )
    return (
        output,
        input_grad,
        reduced[0],
        reduced[1],
        reduced[2],
        reduced[3],
        ffn_grads[0],
        ffn_grads[1],
        ffn_grads[2],
        reduced[4],
        reduced[5],
        reduced[6],
        reduced[7],
        reduced[8],
        reduced[9],
    )


def solution(mesh):
    return jax.shard_map(
        on_device,
        mesh=mesh,
        in_specs=(
            P("fsdp", "seq", None),
            P("fsdp", "seq", None),
            P("fsdp", None),
            P("fsdp", None),
            P(("seq", "fsdp"), None),
            P(("seq", "fsdp"), None),
            P(("seq", "fsdp"), None),
            P(("seq", "fsdp"), None),
            P("seq", "fsdp"),
            P("seq", "fsdp"),
            P("seq", "fsdp"),
            P(("seq", "fsdp")),
            P(("seq", "fsdp")),
            P(("seq", "fsdp")),
            P(("seq", "fsdp")),
            P(("seq", "fsdp")),
            P(("seq", "fsdp")),
        ),
        out_specs=(
            P("fsdp", "seq", None),
            P("fsdp", "seq", None),
            P(("seq", "fsdp"), None),
            P(("seq", "fsdp"), None),
            P(("seq", "fsdp"), None),
            P(("seq", "fsdp"), None),
            P("seq", "fsdp"),
            P("seq", "fsdp"),
            P("seq", "fsdp"),
            P(("seq", "fsdp")),
            P(("seq", "fsdp")),
            P(("seq", "fsdp")),
            P(("seq", "fsdp")),
            P(("seq", "fsdp")),
            P(("seq", "fsdp")),
        ),
        check_vma=False,
    )
```

profile of v0, /device:TPU:0, one launch (start us, length us, event | category | flops | bytes accessed | tf_op | source)
XLA Modules:
  0.0 1011.4 jit_solution(13948614678077658321)
XLA Ops:
  9.5 76.8 %all-gather = bf16[32,36,256]{2,1,0:T(8,128)(2,1)S(1)} all-gather(bf16[1,36,256]{2,1,0:T(8,128)(2,1)} %bitcast.189), channel_id=1, replica_groups=mesh['seq'=8,'fsdp'=4] {'seq','fsdp'}, dimensions={0}, use_global_device_ids=true | all-gather | bytes 608256 | tf_op jit(solution)/shard_map/all_gather | solution.py:122
  86.3 72.6 %all-gather.1 = bf16[32,36,256]{2,1,0:T(8,128)(2,1)S(1)} all-gather(bf16[1,36,256]{2,1,0:T(8,128)(2,1)} %bitcast.190), channel_id=1, replica_groups=mesh['seq'=8,'fsdp'=4] {'seq','fsdp'}, dimensions={0}, use_global_device_ids=true | all-gather | bytes 608256 | tf_op jit(solution)/shard_map/all_gather | solution.py:123
  164.0 38.1 %all-reduce.25 = (bf16[1152]{0:T(1024)(128)(2,1)S(1)}, bf16[256]{0:T(256)(128)(2,1)S(1)}, bf16[256]{0:T(256)(128)(2,1)S(1)}, bf16[1152]{0:T(1024)(128)(2,1)S(1)}...) all-reduce(bf16[1152]{0:T(1024)(128)(2,1)S(1)} %dynamic-update-slic, ...), channel_id=1, replica_groups=mesh['seq'=8,'fsdp'=4] {'seq','fsdp'}, use_global_device_ids=true, to_apply=%add.4 | all-reduce | flops 5120 | bytes 20480
  204.8 4.2 collective-permute-start
  219.2 4.1 reshape.492
  237.3 53.1 %all-gather.12.cloned.1.call-done = bf16[1024,1152]{1,0:T(8,128)(2,1)} async-done(((bf16[256,1152]{1,0:T(8,128)(2,1)}), bf16[1024,1152]{1,0:T(8,128)(2,1)}) %all-gather.12.cloned.1.call-update) | async-done | bytes 2359312 | tf_op jit(solution)/shard_map/all_gather | solution.py:193
  290.4 10.5 %fusion.131 = f32[1024,1728]{0,1:T(8,128)} fusion(bf16[1024,1152]{1,0:T(8,128)(2,1)} %all-gather.12.cloned.1.call-done, bf16[1152,1728]{1,0:T(8,128)(2,1)} %all-gather.14.cloned.1.call-done), kind=kOutput, calls=%fused_computation.210 | convolution fusion | flops 4076863488 | bytes 13418496 | tf_op jit(solution)/shard_map/dot_general | solution.py:21
  300.9 26.5 %all-gather.16.cloned.1.call-done = bf16[1152,1728]{1,0:T(8,128)(2,1)} async-done(((bf16[144,1728]{1,0:T(8,128)(2,1)}), bf16[1152,1728]{1,0:T(8,128)(2,1)}) %all-gather.16.cloned.1.call-update) | async-done | bytes 3981328 | tf_op jit(solution)/shard_map/all_gather | solution.py:142
  327.5 12.7 %multiply_convert_fusion.1 = (bf16[1024,1728]{0,1:T(8,128)(2,1)}, f32[1024,1728]{0,1:T(8,128)}) fusion(f32[1024,1728]{0,1:T(8,128)} %fusion.131, bf16[1024,1152]{1,0:T(8,128)(2,1)} %all-gather.12.cloned.1.call-done, bf16[1152,1728]{1,0:T(8,128)(2,1)} %all-gather.16.cloned.1.call-done), kind=kOutput, calls=%fused_computation.14 | convolution fusion | flops 4094558208 | bytes 24035328 | tf_op jit(solution)/shard_map/dot_general | solution.py:21
  340.2 25.5 %all-gather.18.cloned.1.call-done = bf16[1152,1728]{1,0:T(8,128)(2,1)} async-done(((bf16[144,1728]{1,0:T(8,128)(2,1)}), bf16[1152,1728]{1,0:T(8,128)(2,1)}) %all-gather.18.cloned.1.call-update) | async-done | bytes 3981328 | tf_op jit(solution)/shard_map/all_gather | solution.py:143
  365.7 9.7 convolution_convert_fusion.3
  376.8 46.8 %reduce-scatter.14.cloned.1.call-done = bf16[256,1152]{1,0:T(8,128)(2,1)} async-done(((bf16[1024,1152]{1,0:T(8,128)(2,1)}), bf16[256,1152]{1,0:T(8,128)(2,1)}) %reduce-scatter.14.cloned.1.call-update) | async-done | bytes 589840 | tf_op jit(solution)/shard_map/reduce_scatter | solution.py:200
  429.3 50.1 %all-gather.20.cloned.1.call-done = bf16[1024,1152]{1,0:T(8,128)(2,1)} async-done(((bf16[256,1152]{1,0:T(8,128)(2,1)}), bf16[1024,1152]{1,0:T(8,128)(2,1)}) %all-gather.20.cloned.1.call-update) | async-done | bytes 2359312 | tf_op jit(solution)/shard_map/all_gather | solution.py:207
  479.4 18.0 %multiply_convert_fusion = (bf16[1024,1728]{0,1:T(8,128)(2,1)}, bf16[1024,1728]{0,1:T(8,128)(2,1)}) fusion(f32[1024,1728]{0,1:T(8,128)} %fusion.131, f32[1024,1728]{0,1:T(8,128)} %get-tuple-element.122, bf16[1024,1152]{1,0:T(8,128)(2,1)} %all-gather.20.cloned.1.call-done, bf16[1152,1728]{1,0:T(8,128)(2,1)} %all-gather.18.cloned.1.call-done), kind=kOutput, calls=%fused_computation.13 | convolution fusion | flops 4119330816 | bytes 27574272 | tf_op jit(solution)/shard_map/dot_general | solution.py:21
  497.5 7.2 fusion.132
  504.7 6.5 add_convert_fusion
  511.2 9.3 convolution_convert_fusion
  520.6 9.2 convolution_convert_fusion.2
  531.1 9.3 convolution_convert_fusion.1
  540.4 17.8 %reduce-scatter.16.cloned.1.call-done = bf16[256,1152]{1,0:T(8,128)(2,1)} async-done(((bf16[1024,1152]{1,0:T(8,128)(2,1)}), bf16[256,1152]{1,0:T(8,128)(2,1)}) %reduce-scatter.16.cloned.1.call-update) | async-done | bytes 589840 | tf_op jit(solution)/shard_map/reduce_scatter | solution.py:215
  561.4 4.0 multiply_reduce_fusion
  573.0 7.4 fusion.41
  580.4 7.9 fusion.36
  588.3 4.2 fusion.134
  605.7 282.0 %fusion.125 = (f32[40,1024]{1,0:T(8,128)}, f32[40,256]{1,0:T(8,128)S(1)}, f32[40,256]{1,0:T(8,128)}, f32[40,1024]{1,0:T(8,128)}) fusion(f32[1152,1024]{1,0:T(8,128)} %fusion.72, f32[1152,256]{1,0:T(8,128)S(1)} %fusion.120, f32[1152,256]{1,0:T(8,128)S(1)} %fusion.74, f32[1152,1024]{1,0:T(8,128)} %fusion.134), kind=kCustom, calls=%all-reduce-scatter.4 | all-reduce-scatter fusion | flops 3276801 | bytes 12206080
  891.7 5.4 collective-permute-start.14
  902.9 7.0 collective-permute-start.19
  919.1 4.5 collective-permute-start.10
  925.0 5.0 collective-permute-start.9
  931.4 41.4 %all-reduce.24 = (f32[1152]{0:T(1024)S(1)}, f32[256]{0:T(256)S(1)}, f32[256]{0:T(256)S(1)}, f32[1152]{0:T(1024)S(1)}, f32[1152]{0:T(1024)S(1)}, /*index=5*/f32[1152]{0:T(1024)S(1)}) all-reduce(f32[1152]{0:T(1024)S(1)} %get-tuple-element.61, f32[256]{0:T(256)S(1)} %get-tuple-element.57, ...), channel_id=11, replica_groups=mesh['seq'=8,'fsdp'=4] {'seq','fsdp'}, use_global_device_ids=true, to_apply=%region_29.30.clone | all-reduce | flops 5120 | bytes 40960
  976.9 3.5 collective-permute-start.18
  984.8 5.5 collective-permute-start.6
  (324 shorter events, 109.5 us)
Async XLA Ops:
  7.2 206.7 %all-gather.22.cloned.1.call-start = ((), (), s32[]{:S(2)}) async-start(), calls=%async_computation.15 | async-start | bytes 2703360 | tf_op jit(solution)/shard_map/all_gather | solution.py:121
  7.9 211.3 %all-gather.24.cloned.1.call-start = ((), (), s32[]{:S(2)}) async-start(), calls=%async_computation.16 | async-start | bytes 2703360 | tf_op jit(solution)/shard_map/all_gather | solution.py:124
  8.7 228.6 %all-gather.14.cloned.1.call-start = ((), (), s32[]{:S(2)}) async-start(), calls=%async_computation.6 | async-start | bytes 4644864 | tf_op jit(solution)/shard_map/all_gather | solution.py:141
  9.4 281.0 %all-gather.12.cloned.1.call-start = ((), (), s32[]{:S(2)}) async-start(), calls=%async_computation.5 | async-start | bytes 2949120 | tf_op jit(solution)/shard_map/all_gather | solution.py:193
  204.8 8.1 collective-permute-start
  209.0 3.9 collective-permute-start.1
  235.8 91.6 %all-gather.16.cloned.1.call-start = ((), (), s32[]{:S(2)}) async-start(), calls=%async_computation.7 | async-start | bytes 4644864 | tf_op jit(solution)/shard_map/all_gather | solution.py:142
  236.4 129.3 %all-gather.18.cloned.1.call-start = ((), (), s32[]{:S(2)}) async-start(), calls=%async_computation.8 | async-start | bytes 4644864 | tf_op jit(solution)/shard_map/all_gather | solution.py:143
  237.0 186.6 %reduce-scatter.14.cloned.1.call-start = ((), (), s32[]{:S(2)}) async-start(), calls=%async_computation.9 | async-start | bytes 2949120 | tf_op jit(solution)/shard_map/reduce_scatter | solution.py:200
  375.4 104.0 %all-gather.20.cloned.1.call-start = ((), (), s32[]{:S(2)}) async-start(), calls=%async_computation.10 | async-start | bytes 2949120 | tf_op jit(solution)/shard_map/all_gather | solution.py:207
  429.3 128.9 %reduce-scatter.16.cloned.1.call-start = ((), (), s32[]{:S(2)}) async-start(), calls=%async_computation.11 | async-start | bytes 2949120 | tf_op jit(solution)/shard_map/reduce_scatter | solution.py:215
  511.2 486.7 %reduce-scatter.22.cloned.1.call-start = ((), (), s32[]{:S(2)}) async-start(), calls=%async_computation.14 | async-start | bytes 4644864 | tf_op jit(solution)/shard_map/reduce_scatter | solution.py:296
  520.6 479.4 %reduce-scatter.18.cloned.1.call-start = ((), (), s32[]{:S(2)}) async-start(), calls=%async_computation.12 | async-start | bytes 4644864 | tf_op jit(solution)/shard_map/reduce_scatter | solution.py:290
  529.8 472.2 %reduce-scatter.20.cloned.1.call-start = ((), (), s32[]{:S(2)}) async-start(), calls=%async_computation.13 | async-start | bytes 4644864 | tf_op jit(solution)/shard_map/reduce_scatter | solution.py:293
  592.7 10.4 %collective-permute-start.2 = (bf16[2,256,256]{1,2,0:T(8,128)(2,1)S(1)}, bf16[2,256,256]{1,2,0:T(8,128)(2,1)S(1)}, u32[]{:S(2)}, u32[]{:S(2)}) collective-permute-start(bf16[2,256,256]{1,2,0:T(8,128)(2,1)S(1)} %get-tuple-element.101), channel_id=1, source_target_pairs={{8,0},{12,4},{16,8},{20,12},{24,16},{28,20},{9,1},{13,5},{17,9},{2... | collective-permute-start | bytes 786440 | tf_op jit(solution)/shard_map/ppermute | solution.py:17
  594.1 9.0 collective-permute-start.3
  887.8 31.3 %collective-permute-start.12 = (f32[40,256]{1,0:T(8,128)}, f32[40,256]{1,0:T(8,128)S(1)}, u32[]{:S(2)}, u32[]{:S(2)}) collective-permute-start(f32[40,256]{1,0:T(8,128)} %get-tuple-element.87), channel_id=1, source_target_pairs={{0,1},{1,2},{2,3},{3,4},{4,5},{5,6},{6,7},{7,8},{8,9},{9,10},{10,1... | collective-permute-start | bytes 122888
  889.2 34.4 %collective-permute-start.13 = (f32[40,256]{1,0:T(8,128)}, f32[40,256]{1,0:T(8,128)S(1)}, u32[]{:S(2)}, u32[]{:S(2)}) collective-permute-start(f32[40,256]{1,0:T(8,128)} %get-tuple-element.87), channel_id=1, source_target_pairs={{0,2},{1,3},{2,4},{3,5},{4,6},{5,7},{6,8},{7,9},{8,10},{9,11},{10,... | collective-permute-start | bytes 122888
  891.7 33.3 %collective-permute-start.14 = (f32[40,256]{1,0:T(8,128)}, f32[40,256]{1,0:T(8,128)S(1)}, u32[]{:S(2)}, u32[]{:S(2)}) collective-permute-start(f32[40,256]{1,0:T(8,128)} %get-tuple-element.87), channel_id=1, source_target_pairs={{0,3},{1,4},{2,5},{3,6},{4,7},{5,8},{6,9},{7,10},{8,11},{9,12},{10... | collective-permute-start | bytes 122888
  897.8 12.1 %collective-permute-start.15 = (f32[4,256]{1,0:T(4,128)S(1)}, f32[4,256]{1,0:T(4,128)S(1)}, u32[]{:S(2)}, u32[]{:S(2)}) collective-permute-start(f32[4,256]{1,0:T(4,128)S(1)} %slice.91), channel_id=1, source_target_pairs={{0,4},{1,5},{2,6},{3,7},{4,8},{5,9},{6,10},{7,11},{8,12},{9,13},{1... | collective-permute-start | bytes 12296
  902.9 13.2 %collective-permute-start.19 = (f32[4,1024]{1,0:T(4,128)S(1)}, f32[4,1024]{1,0:T(4,128)S(1)}, u32[]{:S(2)}, u32[]{:S(2)}) collective-permute-start(f32[4,1024]{1,0:T(4,128)S(1)} %slice.92), channel_id=1, source_target_pairs={{0,4},{1,5},{2,6},{3,7},{4,8},{5,9},{6,10},{7,11},{8,12},{9,13},{1... | collective-permute-start | bytes 49160
  909.9 3.7 collective-permute-start.11
  913.6 71.2 %collective-permute-start.16 = (f32[40,1024]{1,0:T(8,128)S(1)}, f32[40,1024]{1,0:T(8,128)S(1)}, u32[]{:S(2)}, u32[]{:S(2)}) collective-permute-start(f32[40,1024]{1,0:T(8,128)S(1)} %copy-done.31), channel_id=1, source_target_pairs={{0,1},{1,2},{2,3},{3,4},{4,5},{5,6},{6,7},{7,8},{8,9},{9,10},{10,1... | collective-permute-start | bytes 491528
  916.1 75.4 %collective-permute-start.17 = (f32[40,1024]{1,0:T(8,128)S(1)}, f32[40,1024]{1,0:T(8,128)S(1)}, u32[]{:S(2)}, u32[]{:S(2)}) collective-permute-start(f32[40,1024]{1,0:T(8,128)S(1)} %copy-done.31), channel_id=1, source_target_pairs={{0,2},{1,3},{2,4},{3,5},{4,6},{5,7},{6,8},{7,9},{8,10},{9,11},{10,... | collective-permute-start | bytes 491528
  919.1 57.8 %collective-permute-start.10 = (f32[40,256]{1,0:T(8,128)S(1)}, f32[40,256]{1,0:T(8,128)S(1)}, u32[]{:S(2)}, u32[]{:S(2)}) collective-permute-start(f32[40,256]{1,0:T(8,128)S(1)} %get-tuple-element.86), channel_id=1, source_target_pairs={{0,3},{1,4},{2,5},{3,6},{4,7},{5,8},{6,9},{7,10},{8,11},{9,12},{10... | collective-permute-start | bytes 122888
  923.6 56.8 %collective-permute-start.8 = (f32[40,256]{1,0:T(8,128)S(1)}, f32[40,256]{1,0:T(8,128)S(1)}, u32[]{:S(2)}, u32[]{:S(2)}) collective-permute-start(f32[40,256]{1,0:T(8,128)S(1)} %get-tuple-element.86), channel_id=1, source_target_pairs={{0,1},{1,2},{2,3},{3,4},{4,5},{5,6},{6,7},{7,8},{8,9},{9,10},{10,1... | collective-permute-start | bytes 122888
  925.0 56.7 %collective-permute-start.9 = (f32[40,256]{1,0:T(8,128)S(1)}, f32[40,256]{1,0:T(8,128)S(1)}, u32[]{:S(2)}, u32[]{:S(2)}) collective-permute-start(f32[40,256]{1,0:T(8,128)S(1)} %get-tuple-element.86), channel_id=1, source_target_pairs={{0,2},{1,3},{2,4},{3,5},{4,6},{5,7},{6,8},{7,9},{8,10},{9,11},{10,... | collective-permute-start | bytes 122888
  976.9 18.2 %collective-permute-start.18 = (f32[40,1024]{1,0:T(8,128)S(1)}, f32[40,1024]{1,0:T(8,128)S(1)}, u32[]{:S(2)}, u32[]{:S(2)}) collective-permute-start(f32[40,1024]{1,0:T(8,128)S(1)} %copy-done.31), channel_id=1, source_target_pairs={{0,3},{1,4},{2,5},{3,6},{4,7},{5,8},{6,9},{7,10},{8,11},{9,12},{10... | collective-permute-start | bytes 491528
  980.4 15.4 %collective-permute-start.4 = (f32[40,1024]{1,0:T(8,128)S(1)}, f32[40,1024]{1,0:T(8,128)S(1)}, u32[]{:S(2)}, u32[]{:S(2)}) collective-permute-start(f32[40,1024]{1,0:T(8,128)S(1)} %copy-done.30), channel_id=1, source_target_pairs={{0,1},{1,2},{2,3},{3,4},{4,5},{5,6},{6,7},{7,8},{8,9},{9,10},{10,1... | collective-permute-start | bytes 491528
  981.7 14.1 %collective-permute-start.5 = (f32[40,1024]{1,0:T(8,128)S(1)}, f32[40,1024]{1,0:T(8,128)S(1)}, u32[]{:S(2)}, u32[]{:S(2)}) collective-permute-start(f32[40,1024]{1,0:T(8,128)S(1)} %copy-done.30), channel_id=1, source_target_pairs={{0,2},{1,3},{2,4},{3,5},{4,6},{5,7},{6,8},{7,9},{8,10},{9,11},{10,... | collective-permute-start | bytes 491528
  984.8 11.0 %collective-permute-start.6 = (f32[40,1024]{1,0:T(8,128)S(1)}, f32[40,1024]{1,0:T(8,128)S(1)}, u32[]{:S(2)}, u32[]{:S(2)}) collective-permute-start(f32[40,1024]{1,0:T(8,128)S(1)} %copy-done.30), channel_id=1, source_target_pairs={{0,3},{1,4},{2,5},{3,6},{4,7},{5,8},{6,9},{7,10},{8,11},{9,12},{10... | collective-permute-start | bytes 491528
  991.5 4.3 collective-permute-start.7
  (77 other events, 1400.4 us)
Sparse Core Ops, SparseCore 0:
  10.9 61.6 all-gather.21
  75.4 57.3 all-gather.23
  134.7 36.0 all-gather.13
  236.0 54.4 all-gather.11
  292.2 35.2 all-gather.15
  329.2 36.4 all-gather.17
  375.5 48.0 reduce-scatter.13
  429.4 49.9 all-gather.19
  511.3 46.8 reduce-scatter.15
  561.5 51.4 reduce-scatter.21
  616.4 56.7 reduce-scatter.17
  676.5 55.8 reduce-scatter.19
where the time goes:
time: 1020 us; the launch traced here: 1010 us
  blocking collectives  511 us (50%)
  waiting for transfers between devices  227 us (22%)
  matrix products  131 us (13%)
  starting transfers between devices  63.5 us (6%)
  local copies, waits for them, and re-layouts  33 us (3%)
  other arithmetic  29.7 us (3%)
  between operations  16.1 us (2%)
    unnamed x3, blocking collectives  362 us
    all_gather x1, blocking collectives, on_device(): lax.all_gather(w_key, ('seq', 'fsdp'), axis=0, tiled=True)  76.8 us
    all_gather x1, blocking collectives, on_device(): lax.all_gather(w_value, ('seq', 'fsdp'), axis=0, tiled=True)  72.6 us
    unnamed x16, starting transfers between devices  54.1 us
    all_gather x1, waiting for transfers between devices, on_device(): ffn_rows_in = lax.all_gather(ffn_in, 'fsdp', axis=0, tiled=True)  53.1 us
    all_gather x1, waiting for transfers between devices, on_device(): d_rows = lax.all_gather(d_ffn_low, 'fsdp', axis=0, tiled=True)  50.1 us
    reduce_scatter x1, waiting for transfers between devices, on_device(): lax.psum_scatter(matmul_t(act_low, wd_full).astype(jnp.bfloat16), 'fsdp',...  46.8 us
    dot_general x7, matrix products, matmul(): return jnp.dot(left_side, right_side, preferred_element_type=jnp.float32)  45.7 us
  transfers between devices with their start and end apart: 32, of which 9 were waited for; matrix products, arithmetic and copies ran while one was open for 41% of the time, Pallas kernels for 0%

commit v1 on v0

--- a/solution.py
+++ b/solution.py
@@ -15,6 +15,93 @@
     count = lax.axis_size(axis)
     first, last = (max(0, -steps), min(count, count - steps))
     return lax.ppermute(value, axis, [(source, source + steps) for source in range(first, last)])
+
+
+def seq_masks():
+    return [1 << bit for bit in range(lax.axis_size("seq").bit_length() - 1)]
+
+
+def swap(value, axis, mask):
+    count = lax.axis_size(axis)
+    return lax.ppermute(value, axis, [(source, source ^ mask) for source in range(count)])
+
+
+def shift(value, axis, steps):
+    count = lax.axis_size(axis)
+    return lax.ppermute(value, axis, [(source, (source + steps) % count) for source in range(count)])
+
+
+def gather_seq(block, order):
+    stack, held = block[None], []
+    for mask in order:
+        place = sum(1 for other in held if other > mask)
+        full = stack.reshape((2,) * len(held) + block.shape)
+        stack = jnp.stack([full, swap(full, "seq", mask)], axis=place)
+        held.append(mask)
+    stack = stack.reshape((-1,) + block.shape)
+    index = jnp.arange(stack.shape[0], dtype=jnp.int32) ^ lax.axis_index("seq")
+    return jnp.take(stack, index, axis=0, mode="clip")
+
+
+def gather_seq_rows(block, split):
+    far = seq_masks()[1:]
+    top = gather_seq(block[:split], far[::-1] + [1])
+    bottom = gather_seq(block[split:], far + [1])
+    whole = jnp.concatenate([top, bottom], axis=1)
+    return whole.reshape((-1,) + block.shape[1:])
+
+
+def scatter_seq(blocks, order):
+    masks = seq_masks()[::-1]
+    shape = blocks.shape[1:]
+    part = blocks.reshape((2,) * len(masks) + shape)
+    me = lax.axis_index("seq")
+    for mask in order:
+        axis = masks.index(mask)
+        bit = (me // mask) % 2
+        keep = lax.dynamic_index_in_dim(part, bit, axis, keepdims=False)
+        send = lax.dynamic_index_in_dim(part, 1 - bit, axis, keepdims=False)
+        got = swap(send.astype(jnp.bfloat16), "seq", mask)
+        part = keep.astype(jnp.float32) + got.astype(jnp.float32)
+        masks.remove(mask)
+    return part
+
+
+def scatter_seq_rows(rows, split):
+    blocks = rows.reshape((lax.axis_size("seq"), -1) + rows.shape[1:])
+    far = seq_masks()[1:]
+    top = scatter_seq(blocks[:, :split], [1] + far[::-1])
+    bottom = scatter_seq(blocks[:, split:], [1] + far)
+    return jnp.concatenate([top, bottom], axis=0)
+
+
+def gather_fsdp(block):
+    count = lax.axis_size("fsdp")
+    parts = [block] + [shift(block, "fsdp", steps) for steps in range(1, count)]
+    index = (lax.axis_index("fsdp") - jnp.arange(count, dtype=jnp.int32)) % count
+    stack = jnp.take(jnp.stack(parts), index, axis=0, mode="clip")
+    return stack.reshape((-1,) + block.shape[1:])
+
+
+def scatter_fsdp(rows):
+    count = lax.axis_size("fsdp")
+    blocks = rows.reshape((count, -1) + rows.shape[1:])
+    mine = lax.axis_index("fsdp")
+    total = lax.dynamic_index_in_dim(blocks, mine, 0, keepdims=False)
+    for steps in range(1, count):
+        send = lax.dynamic_index_in_dim(blocks, (mine + steps) % count, 0, keepdims=False)
+        total = total + shift(send.astype(jnp.bfloat16), "fsdp", steps).astype(jnp.float32)
+    return total
+
+
+def half_rows(count):
+    return (count // 2 + 15) // 16 * 16
+
+
+def pack_gains(wide, narrow):
+    rows = wide[0].shape[0]
+    columns = wide + [jnp.pad(vec, (0, rows - vec.shape[0])) for vec in narrow]
+    return jnp.stack(columns + [jnp.zeros((rows,), wide[0].dtype)] * (128 - len(columns)), axis=1)
 
 
 def matmul(left_side, right_side):
@@ -117,31 +204,37 @@
     position, padded = layout(
         doc_lengths[0], true_counts[0], lax.axis_index("seq") * row_count, row_count
     )
-    gathered = (
-        lax.all_gather(w_query, ("seq", "fsdp"), axis=0, tiled=True),
-        lax.all_gather(w_key, ("seq", "fsdp"), axis=0, tiled=True),
-        lax.all_gather(w_value, ("seq", "fsdp"), axis=0, tiled=True),
-        lax.all_gather(w_out, ("seq", "fsdp"), axis=0, tiled=True),
-        lax.all_gather(attn_norm_gain, ("seq", "fsdp"), axis=0, tiled=True),
-        lax.all_gather(query_gain, ("seq", "fsdp"), axis=0, tiled=True),
-        lax.all_gather(key_gain, ("seq", "fsdp"), axis=0, tiled=True),
-        lax.all_gather(attn_post_gain, ("seq", "fsdp"), axis=0, tiled=True),
-        lax.all_gather(ffn_norm_gain, ("seq", "fsdp"), axis=0, tiled=True),
-        lax.all_gather(ffn_post_gain, ("seq", "fsdp"), axis=0, tiled=True),
-    )
-    wq_full, wk_full, wv_full, wo_full = (gathered[0], gathered[1], gathered[2], gathered[3])
-    gain_an = gathered[4].astype(jnp.float32)
-    gain_q = gathered[5].astype(jnp.float32)
-    gain_k = gathered[6].astype(jnp.float32)
-    gain_ap = gathered[7].astype(jnp.float32)
-    gain_fn = gathered[8].astype(jnp.float32)
-    gain_fp = gathered[9].astype(jnp.float32)
-    gate_part, up_part, down_part = (w_gate, w_up, w_down)
-    wg_full, wu_full, wd_full = (
-        lax.all_gather(gate_part, "seq", axis=0, tiled=True),
-        lax.all_gather(up_part, "seq", axis=0, tiled=True),
-        lax.all_gather(down_part, "seq", axis=0, tiled=True),
-    )
+    shards = lax.axis_size("seq") * lax.axis_size("fsdp")
+    narrow_rows = query_gain.shape[0]
+    first_pack = jnp.concatenate(
+        [
+            w_query,
+            w_key,
+            w_value,
+            pack_gains(
+                [attn_norm_gain, attn_post_gain, ffn_norm_gain, ffn_post_gain],
+                [query_gain, key_gain],
+            ),
+        ],
+        axis=1,
+    )
+    first_rows = gather_fsdp(first_pack)
+    out_rows = gather_fsdp(w_out)
+    split = half_rows(first_rows.shape[0])
+    first_full = gather_seq_rows(first_rows, split)
+    wo_full = gather_seq_rows(out_rows, split)
+    wq_full = first_full[:, :heads_width]
+    wk_full = first_full[:, heads_width : heads_width + head_dim]
+    wv_full = first_full[:, heads_width + head_dim : heads_width + 2 * head_dim]
+    gain_cols = first_full[:, heads_width + 2 * head_dim :].astype(jnp.float32)
+    gain_an, gain_ap, gain_fn, gain_fp = [gain_cols[:, index] for index in range(4)]
+    gain_q, gain_k = [
+        gain_cols[:, index].reshape(shards, -1)[:, :narrow_rows].reshape(-1) for index in (4, 5)
+    ]
+    far = seq_masks()[1:]
+    wg_full = gather_seq(w_gate, far[::-1] + [1]).reshape(-1, w_gate.shape[1])
+    wu_full = gather_seq(w_up, far + [1]).reshape(-1, w_up.shape[1])
+    wd_full = gather_seq_rows(w_down, half_rows(w_down.shape[0]))
     attn_in_f, an_pull = jax.vjp(scaled_norm, inputs, gain_an)
     attn_in = attn_in_f.astype(jnp.bfloat16)
     query_lin = matmul(attn_in, wq_full).reshape(row_count, head_count, head_dim)
@@ -274,28 +367,39 @@
     )
     d_in_part, grad_an = an_pull(d_attn_in)
     input_grad = (d_middle + d_in_part)[None]
+    grad_split = half_rows(first_rows.shape[0])
+    query_rows = scatter_fsdp(scatter_seq_rows(grad_query, grad_split))
+    out_grad_rows = scatter_fsdp(scatter_seq_rows(grad_out, grad_split))
+    spare = grad_an.shape[0] // shards - narrow_rows
+    narrow_grads = [
+        jnp.pad(vec.reshape(shards, -1), ((0, 0), (0, spare))).reshape(-1) for vec in (grad_q, grad_k)
+    ]
+    last_pack = jnp.concatenate(
+        [
+            grad_key,
+            grad_value,
+            pack_gains([grad_an, grad_ap, grad_fn, grad_fp] + narrow_grads, []),
+        ],
+        axis=1,
+    )
+    last_rows = scatter_fsdp(scatter_seq_rows(last_pack, grad_split))
+    gain_rows = last_rows[:, 2 * head_dim :]
+    ffn_grads = (
+        scatter_seq(grad_gate.astype(jnp.bfloat16).reshape((-1,) + w_gate.shape), [1] + far[::-1]),
+        scatter_seq(grad_up.astype(jnp.bfloat16).reshape((-1,) + w_up.shape), [1] + far),
+        scatter_seq_rows(grad_down.astype(jnp.bfloat16), half_rows(w_down.shape[0])),
+    )
     reduced = (
-        lax.psum_scatter(grad_query, ("seq", "fsdp"), scatter_dimension=0, tiled=True),
-        lax.psum_scatter(grad_key, ("seq", "fsdp"), scatter_dimension=0, tiled=True),
-        lax.psum_scatter(grad_value, ("seq", "fsdp"), scatter_dimension=0, tiled=True),
-        lax.psum_scatter(grad_out, ("seq", "fsdp"), scatter_dimension=0, tiled=True),
-        lax.psum_scatter(grad_an, ("seq", "fsdp"), scatter_dimension=0, tiled=True),
-        lax.psum_scatter(grad_q, ("seq", "fsdp"), scatter_dimension=0, tiled=True),
-        lax.psum_scatter(grad_k, ("seq", "fsdp"), scatter_dimension=0, tiled=True),
-        lax.psum_scatter(grad_ap, ("seq", "fsdp"), scatter_dimension=0, tiled=True),
-        lax.psum_scatter(grad_fn, ("seq", "fsdp"), scatter_dimension=0, tiled=True),
-        lax.psum_scatter(grad_fp, ("seq", "fsdp"), scatter_dimension=0, tiled=True),
-    )
-    ffn_grads = (
-        lax.psum_scatter(
-            grad_gate.astype(jnp.bfloat16), "seq", scatter_dimension=0, tiled=True
-        ).astype(jnp.float32),
-        lax.psum_scatter(
-            grad_up.astype(jnp.bfloat16), "seq", scatter_dimension=0, tiled=True
-        ).astype(jnp.float32),
-        lax.psum_scatter(
-            grad_down.astype(jnp.bfloat16), "seq", scatter_dimension=0, tiled=True
-        ).astype(jnp.float32),
+        query_rows,
+        last_rows[:, :head_dim],
+        last_rows[:, head_dim : 2 * head_dim],
+        out_grad_rows,
+        gain_rows[:, 0],
+        gain_rows[:narrow_rows, 4],
+        gain_rows[:narrow_rows, 5],
+        gain_rows[:, 1],
+        gain_rows[:, 2],
+        gain_rows[:, 3],
     )
     return (
         output,

time: 1020 us -> 648 us (0.64)
  blocking collectives: 511 us -> 0 us
  local copies, waits for them, and re-layouts: 33 us -> 123 us
  other arithmetic: 29.7 us -> 102 us
  waiting for transfers between devices: 227 us -> 184 us
  starting transfers between devices: 63.5 us -> 93.6 us
  matrix products: 131 us -> 118 us
    unnamed x3 -> x0, blocking collectives: 362 us -> none
    all_gather x2 -> x0, blocking collectives: 149 us -> none  [the longest x1 76.8 us: on_device(): lax.all_gather(w_key, ('seq', 'fsdp'), axis=0, tiled=True)]
    ppermute x0 -> x69, waiting for transfers between devices: none -> 93.1 us  [the longest x54 88.3 us: swap(): lax.ppermute(value, axis, [(source, source ^ mask) for source in range(co...]
    ppermute x0 -> x69, starting transfers between devices: none -> 75.4 us  [the longest x54 51.1 us: swap(): lax.ppermute(value, axis, [(source, source ^ mask) for source in range(co...]
    unnamed x16 -> x0, starting transfers between devices: 54.1 us -> none
    all_gather x1, waiting for transfers between devices: 53.1 us -> 0.01 us  [on_device(): ffn_rows_in = lax.all_gather(ffn_in, 'fsdp', axis=0, tiled=True)]
    all_gather x5 -> x0, waiting for transfers between devices: 52.1 us -> none  [the longest x1 26.5 us: on_device(): lax.all_gather(up_part, 'seq', axis=0, tiled=True)]
    another operation x3 -> x29, other arithmetic: 0.42 us -> 41.2 us  [the longest x24 40.7 us: gather_seq(): stack = jnp.stack([full, swap(full, 'seq', mask)], axis=place)]
  transfers between devices with their start and end apart: 32 -> 77, of which waited for: 9 -> 25; matrix products, arithmetic and copies ran while one was open for 41% -> 38% of each run, Pallas kernels for 0% -> 0%
where the time goes in v1:
time: 648 us; the launch traced here: 637 us
  waiting for transfers between devices  184 us (28%)
  local copies, waits for them, and re-layouts  123 us (19%)
  matrix products  118 us (18%)
  other arithmetic  102 us (16%)
  starting transfers between devices  93.6 us (14%)
  between operations  16.1 us (2%)
    ppermute x54, waiting for transfers between devices, swap(): lax.ppermute(value, axis, [(source, source ^ mask) for source in range(co...  88.3 us
    ppermute x54, starting transfers between devices, swap(): lax.ppermute(value, axis, [(source, source ^ mask) for source in range(co...  51.1 us
    reduce_scatter x1, waiting for transfers between devices, on_device(): lax.psum_scatter(matmul_t(act_low, wd_full).astype(jnp.bfloat16), 'fsdp',...  46 us
    all_gather x1, waiting for transfers between devices, on_device(): d_rows = lax.all_gather(d_ffn_low, 'fsdp', axis=0, tiled=True)  44.4 us
    another operation x24, other arithmetic, gather_seq(): stack = jnp.stack([full, swap(full, 'seq', mask)], axis=place)  40.7 us
    dot_general x7, matrix products, matmul(): return jnp.dot(left_side, right_side, preferred_element_type=jnp.float32)  37.1 us
    dot_general x7, matrix products, matmul_t(): lax.dot_general(left_side, right_side, (((1,), (1,)), ((), ())), preferre...  31.4 us
    dot_general x7, matrix products, matmul_tn(): lax.dot_general(left_side, right_side, (((0,), (0,)), ((), ())), preferre...  31.4 us
  transfers between devices with their start and end apart: 77, of which 25 were waited for; matrix products, arithmetic and copies ran while one was open for 38% of the time, Pallas kernels for 0%

profile of v1, /device:TPU:0, one launch (start us, length us, event | category | flops | bytes accessed | tf_op | source)
XLA Modules:
  0.0 637.2 jit_solution(17309465806574124701)
XLA Ops:
  13.0 5.1 collective-permute-start.2
  18.1 4.4 collective-permute-start.12
  44.3 4.4 collective-permute-done.14
  62.8 5.2 collective-permute-done.7
  111.8 12.8 %collective-permute-start.9 = (bf16[2,256,256]{1,2,0:T(8,128)(2,1)}, bf16[2,256,256]{1,2,0:T(8,128)(2,1)}, u32[]{:S(2)}, u32[]{:S(2)}) collective-permute-start(bf16[2,256,256]{1,2,0:T(8,128)(2,1)} %pad_maximum_fusion.36), channel_id=1, source_target_pairs={{0,8},{4,12},{8,16},{12,20},{16,24},{20,28},{1,9},{5,13},{9,17},{1... | collective-permute-start | bytes 786440 | tf_op jit(solution)/shard_map/ppermute | solution.py:17
  149.6 9.3 %collective-permute-done.27 = bf16[2,80,1728]{2,1,0:T(8,128)(2,1)S(1)} collective-permute-done((bf16[2,80,1728]{2,1,0:T(8,128)(2,1)S(1)}, bf16[2,80,1728]{2,1,0:T(8,128)(2,1)S(1)}, u32[]{:S(2)}, u32[]{:S(2)}) %collective-permute-start.27) | collective-permute-done | bytes 552992 | tf_op jit(solution)/shard_map/ppermute | solution.py:26
  176.4 4.7 pad_maximum_fusion.2
  185.1 5.0 gather_fusion.6
  190.1 4.6 pad_maximum_fusion.1
  194.7 4.9 gather_fusion.7
  199.6 8.0 %fusion.188 = f32[1024,1728]{0,1:T(8,128)S(1)} fusion(bf16[1024,1152]{1,0:T(8,128)(2,1)} %all-gather.3.cloned.1.call-done, bf16[1152,1728]{1,0:T(8,128)(2,1)} %bitcast.532), kind=kOutput, calls=%fused_computation.425 | convolution fusion | flops 4076863488 | bytes 13418496 | tf_op jit(solution)/shard_map/dot_general | solution.py:108
  207.6 9.5 %multiply_convert_fusion.1 = (bf16[1024,1728]{0,1:T(8,128)(2,1)}, f32[1024,1728]{0,1:T(8,128)}) fusion(f32[1024,1728]{0,1:T(8,128)S(1)} %fusion.188, bf16[1024,1152]{1,0:T(8,128)(2,1)S(1)} %copy-done.98, bf16[1152,1728]{1,0:T(8,128)(2,1)S(1)} %bitcast.530), kind=kOutput, calls=%fused_computation.24 | convolution fusion | flops 4094558208 | bytes 24035328 | tf_op jit(solution)/shard_map/dot_general | solution.py:108
  217.2 8.4 %convolution_convert_fusion.3 = bf16[1024,1152]{1,0:T(8,128)(2,1)} fusion(bf16[1024,1728]{0,1:T(8,128)(2,1)} %get-tuple-element.172, bf16[1152,1728]{1,0:T(8,128)(2,1)S(1)} %bitcast.534), kind=kOutput, calls=%fused_computation.33 | convolution fusion | flops 4078043136 | bytes 9879552 | tf_op jit(solution)/shard_map/dot_general | solution.py:112
  225.7 46.0 %reduce-scatter.3.cloned.1.call-done = bf16[256,1152]{1,0:T(8,128)(2,1)} async-done(((bf16[1024,1152]{1,0:T(8,128)(2,1)}), bf16[256,1152]{1,0:T(8,128)(2,1)}) %reduce-scatter.3.cloned.1.call-update) | async-done | bytes 589840 | tf_op jit(solution)/shard_map/reduce_scatter | solution.py:293
  283.2 44.4 %all-gather.5.cloned.1.call-done = bf16[1024,1152]{1,0:T(8,128)(2,1)} async-done(((bf16[256,1152]{1,0:T(8,128)(2,1)}), bf16[1024,1152]{1,0:T(8,128)(2,1)}) %all-gather.5.cloned.1.call-update) | async-done | bytes 2359312 | tf_op jit(solution)/shard_map/all_gather | solution.py:300
  327.6 9.4 %convolution_convert_fusion = bf16[1152,1728]{0,1:T(8,128)(2,1)} fusion(bf16[1024,1728]{0,1:T(8,128)(2,1)} %get-tuple-element.172, bf16[1024,1152]{1,0:T(8,128)(2,1)} %all-gather.5.cloned.1.call-done), kind=kOutput, calls=%fused_computation.13 | convolution fusion | flops 4078854144 | bytes 9879552 | tf_op jit(solution)/shard_map/dot_general | solution.py:118
  337.0 6.6 %copy.223 = bf16[1152,1728]{1,0:T(8,128)(2,1)} copy(bf16[1152,1728]{0,1:T(8,128)(2,1)} %convolution_convert_fusion) | data formatting | bytes 7962624 | tf_op jit(solution)/shard_map/convert_element_type | solution.py:390
  352.0 15.0 %multiply_convert_fusion = (bf16[1024,1728]{0,1:T(8,128)(2,1)}, bf16[1024,1728]{0,1:T(8,128)(2,1)}) fusion(f32[1024,1728]{0,1:T(8,128)} %copy-done.102, f32[1024,1728]{0,1:T(8,128)} %get-tuple-element.173, bf16[1024,1152]{1,0:T(8,128)(2,1)S(1)} %copy-done.101, bf16[1152,1728]{1,0:T(8,128)(2,1)S(1)} %bitcast.535), kind=kOutput, calls=%fused_computation.23 | convolution fusion | flops 4119330816 | bytes 27574272 | tf_op jit(solution)/shard_map/dot_general | solution.py:108
  367.0 9.2 %convolution_convert_fusion.1 = bf16[1152,1728]{0,1:T(8,128)(2,1)} fusion(bf16[1024,1728]{0,1:T(8,128)(2,1)} %get-tuple-element.86, bf16[1024,1152]{1,0:T(8,128)(2,1)S(1)} %copy-done.99), kind=kOutput, calls=%fused_computation.14 | convolution fusion | flops 4078854144 | bytes 9879552 | tf_op jit(solution)/shard_map/dot_general | solution.py:118
  376.2 6.6 %copy.222 = bf16[1152,1728]{1,0:T(8,128)(2,1)} copy(bf16[1152,1728]{0,1:T(8,128)(2,1)} %convolution_convert_fusion.1) | data formatting | bytes 7962624 | tf_op jit(solution)/shard_map/convert_element_type | solution.py:389
  386.4 9.4 %fusion.189 = f32[1024,1152]{1,0:T(8,128)} fusion(bf16[1024,1728]{0,1:T(8,128)(2,1)} %get-tuple-element.87, bf16[1152,1728]{1,0:T(8,128)(2,1)S(1)} %bitcast.533), kind=kOutput, calls=%fused_computation.426 | convolution fusion | flops 4076863488 | bytes 12238848 | tf_op jit(solution)/shard_map/dot_general | solution.py:112
  395.8 6.2 convolution_convert_fusion.2
  402.0 6.4 %copy.221 = bf16[1152,1728]{1,0:T(8,128)(2,1)} copy(bf16[1152,1728]{0,1:T(8,128)(2,1)} %convolution_convert_fusion.2) | data formatting | bytes 7962624 | tf_op jit(solution)/shard_map/convert_element_type | solution.py:388
  419.7 6.6 %collective-permute-done.71 = bf16[2,64,1728]{2,1,0:T(8,128)(2,1)S(1)} collective-permute-done((bf16[2,64,1728]{2,1,0:T(8,128)(2,1)S(1)}, bf16[2,64,1728]{2,1,0:T(8,128)(2,1)S(1)}, u32[]{:S(2)}, u32[]{:S(2)}) %collective-permute-start.71) | collective-permute-done | bytes 442400 | tf_op jit(solution)/shard_map/ppermute | solution.py:26
  429.5 6.7 %add_convert_fusion = bf16[1024,1152]{1,0:T(8,128)(2,1)} fusion(f32[1024,1152]{1,0:T(8,128)S(1)} %copy-done.103, bf16[1024,1728]{0,1:T(8,128)(2,1)S(1)} %copy-done.104, bf16[1152,1728]{1,0:T(8,128)(2,1)S(1)} %bitcast.531), kind=kOutput, calls=%fused_computation.26 | convolution fusion | flops 4079222784 | bytes 14598144 | tf_op jit(solution)/shard_map/dot_general | solution.py:112
  451.2 19.9 %collective-permute-done.65 = bf16[2,144,1728]{2,1,0:T(8,128)(2,1)S(1)} collective-permute-done((bf16[2,144,1728]{2,1,0:T(8,128)(2,1)S(1)}, bf16[2,144,1728]{2,1,0:T(8,128)(2,1)S(1)}, u32[]{:S(2)}, u32[]{:S(2)}) %collective-permute-start.65) | collective-permute-done | bytes 995360 | tf_op jit(solution)/shard_map/ppermute | solution.py:26
  474.7 8.4 %collective-permute-done.66 = bf16[144,1728]{1,0:T(8,128)(2,1)S(1)} collective-permute-done((bf16[144,1728]{1,0:T(8,128)(2,1)S(1)}, bf16[144,1728]{1,0:T(8,128)(2,1)S(1)}, u32[]{:S(2)}, u32[]{:S(2)}) %collective-permute-start.66) | collective-permute-done | bytes 497696 | tf_op jit(solution)/shard_map/ppermute | solution.py:26
  503.0 6.3 fusion.39
  509.3 7.4 %fusion.34 = f32[256,4,256]{0,2,1:T(8,128)} fusion(f32[768,256,4]{1,0,2:T(8,128)} %fusion.81, f32[4,256,768]{1,2,0:T(8,128)} %copy-done.4, f32[4,256]{1,0:T(4,128)S(1)} %copy-done.76, bf16[2,768,256]{1,2,0:T(8,128)(2,1)S(1)} %copy-done.42), kind=kOutput, calls=%fused_computation.102 | convolution fusion | flops 408160000 | bytes 14032896 | tf_op jit(solution)/shard_map/hqk,kd->qhd/dot_general | solution.py:330
  553.1 5.6 concatenate.124
  573.9 6.2 collective-permute-done.47
  584.8 5.0 collective-permute-done.48
  (600 shorter events, 303.3 us)
Async XLA Ops:
  7.2 192.4 %all-gather.3.cloned.1.call-start = ((), (), s32[]{:S(2)}) async-start(), calls=%async_computation.2 | async-start | bytes 2949120 | tf_op jit(solution)/shard_map/all_gather | solution.py:286
  13.0 21.0 %collective-permute-start.2 = (bf16[36,1664]{1,0:T(8,128)(2,1)S(1)}, bf16[36,1664]{1,0:T(8,128)(2,1)S(1)}, u32[]{:S(2)}, u32[]{:S(2)}) collective-permute-start(bf16[36,1664]{1,0:T(8,128)(2,1)S(1)} %concatenate.103), channel_id=1, source_target_pairs={{0,3},{1,0},{2,1},{3,2},{4,7},{5,4},{6,5},{7,6},{8,11},{9,8},{10,9... | collective-permute-start | bytes 359432 | tf_op jit(solution)/shard_map/ppermute | solution.py:31
  30.3 43.5 %collective-permute-start.20 = (bf16[144,1728]{1,0:T(8,128)(2,1)}, bf16[144,1728]{1,0:T(8,128)(2,1)}, u32[]{:S(2)}, u32[]{:S(2)}) collective-permute-start(bf16[144,1728]{1,0:T(8,128)(2,1)} %param.33), channel_id=1, source_target_pairs={{0,16},{4,20},{8,24},{12,28},{16,0},{20,4},{24,8},{28,12},{1,17},{... | collective-permute-start | bytes 1493000 | tf_op jit(solution)/shard_map/ppermute | solution.py:26
  31.8 24.1 %collective-permute-start.29 = (bf16[64,1728]{1,0:T(8,128)(2,1)S(1)}, bf16[64,1728]{1,0:T(8,128)(2,1)S(1)}, u32[]{:S(2)}, u32[]{:S(2)}) collective-permute-start(bf16[64,1728]{1,0:T(8,128)(2,1)S(1)} %get-tuple-element.132), channel_id=1, source_target_pairs={{0,8},{4,12},{8,0},{12,4},{16,24},{20,28},{24,16},{28,20},{1,9},{5... | collective-permute-start | bytes 663560 | tf_op jit(solution)/shard_map/ppermute | solution.py:26
  60.0 21.2 %collective-permute-start.23 = (bf16[144,1728]{1,0:T(8,128)(2,1)S(1)}, bf16[144,1728]{1,0:T(8,128)(2,1)S(1)}, u32[]{:S(2)}, u32[]{:S(2)}) collective-permute-start(bf16[144,1728]{1,0:T(8,128)(2,1)S(1)} %copy-done.54), channel_id=1, source_target_pairs={{0,8},{4,12},{8,0},{12,4},{16,24},{20,28},{24,16},{28,20},{1,9},{5... | collective-permute-start | bytes 1493000 | tf_op jit(solution)/shard_map/ppermute | solution.py:26
  61.5 21.5 %collective-permute-start.19 = (bf16[2,2,64,1024]{3,2,1,0:T(8,128)(2,1)S(1)}, bf16[2,2,64,1024]{3,2,1,0:T(8,128)(2,1)S(1)}, u32[]{:S(2)}, u32[]{:S(2)}) collective-permute-start(bf16[2,2,64,1024]{3,2,1,0:T(8,128)(2,1)S(1)} %get-tuple-element.128), channel_id=1, source_target_pairs={{0,4},{4,0},{8,12},{12,8},{16,20},{20,16},{24,28},{28,24},{1,5},{5... | collective-permute-start | bytes 1572872 | tf_op jit(solution)/shard_map/ppermute | solution.py:26
  72.3 20.9 %collective-permute-start.8 = (bf16[2,2,64,1664]{3,2,1,0:T(8,128)(2,1)}, bf16[2,2,64,1664]{3,2,1,0:T(8,128)(2,1)}, u32[]{:S(2)}, u32[]{:S(2)}) collective-permute-start(bf16[2,2,64,1664]{3,2,1,0:T(8,128)(2,1)} %get-tuple-element.110), channel_id=1, source_target_pairs={{0,4},{4,0},{8,12},{12,8},{16,20},{20,16},{24,28},{28,24},{1,5},{5... | collective-permute-start | bytes 2555912 | tf_op jit(solution)/shard_map/ppermute | solution.py:26
  73.8 22.9 %collective-permute-start.5 = (bf16[2,2,80,1664]{3,2,0,1:T(8,128)(2,1)}, bf16[2,2,80,1664]{3,2,0,1:T(8,128)(2,1)}, u32[]{:S(2)}, u32[]{:S(2)}) collective-permute-start(bf16[2,2,80,1664]{3,2,0,1:T(8,128)(2,1)} %get-tuple-element.102), channel_id=1, source_target_pairs={{0,4},{4,0},{8,12},{12,8},{16,20},{20,16},{24,28},{28,24},{1,5},{5... | collective-permute-start | bytes 3194888 | tf_op jit(solution)/shard_map/ppermute | solution.py:26
  81.1 60.9 %collective-permute-start.26 = (bf16[80,1728]{1,0:T(8,128)(2,1)}, bf16[80,1728]{1,0:T(8,128)(2,1)}, u32[]{:S(2)}, u32[]{:S(2)}) collective-permute-start(bf16[80,1728]{1,0:T(8,128)(2,1)} %get-tuple-element.130), channel_id=1, source_target_pairs={{0,16},{4,20},{8,24},{12,28},{16,0},{20,4},{24,8},{28,12},{1,17},{... | collective-permute-start | bytes 829448 | tf_op jit(solution)/shard_map/ppermute | solution.py:26
  83.1 61.3 %collective-permute-start.30 = (bf16[2,64,1728]{2,1,0:T(8,128)(2,1)}, bf16[2,64,1728]{2,1,0:T(8,128)(2,1)}, u32[]{:S(2)}, u32[]{:S(2)}) collective-permute-start(bf16[2,64,1728]{2,1,0:T(8,128)(2,1)} %get-tuple-element.138), channel_id=1, source_target_pairs={{0,16},{4,20},{8,24},{12,28},{16,0},{20,4},{24,8},{28,12},{1,17},{... | collective-permute-start | bytes 1327112 | tf_op jit(solution)/shard_map/ppermute | solution.py:26
  85.4 60.4 %collective-permute-start.21 = (bf16[2,144,1728]{2,1,0:T(8,128)(2,1)}, bf16[2,144,1728]{2,1,0:T(8,128)(2,1)}, u32[]{:S(2)}, u32[]{:S(2)}) collective-permute-start(bf16[2,144,1728]{2,1,0:T(8,128)(2,1)} %get-tuple-element.104), channel_id=1, source_target_pairs={{0,8},{4,12},{8,0},{12,4},{16,24},{20,28},{24,16},{28,20},{1,9},{5... | collective-permute-start | bytes 2985992 | tf_op jit(solution)/shard_map/ppermute | solution.py:26
  109.8 24.4 %collective-permute-start.10 = (bf16[2,256,256]{1,2,0:T(8,128)(2,1)}, bf16[2,256,256]{1,2,0:T(8,128)(2,1)}, u32[]{:S(2)}, u32[]{:S(2)}) collective-permute-start(bf16[2,256,256]{1,2,0:T(8,128)(2,1)} %pad_maximum_fusion.36), channel_id=1, source_target_pairs={{0,4},{4,8},{8,12},{12,16},{16,20},{20,24},{24,28},{1,5},{5,9},{9,... | collective-permute-start | bytes 786440 | tf_op jit(solution)/shard_map/ppermute | solution.py:17
  111.8 22.6 %collective-permute-start.9 = (bf16[2,256,256]{1,2,0:T(8,128)(2,1)}, bf16[2,256,256]{1,2,0:T(8,128)(2,1)}, u32[]{:S(2)}, u32[]{:S(2)}) collective-permute-start(bf16[2,256,256]{1,2,0:T(8,128)(2,1)} %pad_maximum_fusion.36), channel_id=1, source_target_pairs={{0,8},{4,12},{8,16},{12,20},{16,24},{20,28},{1,9},{5,13},{9,17},{1... | collective-permute-start | bytes 786440 | tf_op jit(solution)/shard_map/ppermute | solution.py:17
  134.2 26.7 %collective-permute-start.24 = (bf16[2,144,1728]{2,1,0:T(8,128)(2,1)}, bf16[2,144,1728]{2,1,0:T(8,128)(2,1)}, u32[]{:S(2)}, u32[]{:S(2)}) collective-permute-start(bf16[2,144,1728]{2,1,0:T(8,128)(2,1)} %get-tuple-element.106), channel_id=1, source_target_pairs={{0,16},{4,20},{8,24},{12,28},{16,0},{20,4},{24,8},{28,12},{1,17},{... | collective-permute-start | bytes 2985992 | tf_op jit(solution)/shard_map/ppermute | solution.py:26
  142.0 129.7 %reduce-scatter.3.cloned.1.call-start = ((), (), s32[]{:S(2)}) async-start(), calls=%async_computation.3 | async-start | bytes 2949120 | tf_op jit(solution)/shard_map/reduce_scatter | solution.py:293
  145.5 19.0 %collective-permute-start.31 = (bf16[2,2,64,1728]{3,2,1,0:T(8,128)(2,1)S(1)}, bf16[2,2,64,1728]{3,2,1,0:T(8,128)(2,1)S(1)}, u32[]{:S(2)}, u32[]{:S(2)}) collective-permute-start(bf16[2,2,64,1728]{3,2,1,0:T(8,128)(2,1)S(1)} %get-tuple-element.108), channel_id=1, source_target_pairs={{0,4},{4,0},{8,12},{12,8},{16,20},{20,16},{24,28},{28,24},{1,5},{5... | collective-permute-start | bytes 2654216 | tf_op jit(solution)/shard_map/ppermute | solution.py:26
  149.3 31.8 %collective-permute-start.22 = (bf16[2,2,144,1728]{3,2,1,0:T(8,128)(2,1)}, bf16[2,2,144,1728]{3,2,1,0:T(8,128)(2,1)}, u32[]{:S(2)}, u32[]{:S(2)}) collective-permute-start(bf16[2,2,144,1728]{3,2,1,0:T(8,128)(2,1)} %get-tuple-element.89), channel_id=1, source_target_pairs={{0,4},{4,0},{8,12},{12,8},{16,20},{20,16},{24,28},{28,24},{1,5},{5... | collective-permute-start | bytes 5971976 | tf_op jit(solution)/shard_map/ppermute | solution.py:26
  164.5 25.6 %collective-permute-start.25 = (bf16[2,2,144,1728]{3,2,1,0:T(8,128)(2,1)}, bf16[2,2,144,1728]{3,2,1,0:T(8,128)(2,1)}, u32[]{:S(2)}, u32[]{:S(2)}) collective-permute-start(bf16[2,2,144,1728]{3,2,1,0:T(8,128)(2,1)} %get-tuple-element.91), channel_id=1, source_target_pairs={{0,4},{4,0},{8,12},{12,8},{16,20},{20,16},{24,28},{28,24},{1,5},{5... | collective-permute-start | bytes 5971976 | tf_op jit(solution)/shard_map/ppermute | solution.py:26
  225.6 101.9 %all-gather.5.cloned.1.call-start = ((), (), s32[]{:S(2)}) async-start(), calls=%async_computation.4 | async-start | bytes 2949120 | tf_op jit(solution)/shard_map/all_gather | solution.py:300
  277.4 208.5 %reduce-scatter.5.cloned.1.call-start = ((), (), s32[]{:S(2)}) async-start(), calls=%async_computation.5 | async-start | bytes 2949120 | tf_op jit(solution)/shard_map/reduce_scatter | solution.py:308
  348.9 66.0 %collective-permute-start.67 = (bf16[2,2,80,1728]{3,2,1,0:T(8,128)(2,1)}, bf16[2,2,80,1728]{3,2,1,0:T(8,128)(2,1)}, u32[]{:S(2)}, u32[]{:S(2)}) collective-permute-start(bf16[2,2,80,1728]{3,2,1,0:T(8,128)(2,1)} %dynamic-slice_bitcast_fusion.2), channel_id=1, source_target_pairs={{0,4},{4,0},{8,12},{12,8},{16,20},{20,16},{24,28},{28,24},{1,5},{5... | collective-permute-start | bytes 3317768 | tf_op jit(solution)/shard_map/ppermute | solution.py:26
  351.0 60.8 %collective-permute-start.70 = (bf16[2,2,64,1728]{3,2,0,1:T(8,128)(2,1)}, bf16[2,2,64,1728]{3,2,0,1:T(8,128)(2,1)}, u32[]{:S(2)}, u32[]{:S(2)}) collective-permute-start(bf16[2,2,64,1728]{3,2,0,1:T(8,128)(2,1)} %bitcast.489), channel_id=1, source_target_pairs={{0,4},{4,0},{8,12},{12,8},{16,20},{20,16},{24,28},{28,24},{1,5},{5... | collective-permute-start | bytes 2654216 | tf_op jit(solution)/shard_map/ppermute | solution.py:26
  386.0 55.8 %collective-permute-start.64 = (bf16[2,2,144,1728]{3,2,1,0:T(8,128)(2,1)}, bf16[2,2,144,1728]{3,2,1,0:T(8,128)(2,1)}, u32[]{:S(2)}, u32[]{:S(2)}) collective-permute-start(bf16[2,2,144,1728]{3,2,1,0:T(8,128)(2,1)} %dynamic-slice_bitcast_fusion), channel_id=1, source_target_pairs={{0,4},{4,0},{8,12},{12,8},{16,20},{20,16},{24,28},{28,24},{1,5},{5... | collective-permute-start | bytes 5971976 | tf_op jit(solution)/shard_map/ppermute | solution.py:26
  411.7 34.1 %collective-permute-start.61 = (bf16[2,2,144,1728]{3,2,1,0:T(8,128)(2,1)}, bf16[2,2,144,1728]{3,2,1,0:T(8,128)(2,1)}, u32[]{:S(2)}, u32[]{:S(2)}) collective-permute-start(bf16[2,2,144,1728]{3,2,1,0:T(8,128)(2,1)} %dynamic-slice_bitcast_fusion.1), channel_id=1, source_target_pairs={{0,4},{4,0},{8,12},{12,8},{16,20},{20,16},{24,28},{28,24},{1,5},{5... | collective-permute-start | bytes 5971976 | tf_op jit(solution)/shard_map/ppermute | solution.py:26
  418.2 21.2 %collective-permute-start.68 = (bf16[2,80,1728]{2,1,0:T(8,128)(2,1)S(1)}, bf16[2,80,1728]{2,1,0:T(8,128)(2,1)}, u32[]{:S(2)}, u32[]{:S(2)}) collective-permute-start(bf16[2,80,1728]{2,1,0:T(8,128)(2,1)S(1)} %fusion.74), channel_id=1, source_target_pairs={{0,16},{4,20},{8,24},{12,28},{16,0},{20,4},{24,8},{28,12},{1,17},{... | collective-permute-start | bytes 1658888 | tf_op jit(solution)/shard_map/ppermute | solution.py:26
  444.1 27.1 %collective-permute-start.65 = (bf16[2,144,1728]{2,1,0:T(8,128)(2,1)S(1)}, bf16[2,144,1728]{2,1,0:T(8,128)(2,1)S(1)}, u32[]{:S(2)}, u32[]{:S(2)}) collective-permute-start(bf16[2,144,1728]{2,1,0:T(8,128)(2,1)S(1)} %fusion.60), channel_id=1, source_target_pairs={{0,8},{4,12},{8,0},{12,4},{16,24},{20,28},{24,16},{28,20},{1,9},{5... | collective-permute-start | bytes 2985992 | tf_op jit(solution)/shard_map/ppermute | solution.py:26
  447.9 25.0 %collective-permute-start.62 = (bf16[2,144,1728]{2,1,0:T(8,128)(2,1)S(1)}, bf16[2,144,1728]{2,1,0:T(8,128)(2,1)S(1)}, u32[]{:S(2)}, u32[]{:S(2)}) collective-permute-start(bf16[2,144,1728]{2,1,0:T(8,128)(2,1)S(1)} %fusion.59), channel_id=1, source_target_pairs={{0,16},{4,20},{8,24},{12,28},{16,0},{20,4},{24,8},{28,12},{1,17},{... | collective-permute-start | bytes 2985992 | tf_op jit(solution)/shard_map/ppermute | solution.py:26
  519.1 50.3 %collective-permute-start.52 = (bf16[2,2,80,1024]{3,2,1,0:T(8,128)(2,1)}, bf16[2,2,80,1024]{3,2,1,0:T(8,128)(2,1)}, u32[]{:S(2)}, u32[]{:S(2)}) collective-permute-start(bf16[2,2,80,1024]{3,2,1,0:T(8,128)(2,1)} %fusion.70), channel_id=1, source_target_pairs={{0,4},{4,0},{8,12},{12,8},{16,20},{20,16},{24,28},{28,24},{1,5},{5... | collective-permute-start | bytes 1966088 | tf_op jit(solution)/shard_map/ppermute | solution.py:26
  521.3 44.9 %collective-permute-start.55 = (bf16[2,2,64,1024]{3,2,0,1:T(8,128)(2,1)}, bf16[2,2,64,1024]{3,2,0,1:T(8,128)(2,1)}, u32[]{:S(2)}, u32[]{:S(2)}) collective-permute-start(bf16[2,2,64,1024]{3,2,0,1:T(8,128)(2,1)} %fusion.76), channel_id=1, source_target_pairs={{0,4},{4,0},{8,12},{12,8},{16,20},{20,16},{24,28},{28,24},{1,5},{5... | collective-permute-start | bytes 1572872 | tf_op jit(solution)/shard_map/ppermute | solution.py:26
  565.6 26.4 %collective-permute-start.34 = (bf16[2,2,80,1024]{3,2,1,0:T(8,128)(2,1)S(1)}, bf16[2,2,80,1024]{3,2,1,0:T(8,128)(2,1)S(1)}, u32[]{:S(2)}, u32[]{:S(2)}) collective-permute-start(bf16[2,2,80,1024]{3,2,1,0:T(8,128)(2,1)S(1)} %fusion.69), channel_id=1, source_target_pairs={{0,4},{4,0},{8,12},{12,8},{16,20},{20,16},{24,28},{28,24},{1,5},{5... | collective-permute-start | bytes 1966088 | tf_op jit(solution)/shard_map/ppermute | solution.py:26
  572.1 28.6 %collective-permute-start.53 = (bf16[2,80,1024]{2,1,0:T(8,128)(2,1)}, bf16[2,80,1024]{2,1,0:T(8,128)(2,1)}, u32[]{:S(2)}, u32[]{:S(2)}) collective-permute-start(bf16[2,80,1024]{2,1,0:T(8,128)(2,1)} %fusion.95), channel_id=1, source_target_pairs={{0,16},{4,20},{8,24},{12,28},{16,0},{20,4},{24,8},{28,12},{1,17},{... | collective-permute-start | bytes 983048 | tf_op jit(solution)/shard_map/ppermute | solution.py:26
  593.0 22.1 %collective-permute-start.35 = (bf16[2,80,1024]{2,1,0:T(8,128)(2,1)}, bf16[2,80,1024]{2,1,0:T(8,128)(2,1)}, u32[]{:S(2)}, u32[]{:S(2)}) collective-permute-start(bf16[2,80,1024]{2,1,0:T(8,128)(2,1)} %fusion.94), channel_id=1, source_target_pairs={{0,16},{4,20},{8,24},{12,28},{16,0},{20,4},{24,8},{28,12},{1,17},{... | collective-permute-start | bytes 983048 | tf_op jit(solution)/shard_map/ppermute | solution.py:26
  (151 other events, 1140.7 us)
Sparse Core Ops, SparseCore 0:
  142.1 48.7 all-gather.2
  225.7 45.9 reduce-scatter.2
  277.6 49.9 all-gather.4
  436.4 45.9 reduce-scatter.4

commit v2 on v0

v2 whole, which is shorter than its diff:
```python
import functools

import jax
import jax.numpy as jnp
from jax import lax
from jax.experimental import pallas as pl
from jax.experimental.pallas import tpu as pltpu
from jax.sharding import PartitionSpec as P

WINDOW = 512
NORM_EPS = 1e-06
ROPE_BASE = 10000.0
NEGATIVE = -1e30
LANES = 128
VMEM_LIMIT = 56 * 2**20
BF16 = jnp.bfloat16
F32 = jnp.float32


def from_behind(value, steps):
    count = lax.axis_size("seq")
    first, last = (max(0, -steps), min(count, count - steps))
    return lax.ppermute(value, "seq", [(source, source + steps) for source in range(first, last)])


def seq_masks():
    return [1 << bit for bit in range(lax.axis_size("seq").bit_length() - 1)]


def swap(value, axis, mask):
    count = lax.axis_size(axis)
    return lax.ppermute(value, axis, [(source, source ^ mask) for source in range(count)])


def shift(value, axis, steps):
    count = lax.axis_size(axis)
    return lax.ppermute(value, axis, [(source, (source + steps) % count) for source in range(count)])


def diagonal(value):
    seqs, planes = lax.axis_size("seq"), lax.axis_size("fsdp")
    pairs = [
        (seq * planes + plane, (seq ^ 2) * planes + (plane ^ 1))
        for seq in range(seqs)
        for plane in range(planes)
    ]
    return lax.ppermute(value, ("seq", "fsdp"), pairs)


def group_blocks(rows):
    return [diagonal(rows), swap(rows, "seq", 2), swap(rows, "fsdp", 1), rows]


def on_own_slice():
    return (lax.axis_index("seq") // 2) % 2 == lax.axis_index("fsdp") // 2


def ordered(parts):
    parts = [parts[rel] for rel in range(len(parts))]
    if parts[0].shape[0] % 16 == 0:
        return parts
    index = jnp.arange(len(parts), dtype=jnp.int32) ^ lax.axis_index("seq")
    whole = jnp.take(jnp.stack(parts), index, axis=0, mode="clip")
    return [whole.reshape(-1, whole.shape[-1])]


def gather_attn(block):
    parts = {0: block}
    for rel in range(2, lax.axis_size("seq"), 2):
        parts[rel] = swap(block, "seq", rel)
    for rel in list(parts):
        parts[rel ^ 1] = swap(parts[rel], "seq", 1)
    return ordered(parts)


def gather_ffn(block):
    other_plane = swap(block, "fsdp", 2)
    own = on_own_slice()
    mine = jnp.where(own, block, other_plane)
    theirs = jnp.where(own, other_plane, block)
    parts = {0: mine, 2: swap(theirs, "seq", 2)}
    for mask in [mask for mask in seq_masks() if mask > 2] + [1]:
        parts.update({rel ^ mask: swap(part, "seq", mask) for rel, part in parts.items()})
    return ordered(parts)


def add_rounded(first, second):
    return (first.astype(F32) + second.astype(F32)).astype(BF16)


def cut(pair, count):
    if len(pair) == 2:
        return pair
    index = jnp.arange(count, dtype=jnp.int32) ^ lax.axis_index("seq")
    blocks = jnp.take(pair[0].reshape(count, -1, pair[0].shape[-1]), index, axis=0, mode="clip")
    return blocks[0::2], blocks[1::2]


def scatter_ffn(pair):
    keep, send = cut(pair, lax.axis_size("seq"))
    part = add_rounded(keep, swap(send, "seq", 1))
    for mask in [mask for mask in seq_masks() if mask > 2][::-1]:
        half = part.shape[0] // 2
        part = add_rounded(part[:half], swap(part[half:], "seq", mask))
    crossed = swap(part[1], "seq", 2)
    own = on_own_slice()
    stays = jnp.where(own, part[0], crossed)
    leaves = jnp.where(own, crossed, part[0])
    return stays.astype(F32) + swap(leaves, "fsdp", 2).astype(F32)


def scatter_attn(pair):
    keep, send = cut(pair, lax.axis_size("seq"))
    part = add_rounded(keep, swap(send, "seq", 1))
    rows = part[0].astype(F32)
    for index in range(1, part.shape[0]):
        rows = rows + swap(part[index], "seq", 2 * index).astype(F32)
    planes = lax.axis_size("fsdp")
    blocks = rows.reshape((planes, -1) + rows.shape[1:])
    mine = lax.axis_index("fsdp")
    total = lax.dynamic_index_in_dim(blocks, mine, 0, keepdims=False)
    for steps in range(1, planes):
        send = lax.dynamic_index_in_dim(blocks, (mine + steps) % planes, 0, keepdims=False)
        total = total + shift(send.astype(BF16), "fsdp", steps).astype(F32)
    return total


def dot(left, right):
    return jnp.dot(left, right, preferred_element_type=F32)


def dot_t(left, right):
    return lax.dot_general(left, right, (((1,), (1,)), ((), ())), preferred_element_type=F32)


def dot_tn(left, right):
    return lax.dot_general(left, right, (((0,), (0,)), ((), ())), preferred_element_type=F32)


def inverse_rms(values):
    return lax.rsqrt(jnp.mean(values * values, axis=-1, keepdims=True) + NORM_EPS)


def norm_back(normed, scale, gain, upstream):
    scaled = upstream * gain
    back = scale * (scaled - normed * jnp.mean(scaled * normed, axis=-1, keepdims=True))
    return back, jnp.sum(upstream * normed, axis=0, keepdims=True)


def rotate(values, cosine, sine):
    half = values.shape[-1] // 2
    first, second = values[:, :half], values[:, half:]
    return jnp.concatenate(
        [first * cosine - second * sine, second * cosine + first * sine], axis=-1
    )


def iota(shape, dim):
    return lax.broadcasted_iota(jnp.int32, shape, dim)


def unit(shape, hits):
    return jnp.where(hits, 1.0, 0.0).astype(BF16)


def spread_matrix(narrow, wide, narrow_rows, wide_rows):
    row, col = iota((narrow, wide), 0), iota((narrow, wide), 1)
    return unit((narrow, wide), col == (row // narrow_rows) * wide_rows + row % narrow_rows)


def tiles_of(width, step):
    return [(start, min(step, width - start)) for start in range(0, width, step)]


def start_placing(parts, dest, sems, base, seq):
    rows = parts[0].shape[0]
    copies = []
    for rel, part in enumerate(parts):
        start = pl.multiple_of((seq ^ rel) * rows, 16) if len(parts) > 1 else 0
        copies.append(
            pltpu.make_async_copy(part, dest.at[pl.ds(start, rows), :], sems.at[base + rel])
        )
    for copy in copies:
        copy.start()
    return copies


def start_cutting(whole, outs, sems, base, seq):
    if len(outs) == 1:
        copies = [pltpu.make_async_copy(whole, outs[0], sems.at[base])]
    else:
        half, rows = outs[0].shape[0], outs[0].shape[1]
        copies = []
        for rel in range(2 * half):
            start = pl.multiple_of((seq ^ rel) * rows, 16)
            copies.append(
                pltpu.make_async_copy(
                    whole.at[pl.ds(start, rows), :], outs[rel % 2].at[rel // 2], sems.at[base + rel]
                )
            )
    for copy in copies:
        copy.start()
    return copies


def cut_shapes(height, width, count):
    rows = height // count
    if rows % 16:
        return [jax.ShapeDtypeStruct((height, width), BF16)]
    return [jax.ShapeDtypeStruct((count // 2, rows, width), BF16)] * 2


def wait_all(copies):
    for copy in copies:
        copy.wait()


SMEM_SPEC = pl.BlockSpec(memory_space=pltpu.SMEM)
VMEM_SPEC = pl.BlockSpec(memory_space=pltpu.VMEM)
ANY_SPEC = pl.BlockSpec(memory_space=pl.ANY)


def call(kernel, outs, out_specs, ins, in_specs, scratch=(), flops=0, moved=0, exps=0):
    return pl.pallas_call(
        kernel,
        out_shape=tuple(outs),
        in_specs=list(in_specs),
        out_specs=tuple(out_specs),
        scratch_shapes=list(scratch),
        compiler_params=pltpu.CompilerParams(vmem_limit_bytes=VMEM_LIMIT),
        cost_estimate=pl.CostEstimate(flops=flops, bytes_accessed=moved, transcendentals=exps),
    )(*ins)


def shape_of(dims, dtype):
    return jax.ShapeDtypeStruct(dims, dtype)


def pack_kernel(wq_ref, wk_ref, wv_ref, *refs):
    wide, narrow, out_ref = refs[:4], refs[4:6], refs[6]
    rows, heads_width, head_dim = wq_ref.shape[0], wq_ref.shape[1], wk_ref.shape[1]
    out_ref[:, :heads_width] = wq_ref[...]
    out_ref[:, heads_width : heads_width + head_dim] = wk_ref[...]
    out_ref[:, heads_width + head_dim : heads_width + 2 * head_dim] = wv_ref[...]
    row = iota((16, rows), 0)
    held = jnp.zeros((16, rows), F32)
    for index, ref in enumerate(wide):
        held = held + jnp.where(row == index, ref[...].astype(F32), 0.0)
    small = narrow[0].shape[1]
    fit = unit((small, rows), iota((small, rows), 0) == iota((small, rows), 1))
    for index, ref in enumerate(narrow):
        spread = dot(jnp.broadcast_to(ref[...].astype(F32), (16, small)).astype(BF16), fit)
        held = held + jnp.where(row == 4 + index, spread, 0.0)
    place = unit((16, LANES), iota((16, LANES), 0) == iota((16, LANES), 1))
    out_ref[:, heads_width + 2 * head_dim :] = dot_tn(held.astype(BF16), place).astype(BF16)


def pack_first(w_query, w_key, w_value, wide, narrow):
    rows = w_query.shape[0]
    width = w_query.shape[1] + 2 * w_key.shape[1] + LANES
    ins = [w_query, w_key, w_value] + [vec.reshape(1, -1) for vec in wide + narrow]
    return call(
        pack_kernel,
        [shape_of((rows, width), BF16)],
        [VMEM_SPEC],
        ins,
        [VMEM_SPEC] * len(ins),
    )[0]


def planes_kernel(place_ref, *refs):
    parts, out_ref = refs[:-1], refs[-1]
    count, rows = len(parts), parts[0].shape[0]
    total = None
    for steps, part in enumerate(parts):
        plane = lax.rem(place_ref[1] - steps + count, count)
        row, col = iota((count * rows, rows), 0), iota((count * rows, rows), 1)
        term = dot(unit((count * rows, rows), row == col + plane * rows), part[...])
        total = term if total is None else total + term
    out_ref[...] = total.astype(BF16)


def gather_planes(block, place):
    count = lax.axis_size("fsdp")
    parts = [block] + [shift(block, "fsdp", steps) for steps in range(1, count)]
    rows, width = block.shape
    return call(
        planes_kernel,
        [shape_of((count * rows, width), BF16)],
        [VMEM_SPEC],
        [place] + parts,
        [SMEM_SPEC] + [VMEM_SPEC] * count,
        flops=2 * count * count * rows * rows * width,
        moved=4 * count * rows * width,
    )[0]


def attend_kernel(
    part_count,
    narrow_rows,
    wide_rows,
    head_count,
    place_ref,
    near_ref,
    back_ref,
    far_ref,
    cos_ref,
    sin_ref,
    low_ref,
    *refs,
):
    parts = refs[:part_count]
    (
        attn_in_ref,
        query_lin_ref,
        key_lin_ref,
        query_ref,
        keys_ref,
        probs_ref,
        attended_ref,
        gains_ref,
        small_gains_ref,
    ) = refs[part_count : part_count + 9]
    weights, inside, sems = refs[part_count + 9 :]
    copies = start_placing(parts, weights, sems, 0, place_ref[0])
    rows, width = near_ref.shape
    head_dim = key_lin_ref.shape[1]
    heads_width = head_count * head_dim
    score_scale = head_dim**-0.5
    blocks = [far_ref, back_ref, near_ref]
    scales = []
    for ref in blocks:
        scales.append(inverse_rms(ref[...].astype(F32)))
    wait_all(copies)
    gain_cols = weights[:, heads_width + 2 * head_dim :]
    pick = unit((8, LANES), iota((8, LANES), 0) == iota((8, LANES), 1))
    gains = dot_t(pick, gain_cols)
    spread = spread_matrix(head_dim, width, narrow_rows, wide_rows)
    small_gains = dot_t(gains.astype(BF16), spread)
    gains_ref[...] = gains
    small_gains_ref[...] = small_gains
    gain_an, gain_q, gain_k = gains[0:1], small_gains[4:5], small_gains[5:6]
    for index, ref in enumerate(blocks):
        normed = ref[...].astype(F32) * scales[index] * gain_an
        inside[index * rows : (index + 1) * rows, :] = normed.astype(BF16)
    attn_in_ref[...] = inside[2 * rows :, :]
    for index in range(3):
        span = slice(index * rows, (index + 1) * rows)
        part_in = inside[span, :]
        key_lin = dot(part_in, weights[:, heads_width : heads_width + head_dim])
        value = dot(part_in, weights[:, heads_width + head_dim : heads_width + 2 * head_dim])
        key = rotate(key_lin * inverse_rms(key_lin) * gain_k, cos_ref[span, :], sin_ref[span, :])
        keys_ref[span, :head_dim] = key.astype(BF16)
        keys_ref[span, head_dim:] = value.astype(BF16)
        if index == 2:
            key_lin_ref[...] = key_lin
    cosine, sine = cos_ref[2 * rows :, :], sin_ref[2 * rows :, :]
    column = iota((rows, 3 * rows), 1)
    seen = (column >= low_ref[...]) & (column <= iota((rows, 3 * rows), 0) + 2 * rows)
    for head in range(head_count):
        lanes = slice(head * head_dim, (head + 1) * head_dim)
        query_lin = dot(inside[2 * rows :, :], weights[:, lanes])
        query_lin_ref[:, lanes] = query_lin
        query = rotate(query_lin * inverse_rms(query_lin) * gain_q, cosine, sine).astype(BF16)
        query_ref[:, lanes] = query
        scores = jnp.where(seen, dot_t(query, keys_ref[:, :head_dim]) * score_scale, NEGATIVE)
        raised = jnp.exp(scores - jnp.max(scores, axis=-1, keepdims=True))
        probs = (raised / jnp.sum(raised, axis=-1, keepdims=True)).astype(BF16)
        probs_ref[head * rows : (head + 1) * rows, :] = probs
        attended_ref[:, lanes] = dot(probs, keys_ref[:, head_dim:]).astype(BF16)


def attend(place, tokens3, cosine, sine, lowest, parts, head_count, head_dim, narrow_rows, wide_rows):
    rows, width = tokens3[0].shape
    heads_width = head_count * head_dim
    pack = parts[0].shape[1]
    outs = [
        shape_of((rows, width), BF16),
        shape_of((rows, heads_width), F32),
        shape_of((rows, head_dim), F32),
        shape_of((rows, heads_width), BF16),
        shape_of((3 * rows, 2 * head_dim), BF16),
        shape_of((head_count * rows, 3 * rows), BF16),
        shape_of((rows, heads_width), BF16),
        shape_of((8, width), F32),
        shape_of((8, head_dim), F32),
    ]
    return call(
        functools.partial(attend_kernel, len(parts), narrow_rows, wide_rows, head_count),
        outs,
        [VMEM_SPEC] * len(outs),
        [place] + list(tokens3) + [cosine, sine, lowest] + parts,
        [SMEM_SPEC] + [VMEM_SPEC] * 6 + [ANY_SPEC] * len(parts),
        [
            pltpu.VMEM((width, pack), BF16),
            pltpu.VMEM((3 * rows, width), BF16),
            pltpu.SemaphoreType.DMA((len(parts),)),
        ],
        flops=2 * rows * width * (heads_width + 6 * head_dim) + 12 * rows * rows * heads_width,
        moved=2 * width * pack + 16 * rows * width,
        exps=3 * head_count * rows * rows,
    )


def post_kernel(part_count, place_ref, tokens_ref, attended_ref, gains_ref, *refs):
    parts = refs[:part_count]
    attn_out_ref, middle_ref, ffn_in_ref, weights, sems = refs[part_count:]
    copies = start_placing(parts, weights, sems, 0, place_ref[0])
    wait_all(copies)
    attn_out = dot_t(attended_ref[...], weights[...])
    attn_out_ref[...] = attn_out
    middle = tokens_ref[...].astype(F32) + attn_out * inverse_rms(attn_out) * gains_ref[1:2, :]
    middle_ref[...] = middle
    ffn_in_ref[...] = (middle * inverse_rms(middle) * gains_ref[2:3, :]).astype(BF16)


def post_attention(place, tokens, attended, gains, parts):
    rows, width = tokens.shape
    inner = attended.shape[1]
    return call(
        functools.partial(post_kernel, len(parts)),
        [shape_of((rows, width), F32), shape_of((rows, width), F32), shape_of((rows, width), BF16)],
        [VMEM_SPEC] * 3,
        [place, tokens, attended, gains] + parts,
        [SMEM_SPEC] + [VMEM_SPEC] * 3 + [ANY_SPEC] * len(parts),
        [pltpu.VMEM((width, inner), BF16), pltpu.SemaphoreType.DMA((len(parts),))],
        flops=2 * rows * width * inner,
        moved=2 * width * inner + 14 * rows * width,
    )


def gelu_pair(gate):
    square = gate * gate
    tanh = jnp.tanh(gate * (0.7978845608028654 + 0.035677408136300125 * square))
    half = 0.5 + 0.5 * tanh
    value = gate * half
    slope = half + value * (1.0 - tanh) * (0.7978845608028654 + 0.10703222440890037 * square)
    return value, slope


def gate_up_kernel(part_count, place_ref, *refs):
    blocks, refs = refs[:4], refs[4:]
    gate_parts, up_parts = refs[:part_count], refs[part_count : 2 * part_count]
    act_ref, gate_slope_ref, up_slope_ref, held, gate_w, up_w, sems = refs[2 * part_count :]
    step = pl.program_id(0)

    @pl.when(step == 0)
    def _():
        copies = start_placing(gate_parts, gate_w, sems, 0, place_ref[0])
        copies += start_placing(up_parts, up_w, sems, part_count, place_ref[0])
        wait_all(copies)

    for index, block in enumerate(blocks):

        @pl.when(step == index)
        def _(block=block):
            held[...] = block[...]

    rows_in = held[...]
    for start, size in tiles_of(gate_w.shape[1], 256):
        lanes = slice(start, start + size)
        gate = dot(rows_in, gate_w[:, lanes])
        up = dot(rows_in, up_w[:, lanes])
        value, slope = gelu_pair(gate)
        act_ref[:, lanes] = (value * up).astype(BF16)
        gate_slope_ref[:, lanes] = (slope * up).astype(BF16)
        up_slope_ref[:, lanes] = value.astype(BF16)


def gate_up(place, blocks, gate_parts, up_parts):
    rows, width = blocks[0].shape
    hidden = gate_parts[0].shape[1]
    count = len(gate_parts)
    out = shape_of((4 * rows, hidden), BF16)
    return pl.pallas_call(
        functools.partial(gate_up_kernel, count),
        out_shape=(out,) * 3,
        grid=(4,),
        in_specs=[SMEM_SPEC]
        + [pl.BlockSpec((rows, width), lambda step: (0, 0))] * 4
        + [ANY_SPEC] * (2 * count),
        out_specs=(pl.BlockSpec((rows, hidden), lambda step: (step, 0)),) * 3,
        scratch_shapes=[
            pltpu.VMEM((rows, width), BF16),
            pltpu.VMEM((width, hidden), BF16),
            pltpu.VMEM((width, hidden), BF16),
            pltpu.SemaphoreType.DMA((2 * count,)),
        ],
        compiler_params=pltpu.CompilerParams(vmem_limit_bytes=VMEM_LIMIT),
        cost_estimate=pl.CostEstimate(
            flops=16 * rows * width * hidden,
            bytes_accessed=4 * width * hidden + 24 * rows * hidden,
            transcendentals=4 * rows * hidden,
        ),
    )(place, *blocks, *gate_parts, *up_parts)


def down_kernel(part_count, first, span, place_ref, act_ref, *refs):
    parts = refs[:part_count]
    outs = refs[part_count : part_count + span]
    held, weights, sems, act_sem = refs[part_count + span :]
    rows = outs[0].shape[0]
    fetch = pltpu.make_async_copy(
        act_ref.at[pl.ds(first * rows, span * rows), :], held, act_sem.at[0]
    )
    fetch.start()
    wait_all(start_placing(parts, weights, sems, 0, place_ref[0]))
    fetch.wait()
    for index, out in enumerate(outs):
        for start, size in tiles_of(weights.shape[0], 384):
            out[:, start : start + size] = dot_t(
                held[index * rows : (index + 1) * rows, :], weights[start : start + size, :]
            ).astype(BF16)


def down(place, act, first, span, parts):
    rows, hidden = act.shape[0] // 4, act.shape[1]
    width = parts[0].shape[0] * len(parts)
    return call(
        functools.partial(down_kernel, len(parts), first, span),
        [shape_of((rows, width), BF16)] * span,
        [VMEM_SPEC] * span,
        [place, act] + parts,
        [SMEM_SPEC, ANY_SPEC] + [ANY_SPEC] * len(parts),
        [
            pltpu.VMEM((span * rows, hidden), BF16),
            pltpu.VMEM((width, hidden), BF16),
            pltpu.SemaphoreType.DMA((len(parts),)),
            pltpu.SemaphoreType.DMA((1,)),
        ],
        flops=2 * span * rows * hidden * width,
        moved=2 * width * hidden + 2 * span * rows * (width + hidden),
    )


def turn_kernel(
    own_ref, far_ref, across_ref, along_ref, middle_ref, upstream_ref, gains_ref, *outs
):
    output_ref, back_ref, gain_grad_ref = outs
    total = own_ref[...].astype(F32) + far_ref[...].astype(F32)
    total = total + across_ref[...].astype(F32) + along_ref[...].astype(F32)
    scale = inverse_rms(total)
    normed = total * scale
    gain = gains_ref[3:4, :]
    output_ref[...] = (middle_ref[...] + normed * gain).astype(BF16)
    back, gain_grad = norm_back(normed, scale, gain, upstream_ref[...].astype(F32))
    back_ref[...] = back.astype(BF16)
    gain_grad_ref[...] = gain_grad


def turn(sums, middle, upstream, gains):
    rows, width = middle.shape
    return call(
        turn_kernel,
        [shape_of((rows, width), BF16), shape_of((rows, width), BF16), shape_of((1, width), F32)],
        [VMEM_SPEC] * 3,
        list(sums) + [middle, upstream, gains],
        [VMEM_SPEC] * 7,
        moved=20 * rows * width,
    )


def ffn_back_kernel(part_count, first, span, place_ref, *refs):
    backs, refs = refs[:span], refs[span:]
    gate_slope_ref, up_slope_ref = refs[:2]
    refs = refs[2:]
    down_parts, gate_parts, up_parts = [
        refs[index * part_count : (index + 1) * part_count] for index in range(3)
    ]
    refs = refs[3 * part_count :]
    outs, refs = refs[:span], refs[span:]
    d_gate_ref, d_up_ref, gate_slope, up_slope, down_w, gate_w, up_w, sems, slope_sems = refs
    rows = outs[0].shape[0]
    seq = place_ref[0]
    copies = start_placing(down_parts, down_w, sems, 0, seq)
    fetches = [
        pltpu.make_async_copy(
            source.at[pl.ds(first * rows, span * rows), :], dest, slope_sems.at[index]
        )
        for index, (source, dest) in enumerate(
            [(gate_slope_ref, gate_slope), (up_slope_ref, up_slope)]
        )
    ]
    for fetch in fetches:
        fetch.start()
    later = start_placing(gate_parts, gate_w, sems, part_count, seq)
    later += start_placing(up_parts, up_w, sems, 2 * part_count, seq)
    wait_all(copies)
    wait_all(fetches)
    for index in range(span):
        part = slice(index * rows, (index + 1) * rows)
        for start, size in tiles_of(down_w.shape[1], 256):
            lanes = slice(start, start + size)
            d_act = dot(backs[index][...], down_w[:, lanes])
            d_gate_ref[part, lanes] = (d_act * gate_slope[part, lanes].astype(F32)).astype(BF16)
            d_up_ref[part, lanes] = (d_act * up_slope[part, lanes].astype(F32)).astype(BF16)
    wait_all(later)
    for index in range(span):
        part = slice(index * rows, (index + 1) * rows)
        for start, size in tiles_of(gate_w.shape[0], 384):
            lanes = slice(start, start + size)
            total = dot_t(d_gate_ref[part, :], gate_w[lanes, :])
            total = total + dot_t(d_up_ref[part, :], up_w[lanes, :])
            outs[index][:, lanes] = total.astype(BF16)


def ffn_back(place, backs, first, gate_slope, up_slope, down_parts, gate_parts, up_parts):
    span = len(backs)
    rows, width = backs[0].shape
    hidden = gate_slope.shape[1]
    count = len(down_parts)
    hidden_out = shape_of((span * rows, hidden), BF16)
    return call(
        functools.partial(ffn_back_kernel, count, first, span),
        [shape_of((rows, width), BF16)] * span + [hidden_out] * 2,
        [VMEM_SPEC] * (span + 2),
        [place] + list(backs) + [gate_slope, up_slope] + down_parts + gate_parts + up_parts,
        [SMEM_SPEC] + [VMEM_SPEC] * span + [ANY_SPEC] * (2 + 3 * count),
        [
            pltpu.VMEM((span * rows, hidden), BF16),
            pltpu.VMEM((span * rows, hidden), BF16),
            pltpu.VMEM((width, hidden), BF16),
            pltpu.VMEM((width, hidden), BF16),
            pltpu.VMEM((width, hidden), BF16),
            pltpu.SemaphoreType.DMA((3 * count,)),
            pltpu.SemaphoreType.DMA((2,)),
        ],
        flops=6 * span * rows * hidden * width,
        moved=6 * width * hidden + 12 * span * rows * hidden,
    )


def weight_grad_kernel(left_count, right_count, place_ref, *refs):
    lefts, rights = refs[:left_count], refs[left_count : left_count + right_count]
    refs = refs[left_count + right_count :]
    outs, (left, right, whole, sems) = refs[:-4], refs[-4:]
    copies = []
    for pieces, dest in ((lefts, left), (rights, right)):
        start = 0
        for piece in pieces:
            size = piece.shape[0]
            copies.append(
                pltpu.make_async_copy(piece, dest.at[pl.ds(start, size), :], sems.at[len(copies)])
            )
            start += size
    for copy in copies:
        copy.start()
    wait_all(copies)
    for start, size in tiles_of(right.shape[1], 256):
        lanes = slice(start, start + size)
        whole[:, lanes] = dot_tn(left[...], right[:, lanes]).astype(BF16)
    wait_all(start_cutting(whole, outs, sems, 0, place_ref[0]))


def weight_grad(place, lefts, rights):
    height, width = lefts[0].shape[1], rights[0].shape[1]
    rows = sum(piece.shape[0] for piece in lefts)
    count = lax.axis_size("seq")
    outs = cut_shapes(height, width, count)
    return call(
        functools.partial(weight_grad_kernel, len(lefts), len(rights)),
        outs,
        [ANY_SPEC] * len(outs),
        [place] + list(lefts) + list(rights),
        [SMEM_SPEC] + [ANY_SPEC] * (len(lefts) + len(rights)),
        [
            pltpu.VMEM((rows, height), BF16),
            pltpu.VMEM((rows, width), BF16),
            pltpu.VMEM((height, width), BF16),
            pltpu.SemaphoreType.DMA((max(count, len(lefts) + len(rights)),)),
        ],
        flops=2 * rows * height * width,
        moved=2 * (rows * (height + width) + height * width),
    )


def attend_back_kernel(
    part_count,
    first_count,
    out_count,
    head_count,
    place_ref,
    own_ref,
    far_ref,
    across_ref,
    along_ref,
    middle_ref,
    upstream_ref,
    attn_out_ref,
    gains_ref,
    small_gains_ref,
    attended_ref,
    attn_in_ref,
    query_lin_ref,
    query_ref,
    keys_ref,
    probs_ref,
    cos_ref,
    sin_ref,
    *refs,
):
    out_parts, refs = refs[:part_count], refs[part_count:]
    first_parts, refs = refs[:first_count], refs[first_count:]
    grads, refs = refs[:out_count], refs[out_count:]
    d_middle_ref, d_in_ref, far_halo_ref, back_halo_ref, near_ref, rows_ref, query_gain_ref = refs[:7]
    out_w, first_w, whole, d_query, d_keys, sems = refs[7:]
    rows, width = middle_ref.shape
    head_dim = keys_ref.shape[1] // 2
    heads_width = head_count * head_dim
    score_scale = head_dim**-0.5
    seq = place_ref[0]
    copies = start_placing(out_parts, out_w, sems, 0, seq)
    later = start_placing(first_parts, first_w, sems, part_count, seq)
    total = own_ref[...].astype(F32) + far_ref[...].astype(F32)
    total = total + across_ref[...].astype(F32) + along_ref[...].astype(F32)
    middle = middle_ref[...]
    scale = inverse_rms(middle)
    back, grad_fn = norm_back(middle * scale, scale, gains_ref[2:3, :], total)
    d_middle = upstream_ref[...].astype(F32) + back
    d_middle_ref[...] = d_middle
    attn_out = attn_out_ref[...]
    scale = inverse_rms(attn_out)
    d_attn_out, grad_ap = norm_back(attn_out * scale, scale, gains_ref[1:2, :], d_middle)
    row = iota((8, width), 0)
    rows_ref[...] = jnp.where(row == 1, grad_ap, 0.0) + jnp.where(row == 2, grad_fn, 0.0)
    d_attn_low = d_attn_out.astype(BF16)
    for start, size in tiles_of(heads_width, 256):
        lanes = slice(start, start + size)
        whole[:, start : start + size] = dot_tn(d_attn_low, attended_ref[:, lanes]).astype(BF16)
    wait_all(copies)
    cosine, sine = cos_ref[2 * rows :, :], sin_ref[2 * rows :, :]
    gain_q = small_gains_ref[4:5, :]
    query_gain = jnp.zeros((1, head_dim), F32)
    for head in range(head_count):
        lanes = slice(head * head_dim, (head + 1) * head_dim)
        d_attended = dot(d_attn_low, out_w[:, lanes]).astype(BF16)
        probs_low = probs_ref[head * rows : (head + 1) * rows, :]
        probs = probs_low.astype(F32)
        d_probs = dot_t(d_attended, keys_ref[:, head_dim:])
        delta = jnp.sum(probs * d_probs, axis=-1, keepdims=True)
        d_scores = (probs * (d_probs - delta) * score_scale).astype(BF16)
        d_rotated = dot(d_scores, keys_ref[:, :head_dim])
        d_key = dot_tn(d_scores, query_ref[:, lanes])
        d_value = dot_tn(probs_low, d_attended)
        if head == 0:
            d_keys[:, :head_dim] = d_key
            d_keys[:, head_dim:] = d_value
        else:
            d_keys[:, :head_dim] += d_key
            d_keys[:, head_dim:] += d_value
        query_lin = query_lin_ref[:, lanes]
        scale = inverse_rms(query_lin)
        d_normed = rotate(d_rotated, cosine, -sine)
        back, gain_grad = norm_back(query_lin * scale, scale, gain_q, d_normed)
        query_gain = query_gain + gain_grad
        d_query[:, lanes] = back.astype(BF16)
    query_gain_ref[...] = query_gain
    far_halo_ref[...] = d_keys[:rows, :].astype(BF16)
    back_halo_ref[...] = d_keys[rows : 2 * rows, :].astype(BF16)
    near_ref[...] = d_keys[2 * rows :, :]
    for start, size in tiles_of(heads_width, 256):
        lanes = slice(start, start + size)
        whole[:, heads_width + start : heads_width + start + size] = dot_tn(
            attn_in_ref[...], d_query[:, lanes]
        ).astype(BF16)
    cuts = start_cutting(whole, grads, sems, part_count + first_count, seq)
    wait_all(later)
    for start, size in tiles_of(width, 384):
        lanes = slice(start, start + size)
        d_in_ref[:, lanes] = dot_t(d_query[...], first_w[lanes, :heads_width])
    wait_all(cuts)


def attend_back(place, sums, saved, cosine, sine, out_parts, first_parts, head_count):
    middle, upstream, attn_out, gains, small_gains, attended, attn_in, query_lin, query, keys, probs = saved
    rows, width = middle.shape
    head_dim = keys.shape[1] // 2
    heads_width = head_count * head_dim
    count = lax.axis_size("seq")
    cuts = cut_shapes(width, 2 * heads_width, count)
    outs = cuts + [
        shape_of((rows, width), F32),
        shape_of((rows, width), F32),
        shape_of((rows, 2 * head_dim), BF16),
        shape_of((rows, 2 * head_dim), BF16),
        shape_of((rows, 2 * head_dim), F32),
        shape_of((8, width), F32),
        shape_of((1, head_dim), F32),
    ]
    ins = [place] + list(sums) + list(saved) + [cosine, sine] + out_parts + first_parts
    return call(
        functools.partial(
            attend_back_kernel, len(out_parts), len(first_parts), len(cuts), head_count
        ),
        outs,
        [ANY_SPEC] * len(cuts) + [VMEM_SPEC] * 7,
        ins,
        [SMEM_SPEC] + [VMEM_SPEC] * 17 + [ANY_SPEC] * (len(out_parts) + len(first_parts)),
        [
            pltpu.VMEM((width, heads_width), BF16),
            pltpu.VMEM((width, first_parts[0].shape[1]), BF16),
            pltpu.VMEM((width, 2 * heads_width), BF16),
            pltpu.VMEM((rows, heads_width), BF16),
            pltpu.VMEM((3 * rows, 2 * head_dim), F32),
            pltpu.SemaphoreType.DMA((len(out_parts) + len(first_parts) + count,)),
        ],
        flops=8 * rows * width * heads_width + 30 * rows * rows * heads_width,
        moved=12 * width * heads_width + 30 * rows * width,
    )


def finish_kernel(
    first_count,
    out_count,
    narrow_rows,
    wide_rows,
    place_ref,
    near_ref,
    back_ref,
    far_ref,
    key_lin_ref,
    small_gains_ref,
    gains_ref,
    cos_ref,
    sin_ref,
    attn_in_ref,
    tokens_ref,
    d_middle_ref,
    d_in_ref,
    rows_ref,
    ffn_post_ref,
    query_gain_ref,
    *refs,
):
    first_parts, refs = refs[:first_count], refs[first_count:]
    grads, (input_grad_ref, first_w, whole, d_low, sems) = refs[:out_count], refs[out_count:]
    rows, width = tokens_ref.shape
    head_dim = key_lin_ref.shape[1]
    seq = place_ref[0]
    copies = start_placing(first_parts, first_w, sems, 0, seq)
    d_keys = near_ref[...] + back_ref[...].astype(F32) + far_ref[...].astype(F32)
    key_lin = key_lin_ref[...]
    scale = inverse_rms(key_lin)
    d_normed = rotate(d_keys[:, :head_dim], cos_ref[2 * rows :, :], -sin_ref[2 * rows :, :])
    back, key_gain = norm_back(key_lin * scale, scale, small_gains_ref[5:6, :], d_normed)
    d_low[:, :head_dim] = back.astype(BF16)
    d_low[:, head_dim:] = d_keys[:, head_dim:].astype(BF16)
    whole[:, : 2 * head_dim] = dot_tn(attn_in_ref[...], d_low[...]).astype(BF16)
    wait_all(copies)
    heads_width = first_w.shape[1] - 2 * head_dim - LANES
    d_attn_in = d_in_ref[...] + dot_t(
        d_low[...], first_w[:, heads_width : heads_width + 2 * head_dim]
    )
    inputs = tokens_ref[...].astype(F32)
    scale = inverse_rms(inputs)
    back, grad_an = norm_back(inputs * scale, scale, gains_ref[0:1, :], d_attn_in)
    input_grad_ref[...] = d_middle_ref[...] + back
    row = iota((8, width), 0)
    gain_rows = rows_ref[...] + jnp.where(row == 0, grad_an, 0.0)
    gain_rows = gain_rows + jnp.where(row == 3, ffn_post_ref[...], 0.0)
    small_row = iota((8, head_dim), 0)
    small = jnp.where(small_row == 4, query_gain_ref[...], 0.0)
    small = small + jnp.where(small_row == 5, key_gain, 0.0)
    spread = spread_matrix(head_dim, width, narrow_rows, wide_rows)
    gain_rows = gain_rows + dot(small.astype(BF16), spread)
    pick = unit((8, LANES), iota((8, LANES), 0) == iota((8, LANES), 1))
    whole[:, 2 * head_dim :] = dot_tn(gain_rows.astype(BF16), pick).astype(BF16)
    wait_all(start_cutting(whole, grads, sems, first_count, seq))


def finish(place, ins, parts, narrow_rows, wide_rows):
    tokens, key_lin, first_parts = ins[9], ins[3], parts
    rows, width = tokens.shape
    head_dim = key_lin.shape[1]
    count = lax.axis_size("seq")
    pack = 2 * head_dim + LANES
    cuts = cut_shapes(width, pack, count)
    return call(
        functools.partial(finish_kernel, len(parts), len(cuts), narrow_rows, wide_rows),
        cuts + [shape_of((rows, width), F32)],
        [ANY_SPEC] * len(cuts) + [VMEM_SPEC],
        [place] + list(ins) + first_parts,
        [SMEM_SPEC] + [VMEM_SPEC] * len(ins) + [ANY_SPEC] * len(parts),
        [
            pltpu.VMEM((width, first_parts[0].shape[1]), BF16),
            pltpu.VMEM((width, pack), BF16),
            pltpu.VMEM((rows, 2 * head_dim), BF16),
            pltpu.SemaphoreType.DMA((len(parts) + count,)),
        ],
        flops=8 * rows * width * head_dim,
        moved=4 * width * pack + 20 * rows * width,
    )


def layout(lengths, counts, first_slot, row_count):
    starts = jnp.cumsum(lengths) - lengths
    slot_index = first_slot + jnp.arange(row_count, dtype=jnp.int32)
    member = (slot_index[:, None] >= starts[None, :]).astype(jnp.int32)
    document = jnp.sum(member, axis=1) - 1
    onehot = (document[:, None] == jnp.arange(lengths.shape[0], dtype=jnp.int32)[None, :]).astype(
        jnp.int32
    )
    position = slot_index - jnp.sum(onehot * starts[None, :], axis=1)
    padded = jnp.sum(onehot * (lengths - counts)[None, :], axis=1)
    return (position, padded)


def on_device(
    tokens,
    cotangent,
    doc_lengths,
    true_counts,
    w_query,
    w_key,
    w_value,
    w_out,
    w_gate,
    w_up,
    w_down,
    attn_norm_gain,
    query_gain,
    key_gain,
    attn_post_gain,
    ffn_norm_gain,
    ffn_post_gain,
):
    row_count = tokens.shape[1]
    head_dim = w_key.shape[1]
    heads_width = w_query.shape[1]
    head_count = heads_width // head_dim
    seq_index, plane_index = lax.axis_index("seq"), lax.axis_index("fsdp")
    place = jnp.stack([seq_index, plane_index]).astype(jnp.int32)
    inputs, upstream = tokens[0], cotangent[0]
    wide_rows, narrow_rows = attn_norm_gain.shape[0], query_gain.shape[0]

    first_pack = pack_first(
        w_query,
        w_key,
        w_value,
        [attn_norm_gain, attn_post_gain, ffn_norm_gain, ffn_post_gain],
        [query_gain, key_gain],
    )
    first_parts = gather_attn(gather_planes(first_pack, place))
    out_parts = gather_attn(gather_planes(w_out, place))
    gate_parts = gather_ffn(w_gate)
    up_parts = gather_ffn(w_up)
    down_parts = gather_ffn(w_down)

    tokens3 = [from_behind(inputs, 2), from_behind(inputs, 1), inputs]
    first_slot = seq_index * row_count
    position, padded = layout(
        doc_lengths[0], true_counts[0], first_slot - WINDOW, row_count + WINDOW
    )
    frequency = ROPE_BASE ** (-2.0 * jnp.arange(head_dim // 2, dtype=F32) / head_dim)
    angles = position.astype(F32)[:, None] * frequency
    cosine, sine = jnp.cos(angles), jnp.sin(angles)
    reach = jnp.clip(position[WINDOW:] - padded[WINDOW:], 0, WINDOW - 1)
    lowest = (WINDOW + jnp.arange(row_count, dtype=jnp.int32) - reach)[:, None]

    attn_in, query_lin, key_lin, query, keys, probs, attended, gains, small_gains = attend(
        place,
        [tokens3[2], tokens3[1], tokens3[0]],
        cosine,
        sine,
        lowest,
        first_parts,
        head_count,
        head_dim,
        narrow_rows,
        wide_rows,
    )
    attn_out, middle, ffn_in = post_attention(place, inputs, attended, gains, out_parts)
    blocks = group_blocks(ffn_in)
    act, gate_slope, up_slope = gate_up(place, blocks, gate_parts, up_parts)
    (far,) = down(place, act, 0, 1, down_parts)
    far = diagonal(far)
    across, along = down(place, act, 1, 2, down_parts)
    across, along = swap(across, "seq", 2), swap(along, "fsdp", 1)
    (own,) = down(place, act, 3, 1, down_parts)
    output, d_ffn_low, grad_fp = turn([own, far, across, along], middle, upstream, gains)
    backs = group_blocks(d_ffn_low)
    slopes = (gate_slope, up_slope, down_parts, gate_parts, up_parts)
    far, far_gate, far_up = ffn_back(place, backs[:1], 0, *slopes)
    far = diagonal(far)
    across, along, side_gate, side_up = ffn_back(place, backs[1:3], 1, *slopes)
    across, along = swap(across, "seq", 2), swap(along, "fsdp", 1)
    own, own_gate, own_up = ffn_back(place, backs[3:], 3, *slopes)
    grad_down = scatter_ffn(weight_grad(place, backs, [act]))
    grad_gate = scatter_ffn(weight_grad(place, blocks, [far_gate, side_gate, own_gate]))
    grad_up = scatter_ffn(weight_grad(place, blocks, [far_up, side_up, own_up]))
    saved = (
        middle,
        upstream,
        attn_out,
        gains,
        small_gains,
        attended,
        attn_in,
        query_lin,
        query,
        keys,
        probs,
    )
    *head_grads, d_middle, d_in, far_halo, back_halo, near, gain_rows, query_gain_grad = attend_back(
        place, [own, far, across, along], saved, cosine, sine, out_parts, first_parts, head_count
    )
    head_rows = scatter_attn(head_grads)
    ins = [
        near,
        from_behind(back_halo, -1),
        from_behind(far_halo, -2),
        key_lin,
        small_gains,
        gains,
        cosine,
        sine,
        attn_in,
        inputs,
        d_middle,
        d_in,
        gain_rows,
        grad_fp,
        query_gain_grad,
    ]
    *last_grads, input_grad = finish(place, ins, first_parts, narrow_rows, wide_rows)
    last_rows = scatter_attn(last_grads)
    gain_cols = last_rows[:, 2 * head_dim :]
    return (
        output[None],
        input_grad[None],
        head_rows[:, heads_width:],
        last_rows[:, :head_dim],
        last_rows[:, head_dim : 2 * head_dim],
        head_rows[:, :heads_width],
        grad_gate,
        grad_up,
        grad_down,
        gain_cols[:, 0],
        gain_cols[:narrow_rows, 4],
        gain_cols[:narrow_rows, 5],
        gain_cols[:, 1],
        gain_cols[:, 2],
        gain_cols[:, 3],
    )


def solution(mesh):
    rows = P("fsdp", "seq", None)
    shard, tile, vector = P(("seq", "fsdp"), None), P("seq", "fsdp"), P(("seq", "fsdp"))
    groups = P("fsdp", None)
    return jax.shard_map(
        on_device,
        mesh=mesh,
        in_specs=(rows, rows, groups, groups) + (shard,) * 4 + (tile,) * 3 + (vector,) * 6,
        out_specs=(rows, rows) + (shard,) * 4 + (tile,) * 3 + (vector,) * 6,
        check_vma=False,
    )
```

time: 1020 us -> 642 us (0.63)
  blocking collectives: 511 us -> 0 us
  Pallas kernels: 0 us -> 155 us
  matrix products: 131 us -> 0 us
  waiting for transfers between devices: 227 us -> 305 us
  starting transfers between devices: 63.5 us -> 130 us
  between operations: 16.1 us -> 1.85 us
  local copies, waits for them, and re-layouts: 33 us -> 19.2 us
    unnamed x3 -> x0, blocking collectives: 362 us -> none
    ppermute x4 -> x86, waiting for transfers between devices: 3.08 us -> 305 us  [the longest x66 209 us: swap(): lax.ppermute(value, axis, [(source, source ^ mask) for source in range(co...]
    pallas_call x0 -> x18, Pallas kernels: none -> 155 us  [the longest x17 137 us: call(): pl.pallas_call(kernel, out_shape=tuple(outs), in_specs=list(in_specs), ou...]
    all_gather x7 -> x0, waiting for transfers between devices: 155 us -> none  [the longest x1 53.1 us: on_device(): ffn_rows_in = lax.all_gather(ffn_in, 'fsdp', axis=0, tiled=True)]
    all_gather x2 -> x0, blocking collectives: 149 us -> none  [the longest x1 76.8 us: on_device(): lax.all_gather(w_key, ('seq', 'fsdp'), axis=0, tiled=True)]
    dot_general x27 -> x0, matrix products: 131 us -> none  [the longest x7 45.7 us: matmul(): return jnp.dot(left_side, right_side, preferred_element_type=jnp.float32)]
    ppermute x4 -> x86, starting transfers between devices: 8.47 us -> 130 us  [the longest x66 94.6 us: swap(): lax.ppermute(value, axis, [(source, source ^ mask) for source in range(co...]
    reduce_scatter x5 -> x0, waiting for transfers between devices: 64.6 us -> none  [the longest x1 46.8 us: on_device(): lax.psum_scatter(matmul_t(act_low, wd_full).astype(jnp.bfloat16), 'fsdp',...]
  transfers between devices with their start and end apart: 32 -> 86, of which waited for: 9 -> 34; matrix products, arithmetic and copies ran while one was open for 41% -> 5% of each run, Pallas kernels for 0% -> 19%
where the time goes in v2:
time: 642 us; the launch traced here: 637 us
  waiting for transfers between devices  305 us (48%)
  Pallas kernels  155 us (24%)
  starting transfers between devices  130 us (20%)
  other arithmetic  25.3 us (4%)
  local copies, waits for them, and re-layouts  19.2 us (3%)
    ppermute x66, waiting for transfers between devices, swap(): lax.ppermute(value, axis, [(source, source ^ mask) for source in range(co...  209 us
    pallas_call x17, Pallas kernels, call(): pl.pallas_call(kernel, out_shape=tuple(outs), in_specs=list(in_specs), ou...  137 us
    ppermute x66, starting transfers between devices, swap(): lax.ppermute(value, axis, [(source, source ^ mask) for source in range(co...  94.6 us
    ppermute x12, waiting for transfers between devices, shift(): lax.ppermute(value, axis, [(source, (source + steps) % count) for source...  60.1 us
    ppermute x4, waiting for transfers between devices, diagonal(): return lax.ppermute(value, ('seq', 'fsdp'), pairs)  25.6 us
    ppermute x12, starting transfers between devices, shift(): lax.ppermute(value, axis, [(source, (source + steps) % count) for source...  20.2 us
    pallas_call x1, Pallas kernels, gate_up(): pl.pallas_call(functools.partial(gate_up_kernel, count), out_shape=(out,)...  18.1 us
  transfers between devices with their start and end apart: 86, of which 34 were waited for; matrix products, arithmetic and copies ran while one was open for 5% of the time, Pallas kernels for 19%

profile of v2, /device:TPU:0, one launch (start us, length us, event | category | flops | bytes accessed | tf_op | source)
XLA Modules:
  0.0 636.6 jit_solution(10338264071503483619)
XLA Ops:
  25.3 11.4 %collective-permute-done.2.refs_1_ = bf16[36,1664]{1,0:T(8,128)(2,1)S(1)} collective-permute-done((bf16[36,1664]{1,0:T(8,128)(2,1)}, bf16[36,1664]{1,0:T(8,128)(2,1)S(1)}, u32[]{:S(2)}, u32[]{:S(2)}) %collective-permute-start.2) | collective-permute-done | bytes 119840 | tf_op jit(solution)/shard_map/ppermute | solution.py:37
  38.2 14.0 %collective-permute-done.3.refs_2_ = bf16[36,1664]{1,0:T(8,128)(2,1)S(1)} collective-permute-done((bf16[36,1664]{1,0:T(8,128)(2,1)}, bf16[36,1664]{1,0:T(8,128)(2,1)S(1)}, u32[]{:S(2)}, u32[]{:S(2)}) %collective-permute-start.3) | collective-permute-done | bytes 119840 | tf_op jit(solution)/shard_map/ppermute | solution.py:37
  64.0 21.3 %collective-permute-start.33 = (bf16[144,1728]{1,0:T(8,128)(2,1)}, bf16[144,1728]{1,0:T(8,128)(2,1)S(1)}, u32[]{:S(2)}, u32[]{:S(2)}) collective-permute-start(bf16[144,1728]{1,0:T(8,128)(2,1)} %param.26), channel_id=1, source_target_pairs={{0,2},{1,3},{2,0},{3,1},{4,6},{5,7},{6,4},{7,5},{8,10},{9,11},{10,... | collective-permute-start | bytes 1493000 | tf_op jit(solution)/shard_map/ppermute | solution.py:32
  87.1 31.8 %collective-permute-done.33 = bf16[144,1728]{1,0:T(8,128)(2,1)S(1)} collective-permute-done((bf16[144,1728]{1,0:T(8,128)(2,1)}, bf16[144,1728]{1,0:T(8,128)(2,1)S(1)}, u32[]{:S(2)}, u32[]{:S(2)}) %collective-permute-start.33) | collective-permute-done | bytes 497696 | tf_op jit(solution)/shard_map/ppermute | solution.py:32
  119.0 10.6 %collective-permute-done.41 = bf16[144,1728]{1,0:T(8,128)(2,1)S(1)} collective-permute-done((bf16[144,1728]{1,0:T(8,128)(2,1)}, bf16[144,1728]{1,0:T(8,128)(2,1)S(1)}, u32[]{:S(2)}, u32[]{:S(2)}) %collective-permute-start.41) | collective-permute-done | bytes 497696 | tf_op jit(solution)/shard_map/ppermute | solution.py:32
  133.2 9.7 %collective-permute-done.8.refs_4_.refs_12_ = bf16[144,1664]{1,0:T(8,128)(2,1)} collective-permute-done((bf16[144,1664]{1,0:T(8,128)(2,1)S(1)}, bf16[144,1664]{1,0:T(8,128)(2,1)}, u32[]{:S(2)}, u32[]{:S(2)}) %collective-permute-start.8) | collective-permute-done | bytes 479264 | tf_op jit(solution)/shard_map/ppermute | solution.py:32
  148.0 9.6 %collective-permute-done.27.refs_6_.refs_13_.refs_14_ = bf16[144,1728]{1,0:T(8,128)(2,1)S(1)} collective-permute-done((bf16[144,1728]{1,0:T(8,128)(2,1)S(1)}, bf16[144,1728]{1,0:T(8,128)(2,1)S(1)}, u32[]{:S(2)}, u32[]{:S(2)}) %collective-permute-start.27) | collective-permute-done | bytes 497696 | tf_op jit(solution)/shard_map/ppermute | solution.py:32
  157.6 9.1 %collective-permute-done.35.refs_14_.refs_21_.refs_22_ = bf16[144,1728]{1,0:T(8,128)(2,1)S(1)} collective-permute-done((bf16[144,1728]{1,0:T(8,128)(2,1)S(1)}, bf16[144,1728]{1,0:T(8,128)(2,1)S(1)}, u32[]{:S(2)}, u32[]{:S(2)}) %collective-permute-start.35) | collective-permute-done | bytes 497696 | tf_op jit(solution)/shard_map/ppermute | solution.py:32
  170.1 8.4 %collective-permute-done.43.refs_2_.refs_5_.refs_6_ = bf16[144,1728]{1,0:T(8,128)(2,1)S(1)} collective-permute-done((bf16[144,1728]{1,0:T(8,128)(2,1)S(1)}, bf16[144,1728]{1,0:T(8,128)(2,1)S(1)}, u32[]{:S(2)}, u32[]{:S(2)}) %collective-permute-start.43) | collective-permute-done | bytes 497696 | tf_op jit(solution)/shard_map/ppermute | solution.py:32
  185.2 8.2 %collective-permute-done.31.refs_10_.refs_17_.refs_18_ = bf16[144,1728]{1,0:T(8,128)(2,1)} collective-permute-done((bf16[144,1728]{1,0:T(8,128)(2,1)S(1)}, bf16[144,1728]{1,0:T(8,128)(2,1)}, u32[]{:S(2)}, u32[]{:S(2)}) %collective-permute-start.31) | collective-permute-done | bytes 497696 | tf_op jit(solution)/shard_map/ppermute | solution.py:32
  193.3 8.9 %collective-permute-done.39.refs_18_.refs_25_.refs_26_ = bf16[144,1728]{1,0:T(8,128)(2,1)} collective-permute-done((bf16[144,1728]{1,0:T(8,128)(2,1)S(1)}, bf16[144,1728]{1,0:T(8,128)(2,1)}, u32[]{:S(2)}, u32[]{:S(2)}) %collective-permute-start.39) | collective-permute-done | bytes 497696 | tf_op jit(solution)/shard_map/ppermute | solution.py:32
  206.4 10.0 %shard_map.282 = (bf16[256,1152]{1,0:T(8,128)(2,1)}, f32[256,1024]{1,0:T(8,128)}, f32[256,256]{1,0:T(8,128)}, bf16[256,1024]{1,0:T(8,128)(2,1)}, bf16[768,512]{1...) custom-call(s32[2]{0:T(128)} %pad_add_fusion.place_ref, ...), custom_call_target="tpu_custom_call" | custom-call | flops 2315255808 | bytes 8552448 | tf_op jit(solution)/shard_map/pallas_call | solution.py:224
  225.9 13.4 %collective-permute-done.22.refs_0_ = bf16[256,1152]{1,0:T(8,128)(2,1)S(1)} collective-permute-done((bf16[256,1152]{1,0:T(8,128)(2,1)}, bf16[256,1152]{1,0:T(8,128)(2,1)S(1)}, u32[]{:S(2)}, u32[]{:S(2)}) %collective-permute-start.22) | collective-permute-done | bytes 589856 | tf_op jit(solution)/shard_map/ppermute | solution.py:47
  239.3 8.6 %collective-permute-done.23.refs_1_ = bf16[256,1152]{1,0:T(8,128)(2,1)} collective-permute-done((bf16[256,1152]{1,0:T(8,128)(2,1)}, bf16[256,1152]{1,0:T(8,128)(2,1)}, u32[]{:S(2)}, u32[]{:S(2)}) %collective-permute-start.23) | collective-permute-done | bytes 589856 | tf_op jit(solution)/shard_map/ppermute | solution.py:32
  249.9 18.1 %shard_map.285 = (bf16[1024,1728]{1,0:T(8,128)(2,1)}, bf16[1024,1728]{1,0:T(8,128)(2,1)}, bf16[1024,1728]{1,0:T(8,128)(2,1)}) custom-call(s32[2]{0:T(128)} %pad_add_fusion.place_ref, bf16[256,1152]{1,0:T(8,128)(2,1)} %copy-done.57, bf16[256,1152]{1,0:T(8,128)(2,1)} %collective-permute-done.23.refs_1_, bf16[256,1152]{1,0:T(8,128)(2,1)} %collective-permute-done.24.refs_2_, ...), custom_call_target="tpu_custom_call" | custom-call | flops 8153726976 | bytes 18579456 | tf_op jit(solution)/shard_map/pallas_call | solution.py:475
  294.0 12.2 %collective-permute-done.49.far_ref = bf16[256,1152]{1,0:T(8,128)(2,1)S(1)} collective-permute-done((bf16[256,1152]{1,0:T(8,128)(2,1)}, bf16[256,1152]{1,0:T(8,128)(2,1)S(1)}, u32[]{:S(2)}, u32[]{:S(2)}) %collective-permute-start.49) | collective-permute-done | bytes 589856 | tf_op jit(solution)/shard_map/ppermute | solution.py:47
  314.4 12.1 %collective-permute-done.54.refs_0_.refs_1_ = bf16[256,1152]{1,0:T(8,128)(2,1)S(1)} collective-permute-done((bf16[256,1152]{1,0:T(8,128)(2,1)}, bf16[256,1152]{1,0:T(8,128)(2,1)S(1)}, u32[]{:S(2)}, u32[]{:S(2)}) %collective-permute-start.54) | collective-permute-done | bytes 589856 | tf_op jit(solution)/shard_map/ppermute | solution.py:32
  329.4 17.1 %shard_map.292 = (bf16[256,1152]{1,0:T(8,128)(2,1)}, bf16[256,1152]{1,0:T(8,128)(2,1)}, bf16[512,1728]{1,0:T(8,128)(2,1)}, bf16[512,1728]{1,0:T(8,128)(2,1)}) custom-call(s32[2]{0:T(128)} %pad_add_fusion.place_ref, bf16[256,1152]{1,0:T(8,128)(2,1)} %copy-done.58, bf16[256,1152]{1,0:T(8,128)(2,1)} %copy-done.59, ...), custom_call_target="tpu_custom_call" | custom-call | flops 6115295232 | bytes 22560768 | tf_op jit(solution)/shard_map/pallas_call | solution.py:224
  348.5 10.1 %shard_map.291 = (bf16[256,1152]{1,0:T(8,128)(2,1)}, bf16[256,1728]{1,0:T(8,128)(2,1)}, bf16[256,1728]{1,0:T(8,128)(2,1)}) custom-call(s32[2]{0:T(128)} %pad_add_fusion.place_ref, bf16[256,1152]{1,0:T(8,128)(2,1)} %copy-done.39, bf16[1024,1728]{1,0:T(8,128)(2,1)} %get-tuple-element.72.refs_1_.refs_2_, bf16[1024,1728]{1,0:T(8,128)(2,1)} %get-tuple-element.73.refs_2_.refs_3_, ...), custom_call_target="tpu_custom_call" | custom-call | flops 3057647616 | bytes 17252352 | tf_op jit(solution)/shard_map/pallas_call | solution.py:224
  361.0 11.5 %shard_map.290 = (bf16[256,1152]{1,0:T(8,128)(2,1)}, bf16[256,1728]{1,0:T(8,128)(2,1)}, bf16[256,1728]{1,0:T(8,128)(2,1)}) custom-call(s32[2]{0:T(128)} %pad_add_fusion.place_ref, bf16[256,1152]{1,0:T(8,128)(2,1)} %get-tuple-element.71.refs_0_.refs_3_, bf16[1024,1728]{1,0:T(8,128)(2,1)} %get-tuple-element.72.refs_1_.refs_2_, ...), custom_call_target="tpu_custom_call" | custom-call | flops 3057647616 | bytes 17252352 | tf_op jit(solution)/shard_map/pallas_call | solution.py:224
  373.8 16.1 %shard_map.293 = (bf16[4,144,2048]{2,1,0:T(8,128)(2,1)}, bf16[4,144,2048]{2,1,0:T(8,128)(2,1)}, f32[256,1152]{1,0:T(8,128)}, f32[256,1152]{1,0:T(8,128)}, bf16[2...) custom-call(s32[2]{0:T(128)} %pad_add_fusion.place_ref, ...), custom_call_target="tpu_custom_call" | custom-call | flops 4429185024 | bytes 23003136 | tf_op jit(solution)/shard_map/pallas_call | solution.py:224
  393.5 9.3 %collective-permute-done.59.far_ref = bf16[256,512]{1,0:T(8,128)(2,1)S(1)} collective-permute-done((bf16[256,512]{1,0:T(8,128)(2,1)}, bf16[256,512]{1,0:T(8,128)(2,1)S(1)}, u32[]{:S(2)}, u32[]{:S(2)}) %collective-permute-start.59) | collective-permute-done | bytes 262176 | tf_op jit(solution)/shard_map/ppermute | solution.py:23
  411.6 10.2 %shard_map.297 = (bf16[4,144,1728]{2,1,0:T(8,128)(2,1)}, bf16[4,144,1728]{2,1,0:T(8,128)(2,1)}) custom-call(s32[2]{0:T(128)} %pad_add_fusion.place_ref, bf16[256,1152]{1,0:T(8,128)(2,1)} %copy-done.39, bf16[256,1152]{1,0:T(8,128)(2,1)} %copy-done.58, bf16[256,1152]{1,0:T(8,128)(2,1)} %copy-done.59, bf16[256,1152]{1,0:T(8,128)(2,1)} %get-tuple-element.71.refs_0_.refs_3_, ...), custom_call_target="tpu_custom_call" | custom-call | flops 4076863488 | bytes 9879552 | tf_op jit(solution)/shard_map/pallas_call | solution.py:224
  426.1 10.0 %shard_map.296 = (bf16[4,144,1728]{2,1,0:T(8,128)(2,1)}, bf16[4,144,1728]{2,1,0:T(8,128)(2,1)}) custom-call(s32[2]{0:T(128)} %pad_add_fusion.place_ref, bf16[256,1152]{1,0:T(8,128)(2,1)} %copy-done.57, bf16[256,1152]{1,0:T(8,128)(2,1)} %collective-permute-done.23.refs_1_, bf16[256,1152]{1,0:T(8,128)(2,1)} %collective-permute-done.24.refs_2_, ...), custom_call_target="tpu_custom_call" | custom-call | flops 4076863488 | bytes 9879552 | tf_op jit(solution)/shard_map/pallas_call | solution.py:224
  437.1 10.0 %shard_map.295 = (bf16[4,144,1728]{2,1,0:T(8,128)(2,1)}, bf16[4,144,1728]{2,1,0:T(8,128)(2,1)}) custom-call(s32[2]{0:T(128)} %pad_add_fusion.place_ref, bf16[256,1152]{1,0:T(8,128)(2,1)} %copy-done.57, bf16[256,1152]{1,0:T(8,128)(2,1)} %collective-permute-done.23.refs_1_, bf16[256,1152]{1,0:T(8,128)(2,1)} %collective-permute-done.24.refs_2_, ...), custom_call_target="tpu_custom_call" | custom-call | flops 4076863488 | bytes 9879552 | tf_op jit(solution)/shard_map/pallas_call | solution.py:224
  470.4 13.3 %collective-permute-done.83 = bf16[2,144,1728]{2,1,0:T(8,128)(2,1)S(1)} collective-permute-done((bf16[2,144,1728]{2,1,0:T(8,128)(2,1)S(1)}, bf16[2,144,1728]{2,1,0:T(8,128)(2,1)S(1)}, u32[]{:S(2)}, u32[]{:S(2)}) %collective-permute-start.83) | collective-permute-done | bytes 995360 | tf_op jit(solution)/shard_map/ppermute | solution.py:32
  485.0 33.5 %collective-permute-done.79 = bf16[2,144,1728]{2,1,0:T(8,128)(2,1)S(1)} collective-permute-done((bf16[2,144,1728]{2,1,0:T(8,128)(2,1)S(1)}, bf16[2,144,1728]{2,1,0:T(8,128)(2,1)S(1)}, u32[]{:S(2)}, u32[]{:S(2)}) %collective-permute-start.79) | collective-permute-done | bytes 995360 | tf_op jit(solution)/shard_map/ppermute | solution.py:32
  520.3 20.3 %collective-permute-done.75 = bf16[2,144,1728]{2,1,0:T(8,128)(2,1)S(1)} collective-permute-done((bf16[2,144,1728]{2,1,0:T(8,128)(2,1)S(1)}, bf16[2,144,1728]{2,1,0:T(8,128)(2,1)S(1)}, u32[]{:S(2)}, u32[]{:S(2)}) %collective-permute-start.75) | collective-permute-done | bytes 995360 | tf_op jit(solution)/shard_map/ppermute | solution.py:32
  544.9 10.4 %collective-permute-done.80 = bf16[144,1728]{1,0:T(8,128)(2,1)S(1)} collective-permute-done((bf16[144,1728]{1,0:T(8,128)(2,1)S(1)}, bf16[144,1728]{1,0:T(8,128)(2,1)S(1)}, u32[]{:S(2)}, u32[]{:S(2)}) %collective-permute-start.80) | collective-permute-done | bytes 497696 | tf_op jit(solution)/shard_map/ppermute | solution.py:32
  569.8 15.7 %collective-permute-done.64 = bf16[36,2048]{1,0:T(8,128)(2,1)S(1)} collective-permute-done((bf16[36,2048]{1,0:T(8,128)(2,1)S(1)}, bf16[36,2048]{1,0:T(8,128)(2,1)S(1)}, u32[]{:S(2)}, u32[]{:S(2)}) %collective-permute-start.64) | collective-permute-done | bytes 147488 | tf_op jit(solution)/shard_map/ppermute | solution.py:37
  585.5 24.6 %collective-permute-start.77 = (bf16[144,1728]{1,0:T(8,128)(2,1)S(1)}, bf16[144,1728]{1,0:T(8,128)(2,1)S(1)}, u32[]{:S(2)}, u32[]{:S(2)}) collective-permute-start(bf16[144,1728]{1,0:T(8,128)(2,1)S(1)} %broadcast_select_fusion.2), channel_id=1, source_target_pairs={{0,2},{1,3},{2,0},{3,1},{4,6},{5,7},{6,4},{7,5},{8,10},{9,11},{10,... | collective-permute-start | bytes 1493000 | tf_op jit(solution)/shard_map/ppermute | solution.py:32
  610.0 12.3 %collective-permute-done.65 = bf16[36,2048]{1,0:T(8,128)(2,1)S(1)} collective-permute-done((bf16[36,2048]{1,0:T(8,128)(2,1)S(1)}, bf16[36,2048]{1,0:T(8,128)(2,1)S(1)}, u32[]{:S(2)}, u32[]{:S(2)}) %collective-permute-start.65) | collective-permute-done | bytes 147488 | tf_op jit(solution)/shard_map/ppermute | solution.py:37
  (327 shorter events, 193.2 us)
Async XLA Ops:
  15.5 41.2 %collective-permute-start.16 = (bf16[144,1024]{1,0:T(8,128)(2,1)}, bf16[144,1024]{1,0:T(8,128)(2,1)S(1)}, u32[]{:S(2)}, u32[]{:S(2)}) collective-permute-start(bf16[144,1024]{1,0:T(8,128)(2,1)} %shard_map.283.refs_0_), channel_id=1, source_target_pairs={{0,8},{4,12},{8,0},{12,4},{16,24},{20,28},{24,16},{28,20},{1,9},{5... | collective-permute-start | bytes 884744 | tf_op jit(solution)/shard_map/ppermute | solution.py:32
  17.1 68.2 %collective-permute-start.25 = (bf16[144,1728]{1,0:T(8,128)(2,1)}, bf16[144,1728]{1,0:T(8,128)(2,1)}, u32[]{:S(2)}, u32[]{:S(2)}) collective-permute-start(bf16[144,1728]{1,0:T(8,128)(2,1)} %param.25), channel_id=1, source_target_pairs={{0,2},{1,3},{2,0},{3,1},{4,6},{5,7},{6,4},{7,5},{8,10},{9,11},{10,... | collective-permute-start | bytes 1493000 | tf_op jit(solution)/shard_map/ppermute | solution.py:32
  23.0 29.2 %collective-permute-start.3 = (bf16[36,1664]{1,0:T(8,128)(2,1)}, bf16[36,1664]{1,0:T(8,128)(2,1)S(1)}, u32[]{:S(2)}, u32[]{:S(2)}) collective-permute-start(bf16[36,1664]{1,0:T(8,128)(2,1)} %shard_map.280.refs_0_), channel_id=1, source_target_pairs={{0,2},{1,3},{2,0},{3,1},{4,6},{5,7},{6,4},{7,5},{8,10},{9,11},{10,... | collective-permute-start | bytes 359432 | tf_op jit(solution)/shard_map/ppermute | solution.py:37
  23.4 31.1 %collective-permute-start.4 = (bf16[36,1664]{1,0:T(8,128)(2,1)}, bf16[36,1664]{1,0:T(8,128)(2,1)S(1)}, u32[]{:S(2)}, u32[]{:S(2)}) collective-permute-start(bf16[36,1664]{1,0:T(8,128)(2,1)} %shard_map.280.refs_0_), channel_id=1, source_target_pairs={{0,3},{1,0},{2,1},{3,2},{4,7},{5,4},{6,5},{7,6},{8,11},{9,8},{10,9... | collective-permute-start | bytes 359432 | tf_op jit(solution)/shard_map/ppermute | solution.py:37
  36.7 27.3 %collective-permute-start.18 = (bf16[144,1024]{1,0:T(8,128)(2,1)}, bf16[144,1024]{1,0:T(8,128)(2,1)S(1)}, u32[]{:S(2)}, u32[]{:S(2)}) collective-permute-start(bf16[144,1024]{1,0:T(8,128)(2,1)} %shard_map.283.refs_0_), channel_id=1, source_target_pairs={{0,16},{4,20},{8,24},{12,28},{16,0},{20,4},{24,8},{28,12},{1,17},{... | collective-permute-start | bytes 884744 | tf_op jit(solution)/shard_map/ppermute | solution.py:32
  52.2 33.1 %collective-permute-start.20 = (bf16[144,1024]{1,0:T(8,128)(2,1)}, bf16[144,1024]{1,0:T(8,128)(2,1)}, u32[]{:S(2)}, u32[]{:S(2)}) collective-permute-start(bf16[144,1024]{1,0:T(8,128)(2,1)} %shard_map.283.refs_0_), channel_id=1, source_target_pairs={{0,24},{4,28},{8,16},{12,20},{16,8},{20,12},{24,0},{28,4},{1,25},{... | collective-permute-start | bytes 884744 | tf_op jit(solution)/shard_map/ppermute | solution.py:32
  54.5 77.5 %collective-permute-start = (bf16[256,1152]{1,0:T(8,128)(2,1)}, bf16[256,1152]{1,0:T(8,128)(2,1)}, u32[]{:S(2)}, u32[]{:S(2)}) collective-permute-start(bf16[256,1152]{1,0:T(8,128)(2,1)} %bitcast.87), channel_id=1, source_target_pairs={{0,4},{4,8},{8,12},{12,16},{16,20},{20,24},{24,28},{1,5},{5,9},{9,... | collective-permute-start | bytes 1769480 | tf_op jit(solution)/shard_map/ppermute | solution.py:23
  56.6 75.4 %collective-permute-start.1 = (bf16[256,1152]{1,0:T(8,128)(2,1)}, bf16[256,1152]{1,0:T(8,128)(2,1)}, u32[]{:S(2)}, u32[]{:S(2)}) collective-permute-start(bf16[256,1152]{1,0:T(8,128)(2,1)} %bitcast.88), channel_id=1, source_target_pairs={{0,8},{4,12},{8,16},{12,20},{16,24},{20,28},{1,9},{5,13},{9,17},{1... | collective-permute-start | bytes 1769480 | tf_op jit(solution)/shard_map/ppermute | solution.py:23
  64.0 55.0 %collective-permute-start.33 = (bf16[144,1728]{1,0:T(8,128)(2,1)}, bf16[144,1728]{1,0:T(8,128)(2,1)S(1)}, u32[]{:S(2)}, u32[]{:S(2)}) collective-permute-start(bf16[144,1728]{1,0:T(8,128)(2,1)} %param.26), channel_id=1, source_target_pairs={{0,2},{1,3},{2,0},{3,1},{4,6},{5,7},{6,4},{7,5},{8,10},{9,11},{10,... | collective-permute-start | bytes 1493000 | tf_op jit(solution)/shard_map/ppermute | solution.py:32
  85.2 44.4 %collective-permute-start.41 = (bf16[144,1728]{1,0:T(8,128)(2,1)}, bf16[144,1728]{1,0:T(8,128)(2,1)S(1)}, u32[]{:S(2)}, u32[]{:S(2)}) collective-permute-start(bf16[144,1728]{1,0:T(8,128)(2,1)} %param.27), channel_id=1, source_target_pairs={{0,2},{1,3},{2,0},{3,1},{4,6},{5,7},{6,4},{7,5},{8,10},{9,11},{10,... | collective-permute-start | bytes 1493000 | tf_op jit(solution)/shard_map/ppermute | solution.py:32
  87.1 45.5 %collective-permute-start.10 = (bf16[144,1664]{1,0:T(8,128)(2,1)S(1)}, bf16[144,1664]{1,0:T(8,128)(2,1)}, u32[]{:S(2)}, u32[]{:S(2)}) collective-permute-start(bf16[144,1664]{1,0:T(8,128)(2,1)S(1)} %copy-done.10), channel_id=1, source_target_pairs={{0,24},{4,28},{8,16},{12,20},{16,8},{20,12},{24,0},{28,4},{1,25},{... | collective-permute-start | bytes 1437704 | tf_op jit(solution)/shard_map/ppermute | solution.py:32
  184.5 37.3 %collective-permute-start.28 = (bf16[144,1728]{1,0:T(8,128)(2,1)S(1)}, bf16[144,1728]{1,0:T(8,128)(2,1)S(1)}, u32[]{:S(2)}, u32[]{:S(2)}) collective-permute-start(bf16[144,1728]{1,0:T(8,128)(2,1)S(1)} %collective-permute-done.27.refs_6_.refs_13_.refs_14_), channel_id=1, source_target_pairs={{0,4},{4,0},{8,12},{12,8},{16,20},{20,16},{24,28},{28,24},{1,5},{5... | collective-permute-start | bytes 1493000 | tf_op jit(solution)/shard_map/ppermute | solution.py:32
  184.6 38.1 %collective-permute-start.36 = (bf16[144,1728]{1,0:T(8,128)(2,1)S(1)}, bf16[144,1728]{1,0:T(8,128)(2,1)S(1)}, u32[]{:S(2)}, u32[]{:S(2)}) collective-permute-start(bf16[144,1728]{1,0:T(8,128)(2,1)S(1)} %collective-permute-done.35.refs_14_.refs_21_.refs_22_), channel_id=1, source_target_pairs={{0,4},{4,0},{8,12},{12,8},{16,20},{20,16},{24,28},{28,24},{1,5},{5... | collective-permute-start | bytes 1493000 | tf_op jit(solution)/shard_map/ppermute | solution.py:32
  185.1 36.8 %collective-permute-start.30 = (bf16[144,1728]{1,0:T(8,128)(2,1)}, bf16[144,1728]{1,0:T(8,128)(2,1)S(1)}, u32[]{:S(2)}, u32[]{:S(2)}) collective-permute-start(bf16[144,1728]{1,0:T(8,128)(2,1)} %copy-done.17), channel_id=1, source_target_pairs={{0,4},{4,0},{8,12},{12,8},{16,20},{20,16},{24,28},{28,24},{1,5},{5... | collective-permute-start | bytes 1493000 | tf_op jit(solution)/shard_map/ppermute | solution.py:32
  193.3 32.0 %collective-permute-start.38 = (bf16[144,1728]{1,0:T(8,128)(2,1)}, bf16[144,1728]{1,0:T(8,128)(2,1)S(1)}, u32[]{:S(2)}, u32[]{:S(2)}) collective-permute-start(bf16[144,1728]{1,0:T(8,128)(2,1)} %copy-done.19), channel_id=1, source_target_pairs={{0,4},{4,0},{8,12},{12,8},{16,20},{20,16},{24,28},{28,24},{1,5},{5... | collective-permute-start | bytes 1493000 | tf_op jit(solution)/shard_map/ppermute | solution.py:32
  221.9 25.9 %collective-permute-start.23 = (bf16[256,1152]{1,0:T(8,128)(2,1)}, bf16[256,1152]{1,0:T(8,128)(2,1)}, u32[]{:S(2)}, u32[]{:S(2)}) collective-permute-start(bf16[256,1152]{1,0:T(8,128)(2,1)} %get-tuple-element.65.refs_3_), channel_id=1, source_target_pairs={{0,8},{4,12},{8,0},{12,4},{16,24},{20,28},{24,16},{28,20},{1,9},{5... | collective-permute-start | bytes 1769480 | tf_op jit(solution)/shard_map/ppermute | solution.py:32
  222.7 25.3 %collective-permute-start.24 = (bf16[256,1152]{1,0:T(8,128)(2,1)}, bf16[256,1152]{1,0:T(8,128)(2,1)}, u32[]{:S(2)}, u32[]{:S(2)}) collective-permute-start(bf16[256,1152]{1,0:T(8,128)(2,1)} %get-tuple-element.65.refs_3_), channel_id=1, source_target_pairs={{0,1},{1,0},{2,3},{3,2},{4,5},{5,4},{6,7},{7,6},{8,9},{9,8},{10,11... | collective-permute-start | bytes 1769480 | tf_op jit(solution)/shard_map/ppermute | solution.py:32
  239.3 28.8 %collective-permute-start.42 = (bf16[144,1728]{1,0:T(8,128)(2,1)S(1)}, bf16[144,1728]{1,0:T(8,128)(2,1)S(1)}, u32[]{:S(2)}, u32[]{:S(2)}) collective-permute-start(bf16[144,1728]{1,0:T(8,128)(2,1)S(1)} %get-tuple-element.128.refs_0_.refs_3_.refs_4_), channel_id=1, source_target_pairs={{0,4},{4,0},{8,12},{12,8},{16,20},{20,16},{24,28},{28,24},{1,5},{5... | collective-permute-start | bytes 1493000 | tf_op jit(solution)/shard_map/ppermute | solution.py:32
  312.4 35.3 %collective-permute-start.52 = (bf16[256,1152]{1,0:T(8,128)(2,1)}, bf16[256,1152]{1,0:T(8,128)(2,1)S(1)}, u32[]{:S(2)}, u32[]{:S(2)}) collective-permute-start(bf16[256,1152]{1,0:T(8,128)(2,1)} %get-tuple-element.71.refs_0_.refs_3_), channel_id=1, source_target_pairs={{0,9},{1,8},{2,11},{3,10},{4,13},{5,12},{6,15},{7,14},{8,1},{9,0},... | collective-permute-start | bytes 1769480 | tf_op jit(solution)/shard_map/ppermute | solution.py:47
  346.5 26.1 %collective-permute-start.56 = (bf16[256,1152]{1,0:T(8,128)(2,1)}, bf16[256,1152]{1,0:T(8,128)(2,1)S(1)}, u32[]{:S(2)}, u32[]{:S(2)}) collective-permute-start(bf16[256,1152]{1,0:T(8,128)(2,1)} %get-tuple-element.76), channel_id=1, source_target_pairs={{0,8},{4,12},{8,0},{12,4},{16,24},{20,28},{24,16},{28,20},{1,9},{5... | collective-permute-start | bytes 1769480 | tf_op jit(solution)/shard_map/ppermute | solution.py:32
  421.8 34.0 %collective-permute-start.82 = (bf16[4,144,1728]{2,1,0:T(8,128)(2,1)}, bf16[4,144,1728]{2,1,0:T(8,128)(2,1)}, u32[]{:S(2)}, u32[]{:S(2)}) collective-permute-start(bf16[4,144,1728]{2,1,0:T(8,128)(2,1)} %get-tuple-element.110), channel_id=1, source_target_pairs={{0,4},{4,0},{8,12},{12,8},{16,20},{20,16},{24,28},{28,24},{1,5},{5... | collective-permute-start | bytes 5971976 | tf_op jit(solution)/shard_map/ppermute | solution.py:32
  458.0 25.7 %collective-permute-start.83 = (bf16[2,144,1728]{2,1,0:T(8,128)(2,1)S(1)}, bf16[2,144,1728]{2,1,0:T(8,128)(2,1)S(1)}, u32[]{:S(2)}, u32[]{:S(2)}) collective-permute-start(bf16[2,144,1728]{2,1,0:T(8,128)(2,1)S(1)} %slice.159), channel_id=1, source_target_pairs={{0,16},{4,20},{8,24},{12,28},{16,0},{20,4},{24,8},{28,12},{1,17},{... | collective-permute-start | bytes 2985992 | tf_op jit(solution)/shard_map/ppermute | solution.py:32
  461.7 56.8 %collective-permute-start.79 = (bf16[2,144,1728]{2,1,0:T(8,128)(2,1)S(1)}, bf16[2,144,1728]{2,1,0:T(8,128)(2,1)S(1)}, u32[]{:S(2)}, u32[]{:S(2)}) collective-permute-start(bf16[2,144,1728]{2,1,0:T(8,128)(2,1)S(1)} %slice.155), channel_id=1, source_target_pairs={{0,16},{4,20},{8,24},{12,28},{16,0},{20,4},{24,8},{28,12},{1,17},{... | collective-permute-start | bytes 2985992 | tf_op jit(solution)/shard_map/ppermute | solution.py:32
  465.4 75.2 %collective-permute-start.75 = (bf16[2,144,1728]{2,1,0:T(8,128)(2,1)S(1)}, bf16[2,144,1728]{2,1,0:T(8,128)(2,1)S(1)}, u32[]{:S(2)}, u32[]{:S(2)}) collective-permute-start(bf16[2,144,1728]{2,1,0:T(8,128)(2,1)S(1)} %slice.151), channel_id=1, source_target_pairs={{0,16},{4,20},{8,24},{12,28},{16,0},{20,4},{24,8},{28,12},{1,17},{... | collective-permute-start | bytes 2985992 | tf_op jit(solution)/shard_map/ppermute | solution.py:32
  468.0 89.2 %collective-permute-start.61 = (bf16[144,2048]{1,0:T(8,128)(2,1)S(1)}, bf16[144,2048]{1,0:T(8,128)(2,1)S(1)}, u32[]{:S(2)}, u32[]{:S(2)}) collective-permute-start(bf16[144,2048]{1,0:T(8,128)(2,1)S(1)} %get-tuple-element.121), channel_id=1, source_target_pairs={{0,8},{4,12},{8,0},{12,4},{16,24},{20,28},{24,16},{28,20},{1,9},{5... | collective-permute-start | bytes 1769480 | tf_op jit(solution)/shard_map/ppermute | solution.py:32
  469.0 90.1 %collective-permute-start.62 = (bf16[144,2048]{1,0:T(8,128)(2,1)S(1)}, bf16[144,2048]{1,0:T(8,128)(2,1)S(1)}, u32[]{:S(2)}, u32[]{:S(2)}) collective-permute-start(bf16[144,2048]{1,0:T(8,128)(2,1)S(1)} %get-tuple-element.123), channel_id=1, source_target_pairs={{0,16},{4,20},{8,24},{12,28},{16,0},{20,4},{24,8},{28,12},{1,17},{... | collective-permute-start | bytes 1769480 | tf_op jit(solution)/shard_map/ppermute | solution.py:32
  483.7 75.4 %collective-permute-start.63 = (bf16[144,2048]{1,0:T(8,128)(2,1)S(1)}, bf16[144,2048]{1,0:T(8,128)(2,1)S(1)}, u32[]{:S(2)}, u32[]{:S(2)}) collective-permute-start(bf16[144,2048]{1,0:T(8,128)(2,1)S(1)} %get-tuple-element.122), channel_id=1, source_target_pairs={{0,24},{4,28},{8,16},{12,20},{16,8},{20,12},{24,0},{28,4},{1,25},{... | collective-permute-start | bytes 1769480 | tf_op jit(solution)/shard_map/ppermute | solution.py:32
  555.3 68.8 %collective-permute-start.85 = (bf16[144,1728]{1,0:T(8,128)(2,1)}, bf16[144,1728]{1,0:T(8,128)(2,1)}, u32[]{:S(2)}, u32[]{:S(2)}) collective-permute-start(bf16[144,1728]{1,0:T(8,128)(2,1)} %broadcast_select_fusion), channel_id=1, source_target_pairs={{0,2},{1,3},{2,0},{3,1},{4,6},{5,7},{6,4},{7,5},{8,10},{9,11},{10,... | collective-permute-start | bytes 1493000 | tf_op jit(solution)/shard_map/ppermute | solution.py:32
  557.2 69.0 %collective-permute-start.81 = (bf16[144,1728]{1,0:T(8,128)(2,1)}, bf16[144,1728]{1,0:T(8,128)(2,1)}, u32[]{:S(2)}, u32[]{:S(2)}) collective-permute-start(bf16[144,1728]{1,0:T(8,128)(2,1)} %broadcast_select_fusion.1), channel_id=1, source_target_pairs={{0,2},{1,3},{2,0},{3,1},{4,6},{5,7},{6,4},{7,5},{8,10},{9,11},{10,... | collective-permute-start | bytes 1493000 | tf_op jit(solution)/shard_map/ppermute | solution.py:32
  566.2 56.1 %collective-permute-start.65 = (bf16[36,2048]{1,0:T(8,128)(2,1)S(1)}, bf16[36,2048]{1,0:T(8,128)(2,1)S(1)}, u32[]{:S(2)}, u32[]{:S(2)}) collective-permute-start(bf16[36,2048]{1,0:T(8,128)(2,1)S(1)} %get-tuple-element.126), channel_id=1, source_target_pairs={{0,2},{1,3},{2,0},{3,1},{4,6},{5,7},{6,4},{7,5},{8,10},{9,11},{10,... | collective-permute-start | bytes 442376 | tf_op jit(solution)/shard_map/ppermute | solution.py:37
  568.1 54.2 %collective-permute-start.66 = (bf16[36,2048]{1,0:T(8,128)(2,1)S(1)}, bf16[36,2048]{1,0:T(8,128)(2,1)S(1)}, u32[]{:S(2)}, u32[]{:S(2)}) collective-permute-start(bf16[36,2048]{1,0:T(8,128)(2,1)S(1)} %get-tuple-element.125), channel_id=1, source_target_pairs={{0,3},{1,0},{2,1},{3,2},{4,7},{5,4},{6,5},{7,6},{8,11},{9,8},{10,9... | collective-permute-start | bytes 442376 | tf_op jit(solution)/shard_map/ppermute | solution.py:37
  585.5 49.8 %collective-permute-start.77 = (bf16[144,1728]{1,0:T(8,128)(2,1)S(1)}, bf16[144,1728]{1,0:T(8,128)(2,1)S(1)}, u32[]{:S(2)}, u32[]{:S(2)}) collective-permute-start(bf16[144,1728]{1,0:T(8,128)(2,1)S(1)} %broadcast_select_fusion.2), channel_id=1, source_target_pairs={{0,2},{1,3},{2,0},{3,1},{4,6},{5,7},{6,4},{7,5},{8,10},{9,11},{10,... | collective-permute-start | bytes 1493000 | tf_op jit(solution)/shard_map/ppermute | solution.py:32
  (114 other events, 2390.6 us)

commit v3 on v2

--- a/solution.py
+++ b/solution.py
@@ -64,24 +64,33 @@
     return [whole.reshape(-1, whole.shape[-1])]
 
 
-def gather_attn(block):
+def after(value, *earlier):
+    return lax.optimization_barrier((value,) + earlier)[0]
+
+
+def gather_far(block):
     parts = {0: block}
-    for rel in range(2, lax.axis_size("seq"), 2):
-        parts[rel] = swap(block, "seq", rel)
-    for rel in list(parts):
-        parts[rel ^ 1] = swap(parts[rel], "seq", 1)
+    for mask in [mask for mask in seq_masks() if mask > 2] + [2]:
+        parts.update({rel ^ mask: swap(part, "seq", mask) for rel, part in parts.items()})
+    return parts
+
+
+def gather_core(parts):
+    parts = dict(parts)
+    parts.update({rel ^ 1: swap(part, "seq", 1) for rel, part in parts.items()})
     return ordered(parts)
 
 
-def gather_ffn(block):
-    other_plane = swap(block, "fsdp", 2)
+def pick_slices(block, other_plane):
     own = on_own_slice()
-    mine = jnp.where(own, block, other_plane)
-    theirs = jnp.where(own, other_plane, block)
-    parts = {0: mine, 2: swap(theirs, "seq", 2)}
-    for mask in [mask for mask in seq_masks() if mask > 2] + [1]:
+    return jnp.where(own, block, other_plane), jnp.where(own, other_plane, block)
+
+
+def spread_far(parts):
+    parts = dict(parts)
+    for mask in [mask for mask in seq_masks() if mask > 2]:
         parts.update({rel ^ mask: swap(part, "seq", mask) for rel, part in parts.items()})
-    return ordered(parts)
+    return parts
 
 
 def add_rounded(first, second):
@@ -96,32 +105,50 @@
     return blocks[0::2], blocks[1::2]
 
 
-def scatter_ffn(pair):
+def merge_cores(pair):
     keep, send = cut(pair, lax.axis_size("seq"))
-    part = add_rounded(keep, swap(send, "seq", 1))
+    return add_rounded(keep, swap(send, "seq", 1))
+
+
+def merge_column(part, which, *earlier):
+    part = part.reshape((-1, 2) + part.shape[1:])[:, which]
+    got = None
+    for mask in [mask for mask in seq_masks() if mask > 2][::-1]:
+        half = part.shape[0] // 2
+        leaving = part[half:]
+        if got is None and earlier:
+            leaving = after(leaving, *earlier)
+        got = swap(leaving, "seq", mask)
+        part = add_rounded(part[:half], got)
+    return part[0], got
+
+
+def merge_planes(near, crossed, *earlier):
+    own = on_own_slice()
+    stays = jnp.where(own, near, crossed)
+    leaves = jnp.where(own, crossed, near)
+    if earlier:
+        leaves = after(leaves, *earlier)
+    got = swap(leaves, "fsdp", 2)
+    return stays.astype(F32) + got.astype(F32), got
+
+
+def scatter_attn(pair):
+    part = merge_cores(pair)
+    half = part.shape[0] // 2
+    part = part.reshape((half, 2) + part.shape[1:])
+    part = add_rounded(part[:, 0], swap(part[:, 1], "seq", 2))
     for mask in [mask for mask in seq_masks() if mask > 2][::-1]:
         half = part.shape[0] // 2
         part = add_rounded(part[:half], swap(part[half:], "seq", mask))
-    crossed = swap(part[1], "seq", 2)
-    own = on_own_slice()
-    stays = jnp.where(own, part[0], crossed)
-    leaves = jnp.where(own, crossed, part[0])
-    return stays.astype(F32) + swap(leaves, "fsdp", 2).astype(F32)
-
-
-def scatter_attn(pair):
-    keep, send = cut(pair, lax.axis_size("seq"))
-    part = add_rounded(keep, swap(send, "seq", 1))
-    rows = part[0].astype(F32)
-    for index in range(1, part.shape[0]):
-        rows = rows + swap(part[index], "seq", 2 * index).astype(F32)
+    rows = part[0]
     planes = lax.axis_size("fsdp")
     blocks = rows.reshape((planes, -1) + rows.shape[1:])
     mine = lax.axis_index("fsdp")
-    total = lax.dynamic_index_in_dim(blocks, mine, 0, keepdims=False)
+    total = lax.dynamic_index_in_dim(blocks, mine, 0, keepdims=False).astype(F32)
     for steps in range(1, planes):
         send = lax.dynamic_index_in_dim(blocks, (mine + steps) % planes, 0, keepdims=False)
-        total = total + shift(send.astype(BF16), "fsdp", steps).astype(F32)
+        total = total + shift(send, "fsdp", steps).astype(F32)
     return total
 
 
@@ -172,11 +199,17 @@
     return [(start, min(step, width - start)) for start in range(0, width, step)]
 
 
-def start_placing(parts, dest, sems, base, seq):
+def parts_width(part, head_dim):
+    return (part.shape[1] - 2 * head_dim - LANES) // 2
+
+
+def start_placing(parts, dest, sems, base, seq, lane=0, lanes=None):
     rows = parts[0].shape[0]
     copies = []
     for rel, part in enumerate(parts):
         start = pl.multiple_of((seq ^ rel) * rows, 16) if len(parts) > 1 else 0
+        if lanes is not None:
+            part = part.at[:, pl.ds(lane, lanes)]
         copies.append(
             pltpu.make_async_copy(part, dest.at[pl.ds(start, rows), :], sems.at[base + rel])
         )
@@ -236,7 +269,7 @@
     return jax.ShapeDtypeStruct(dims, dtype)
 
 
-def pack_kernel(wq_ref, wk_ref, wv_ref, *refs):
+def pack_kernel(wq_ref, wk_ref, wv_ref, wo_ref, *refs):
     wide, narrow, out_ref = refs[:4], refs[4:6], refs[6]
     rows, heads_width, head_dim = wq_ref.shape[0], wq_ref.shape[1], wk_ref.shape[1]
     out_ref[:, :heads_width] = wq_ref[...]
@@ -252,13 +285,15 @@
         spread = dot(jnp.broadcast_to(ref[...].astype(F32), (16, small)).astype(BF16), fit)
         held = held + jnp.where(row == 4 + index, spread, 0.0)
     place = unit((16, LANES), iota((16, LANES), 0) == iota((16, LANES), 1))
-    out_ref[:, heads_width + 2 * head_dim :] = dot_tn(held.astype(BF16), place).astype(BF16)
-
-
-def pack_first(w_query, w_key, w_value, wide, narrow):
+    gain_start = heads_width + 2 * head_dim
+    out_ref[:, gain_start : gain_start + LANES] = dot_tn(held.astype(BF16), place).astype(BF16)
+    out_ref[:, gain_start + LANES :] = wo_ref[...]
+
+
+def pack_attn(w_query, w_key, w_value, w_out, wide, narrow):
     rows = w_query.shape[0]
-    width = w_query.shape[1] + 2 * w_key.shape[1] + LANES
-    ins = [w_query, w_key, w_value] + [vec.reshape(1, -1) for vec in wide + narrow]
+    width = 2 * w_query.shape[1] + 2 * w_key.shape[1] + LANES
+    ins = [w_query, w_key, w_value, w_out] + [vec.reshape(1, -1) for vec in wide + narrow]
     return call(
         pack_kernel,
         [shape_of((rows, width), BF16)],
@@ -320,8 +355,11 @@
         attended_ref,
         gains_ref,
         small_gains_ref,
-    ) = refs[part_count : part_count + 9]
-    weights, inside, sems = refs[part_count + 9 :]
+        attn_out_ref,
+        middle_ref,
+        ffn_in_ref,
+    ) = refs[part_count : part_count + 12]
+    weights, inside, sems = refs[part_count + 12 :]
     copies = start_placing(parts, weights, sems, 0, place_ref[0])
     rows, width = near_ref.shape
     head_dim = key_lin_ref.shape[1]
@@ -332,7 +370,8 @@
     for ref in blocks:
         scales.append(inverse_rms(ref[...].astype(F32)))
     wait_all(copies)
-    gain_cols = weights[:, heads_width + 2 * head_dim :]
+    gain_start = heads_width + 2 * head_dim
+    gain_cols = weights[:, gain_start : gain_start + LANES]
     pick = unit((8, LANES), iota((8, LANES), 0) == iota((8, LANES), 1))
     gains = dot_t(pick, gain_cols)
     spread = spread_matrix(head_dim, width, narrow_rows, wide_rows)
@@ -368,6 +407,14 @@
         probs = (raised / jnp.sum(raised, axis=-1, keepdims=True)).astype(BF16)
         probs_ref[head * rows : (head + 1) * rows, :] = probs
         attended_ref[:, lanes] = dot(probs, keys_ref[:, head_dim:]).astype(BF16)
+    for start, size in tiles_of(width, 384):
+        attn_out_ref[:, start : start + size] = dot_t(
+            attended_ref[...], weights[start : start + size, gain_start + LANES :]
+        )
+    attn_out = attn_out_ref[...]
+    middle = near_ref[...].astype(F32) + attn_out * inverse_rms(attn_out) * gains[1:2]
+    middle_ref[...] = middle
+    ffn_in_ref[...] = (middle * inverse_rms(middle) * gains[2:3]).astype(BF16)
 
 
 def attend(place, tokens3, cosine, sine, lowest, parts, head_count, head_dim, narrow_rows, wide_rows):
@@ -384,6 +431,9 @@
         shape_of((rows, heads_width), BF16),
         shape_of((8, width), F32),
         shape_of((8, head_dim), F32),
+        shape_of((rows, width), F32),
+        shape_of((rows, width), F32),
+        shape_of((rows, width), BF16),
     ]
     return call(
         functools.partial(attend_kernel, len(parts), narrow_rows, wide_rows, head_count),
@@ -402,33 +452,6 @@
     )
 
 
-def post_kernel(part_count, place_ref, tokens_ref, attended_ref, gains_ref, *refs):
-    parts = refs[:part_count]
-    attn_out_ref, middle_ref, ffn_in_ref, weights, sems = refs[part_count:]
-    copies = start_placing(parts, weights, sems, 0, place_ref[0])
-    wait_all(copies)
-    attn_out = dot_t(attended_ref[...], weights[...])
-    attn_out_ref[...] = attn_out
-    middle = tokens_ref[...].astype(F32) + attn_out * inverse_rms(attn_out) * gains_ref[1:2, :]
-    middle_ref[...] = middle
-    ffn_in_ref[...] = (middle * inverse_rms(middle) * gains_ref[2:3, :]).astype(BF16)
-
-
-def post_attention(place, tokens, attended, gains, parts):
-    rows, width = tokens.shape
-    inner = attended.shape[1]
-    return call(
-        functools.partial(post_kernel, len(parts)),
-        [shape_of((rows, width), F32), shape_of((rows, width), F32), shape_of((rows, width), BF16)],
-        [VMEM_SPEC] * 3,
-        [place, tokens, attended, gains] + parts,
-        [SMEM_SPEC] + [VMEM_SPEC] * 3 + [ANY_SPEC] * len(parts),
-        [pltpu.VMEM((width, inner), BF16), pltpu.SemaphoreType.DMA((len(parts),))],
-        flops=2 * rows * width * inner,
-        moved=2 * width * inner + 14 * rows * width,
-    )
-
-
 def gelu_pair(gate):
     square = gate * gate
     tanh = jnp.tanh(gate * (0.7978845608028654 + 0.035677408136300125 * square))
@@ -440,15 +463,14 @@
 
 def gate_up_kernel(part_count, place_ref, *refs):
     blocks, refs = refs[:4], refs[4:]
-    gate_parts, up_parts = refs[:part_count], refs[part_count : 2 * part_count]
-    act_ref, gate_slope_ref, up_slope_ref, held, gate_w, up_w, sems = refs[2 * part_count :]
+    parts = refs[:part_count]
+    act_ref, gate_slope_ref, up_slope_ref, held, weights, sems = refs[part_count:]
+    hidden, up_start = act_ref.shape[1], weights.shape[1] - act_ref.shape[1]
     step = pl.program_id(0)
 
     @pl.when(step == 0)
     def _():
-        copies = start_placing(gate_parts, gate_w, sems, 0, place_ref[0])
-        copies += start_placing(up_parts, up_w, sems, part_count, place_ref[0])
-        wait_all(copies)
+        wait_all(start_placing(parts, weights, sems, 0, place_ref[0]))
 
     for index, block in enumerate(blocks):
 
@@ -457,20 +479,19 @@
             held[...] = block[...]
 
     rows_in = held[...]
-    for start, size in tiles_of(gate_w.shape[1], 256):
+    for start, size in tiles_of(hidden, 256):
         lanes = slice(start, start + size)
-        gate = dot(rows_in, gate_w[:, lanes])
-        up = dot(rows_in, up_w[:, lanes])
+        gate = dot(rows_in, weights[:, lanes])
+        up = dot(rows_in, weights[:, up_start + start : up_start + start + size])
         value, slope = gelu_pair(gate)
         act_ref[:, lanes] = (value * up).astype(BF16)
         gate_slope_ref[:, lanes] = (slope * up).astype(BF16)
         up_slope_ref[:, lanes] = value.astype(BF16)
 
 
-def gate_up(place, blocks, gate_parts, up_parts):
+def gate_up(place, blocks, parts, hidden):
     rows, width = blocks[0].shape
-    hidden = gate_parts[0].shape[1]
-    count = len(gate_parts)
+    count = len(parts)
     out = shape_of((4 * rows, hidden), BF16)
     return pl.pallas_call(
         functools.partial(gate_up_kernel, count),
@@ -478,13 +499,12 @@
         grid=(4,),
         in_specs=[SMEM_SPEC]
         + [pl.BlockSpec((rows, width), lambda step: (0, 0))] * 4
-        + [ANY_SPEC] * (2 * count),
+        + [ANY_SPEC] * count,
         out_specs=(pl.BlockSpec((rows, hidden), lambda step: (step, 0)),) * 3,
         scratch_shapes=[
             pltpu.VMEM((rows, width), BF16),
-            pltpu.VMEM((width, hidden), BF16),
-            pltpu.VMEM((width, hidden), BF16),
-            pltpu.SemaphoreType.DMA((2 * count,)),
+            pltpu.VMEM((width, parts[0].shape[1]), BF16),
+            pltpu.SemaphoreType.DMA((count,)),
         ],
         compiler_params=pltpu.CompilerParams(vmem_limit_bytes=VMEM_LIMIT),
         cost_estimate=pl.CostEstimate(
@@ -492,44 +512,34 @@
             bytes_accessed=4 * width * hidden + 24 * rows * hidden,
             transcendentals=4 * rows * hidden,
         ),
-    )(place, *blocks, *gate_parts, *up_parts)
-
-
-def down_kernel(part_count, first, span, place_ref, act_ref, *refs):
+    )(place, *blocks, *parts)
+
+
+def down_kernel(part_count, place_ref, act_ref, *refs):
     parts = refs[:part_count]
-    outs = refs[part_count : part_count + span]
-    held, weights, sems, act_sem = refs[part_count + span :]
+    outs = refs[part_count : part_count + 4]
+    weights, sems = refs[part_count + 4 :]
     rows = outs[0].shape[0]
-    fetch = pltpu.make_async_copy(
-        act_ref.at[pl.ds(first * rows, span * rows), :], held, act_sem.at[0]
-    )
-    fetch.start()
     wait_all(start_placing(parts, weights, sems, 0, place_ref[0]))
-    fetch.wait()
-    for index, out in enumerate(outs):
-        for start, size in tiles_of(weights.shape[0], 384):
-            out[:, start : start + size] = dot_t(
-                held[index * rows : (index + 1) * rows, :], weights[start : start + size, :]
-            ).astype(BF16)
-
-
-def down(place, act, first, span, parts):
+    for start, size in tiles_of(weights.shape[0], 256):
+        lanes = slice(start, start + size)
+        total = dot_t(act_ref[...], weights[lanes, :]).astype(BF16)
+        for index, out in enumerate(outs):
+            out[:, lanes] = total[index * rows : (index + 1) * rows]
+
+
+def down(place, act, parts):
     rows, hidden = act.shape[0] // 4, act.shape[1]
     width = parts[0].shape[0] * len(parts)
     return call(
-        functools.partial(down_kernel, len(parts), first, span),
-        [shape_of((rows, width), BF16)] * span,
-        [VMEM_SPEC] * span,
+        functools.partial(down_kernel, len(parts)),
+        [shape_of((rows, width), BF16)] * 4,
+        [VMEM_SPEC] * 4,
         [place, act] + parts,
-        [SMEM_SPEC, ANY_SPEC] + [ANY_SPEC] * len(parts),
-        [
-            pltpu.VMEM((span * rows, hidden), BF16),
-            pltpu.VMEM((width, hidden), BF16),
-            pltpu.SemaphoreType.DMA((len(parts),)),
-            pltpu.SemaphoreType.DMA((1,)),
-        ],
-        flops=2 * span * rows * hidden * width,
-        moved=2 * width * hidden + 2 * span * rows * (width + hidden),
+        [SMEM_SPEC, VMEM_SPEC] + [ANY_SPEC] * len(parts),
+        [pltpu.VMEM((width, hidden), BF16), pltpu.SemaphoreType.DMA((len(parts),))],
+        flops=8 * rows * hidden * width,
+        moved=2 * width * hidden + 8 * rows * (width + hidden),
     )
 
 
@@ -564,13 +574,12 @@
     backs, refs = refs[:span], refs[span:]
     gate_slope_ref, up_slope_ref = refs[:2]
     refs = refs[2:]
-    down_parts, gate_parts, up_parts = [
-        refs[index * part_count : (index + 1) * part_count] for index in range(3)
-    ]
-    refs = refs[3 * part_count :]
+    down_parts, gate_up_parts = refs[:part_count], refs[part_count : 2 * part_count]
+    refs = refs[2 * part_count :]
     outs, refs = refs[:span], refs[span:]
-    d_gate_ref, d_up_ref, gate_slope, up_slope, down_w, gate_w, up_w, sems, slope_sems = refs
-    rows = outs[0].shape[0]
+    d_gate_ref, d_up_ref, held, gate_slope, up_slope, down_w, gate_up_w, sems, slope_sems = refs
+    rows, hidden = outs[0].shape[0], d_gate_ref.shape[1]
+    up_start = gate_up_w.shape[1] - hidden
     seq = place_ref[0]
     copies = start_placing(down_parts, down_w, sems, 0, seq)
     fetches = [
@@ -583,28 +592,26 @@
     ]
     for fetch in fetches:
         fetch.start()
-    later = start_placing(gate_parts, gate_w, sems, part_count, seq)
-    later += start_placing(up_parts, up_w, sems, 2 * part_count, seq)
+    later = start_placing(gate_up_parts, gate_up_w, sems, part_count, seq)
+    for index, back in enumerate(backs):
+        held[index * rows : (index + 1) * rows, :] = back[...]
     wait_all(copies)
     wait_all(fetches)
-    for index in range(span):
-        part = slice(index * rows, (index + 1) * rows)
-        for start, size in tiles_of(down_w.shape[1], 256):
-            lanes = slice(start, start + size)
-            d_act = dot(backs[index][...], down_w[:, lanes])
-            d_gate_ref[part, lanes] = (d_act * gate_slope[part, lanes].astype(F32)).astype(BF16)
-            d_up_ref[part, lanes] = (d_act * up_slope[part, lanes].astype(F32)).astype(BF16)
+    for start, size in tiles_of(hidden, 256):
+        lanes = slice(start, start + size)
+        d_act = dot(held[...], down_w[:, lanes])
+        d_gate_ref[:, lanes] = (d_act * gate_slope[:, lanes].astype(F32)).astype(BF16)
+        d_up_ref[:, lanes] = (d_act * up_slope[:, lanes].astype(F32)).astype(BF16)
     wait_all(later)
-    for index in range(span):
-        part = slice(index * rows, (index + 1) * rows)
-        for start, size in tiles_of(gate_w.shape[0], 384):
-            lanes = slice(start, start + size)
-            total = dot_t(d_gate_ref[part, :], gate_w[lanes, :])
-            total = total + dot_t(d_up_ref[part, :], up_w[lanes, :])
-            outs[index][:, lanes] = total.astype(BF16)
-
-
-def ffn_back(place, backs, first, gate_slope, up_slope, down_parts, gate_parts, up_parts):
+    for start, size in tiles_of(gate_up_w.shape[0], 256):
+        lanes = slice(start, start + size)
+        total = dot_t(d_gate_ref[...], gate_up_w[lanes, :hidden])
+        total = (total + dot_t(d_up_ref[...], gate_up_w[lanes, up_start:])).astype(BF16)
+        for index, out in enumerate(outs):
+            out[:, lanes] = total[index * rows : (index + 1) * rows]
+
+
+def ffn_back(place, backs, first, gate_slope, up_slope, down_parts, gate_up_parts):
     span = len(backs)
     rows, width = backs[0].shape
     hidden = gate_slope.shape[1]
@@ -614,15 +621,15 @@
         functools.partial(ffn_back_kernel, count, first, span),
         [shape_of((rows, width), BF16)] * span + [hidden_out] * 2,
         [VMEM_SPEC] * (span + 2),
-        [place] + list(backs) + [gate_slope, up_slope] + down_parts + gate_parts + up_parts,
-        [SMEM_SPEC] + [VMEM_SPEC] * span + [ANY_SPEC] * (2 + 3 * count),
+        [place] + list(backs) + [gate_slope, up_slope] + down_parts + gate_up_parts,
+        [SMEM_SPEC] + [VMEM_SPEC] * span + [ANY_SPEC] * (2 + 2 * count),
         [
+            pltpu.VMEM((span * rows, width), BF16),
             pltpu.VMEM((span * rows, hidden), BF16),
             pltpu.VMEM((span * rows, hidden), BF16),
             pltpu.VMEM((width, hidden), BF16),
-            pltpu.VMEM((width, hidden), BF16),
-            pltpu.VMEM((width, hidden), BF16),
-            pltpu.SemaphoreType.DMA((3 * count,)),
+            pltpu.VMEM((width, gate_up_parts[0].shape[1]), BF16),
+            pltpu.SemaphoreType.DMA((2 * count,)),
             pltpu.SemaphoreType.DMA((2,)),
         ],
         flops=6 * span * rows * hidden * width,
@@ -634,20 +641,34 @@
     lefts, rights = refs[:left_count], refs[left_count : left_count + right_count]
     refs = refs[left_count + right_count :]
     outs, (left, right, whole, sems) = refs[:-4], refs[-4:]
-    copies = []
-    for pieces, dest in ((lefts, left), (rights, right)):
-        start = 0
-        for piece in pieces:
-            size = piece.shape[0]
+    tiles = tiles_of(right.shape[1], 512)
+    first, start = [], 0
+    for piece in lefts:
+        size = piece.shape[0]
+        first.append(
+            pltpu.make_async_copy(piece, left.at[pl.ds(start, size), :], sems.at[len(first)])
+        )
+        start += size
+    waits = []
+    for number, (lane, size) in enumerate(tiles):
+        copies, start = [], 0
+        for piece in rights:
+            rows = piece.shape[0]
             copies.append(
-                pltpu.make_async_copy(piece, dest.at[pl.ds(start, size), :], sems.at[len(copies)])
+                pltpu.make_async_copy(
+                    piece.at[:, pl.ds(lane, size)],
+                    right.at[pl.ds(start, rows), pl.ds(lane, size)],
+                    sems.at[left_count + number * right_count + len(copies)],
+                )
             )
-            start += size
-    for copy in copies:
+            start += rows
+        waits.append(copies)
+    for copy in first + [copy for copies in waits for copy in copies]:
         copy.start()
-    wait_all(copies)
-    for start, size in tiles_of(right.shape[1], 256):
-        lanes = slice(start, start + size)
+    wait_all(first)
+    for copies, (lane, size) in zip(waits, tiles):
+        wait_all(copies)
+        lanes = slice(lane, lane + size)
         whole[:, lanes] = dot_tn(left[...], right[:, lanes]).astype(BF16)
     wait_all(start_cutting(whole, outs, sems, 0, place_ref[0]))
 
@@ -667,7 +688,7 @@
             pltpu.VMEM((rows, height), BF16),
             pltpu.VMEM((rows, width), BF16),
             pltpu.VMEM((height, width), BF16),
-            pltpu.SemaphoreType.DMA((max(count, len(lefts) + len(rights)),)),
+            pltpu.SemaphoreType.DMA((count + len(lefts) + 4 * len(rights),)),
         ],
         flops=2 * rows * height * width,
         moved=2 * (rows * (height + width) + height * width),
@@ -676,7 +697,6 @@
 
 def attend_back_kernel(
     part_count,
-    first_count,
     out_count,
     head_count,
     place_ref,
@@ -699,18 +719,17 @@
     sin_ref,
     *refs,
 ):
-    out_parts, refs = refs[:part_count], refs[part_count:]
-    first_parts, refs = refs[:first_count], refs[first_count:]
+    parts, refs = refs[:part_count], refs[part_count:]
     grads, refs = refs[:out_count], refs[out_count:]
     d_middle_ref, d_in_ref, far_halo_ref, back_halo_ref, near_ref, rows_ref, query_gain_ref = refs[:7]
-    out_w, first_w, whole, d_query, d_keys, sems = refs[7:]
+    weights, whole, d_query, d_keys, sems = refs[7:]
     rows, width = middle_ref.shape
     head_dim = keys_ref.shape[1] // 2
     heads_width = head_count * head_dim
     score_scale = head_dim**-0.5
     seq = place_ref[0]
-    copies = start_placing(out_parts, out_w, sems, 0, seq)
-    later = start_placing(first_parts, first_w, sems, part_count, seq)
+    copies = start_placing(parts, weights, sems, 0, seq)
+    out_start = weights.shape[1] - heads_width
     total = own_ref[...].astype(F32) + far_ref[...].astype(F32)
     total = total + across_ref[...].astype(F32) + along_ref[...].astype(F32)
     middle = middle_ref[...]
@@ -733,7 +752,8 @@
     query_gain = jnp.zeros((1, head_dim), F32)
     for head in range(head_count):
         lanes = slice(head * head_dim, (head + 1) * head_dim)
-        d_attended = dot(d_attn_low, out_w[:, lanes]).astype(BF16)
+        out_lanes = slice(out_start + head * head_dim, out_start + (head + 1) * head_dim)
+        d_attended = dot(d_attn_low, weights[:, out_lanes]).astype(BF16)
         probs_low = probs_ref[head * rows : (head + 1) * rows, :]
         probs = probs_low.astype(F32)
         d_probs = dot_t(d_attended, keys_ref[:, head_dim:])
@@ -763,15 +783,14 @@
         whole[:, heads_width + start : heads_width + start + size] = dot_tn(
             attn_in_ref[...], d_query[:, lanes]
         ).astype(BF16)
-    cuts = start_cutting(whole, grads, sems, part_count + first_count, seq)
-    wait_all(later)
+    cuts = start_cutting(whole, grads, sems, part_count, seq)
     for start, size in tiles_of(width, 384):
         lanes = slice(start, start + size)
-        d_in_ref[:, lanes] = dot_t(d_query[...], first_w[lanes, :heads_width])
+        d_in_ref[:, lanes] = dot_t(d_query[...], weights[lanes, :heads_width])
     wait_all(cuts)
 
 
-def attend_back(place, sums, saved, cosine, sine, out_parts, first_parts, head_count):
+def attend_back(place, sums, saved, cosine, sine, parts, head_count):
     middle, upstream, attn_out, gains, small_gains, attended, attn_in, query_lin, query, keys, probs = saved
     rows, width = middle.shape
     head_dim = keys.shape[1] // 2
@@ -787,22 +806,19 @@
         shape_of((8, width), F32),
         shape_of((1, head_dim), F32),
     ]
-    ins = [place] + list(sums) + list(saved) + [cosine, sine] + out_parts + first_parts
+    ins = [place] + list(sums) + list(saved) + [cosine, sine] + parts
     return call(
-        functools.partial(
-            attend_back_kernel, len(out_parts), len(first_parts), len(cuts), head_count
-        ),
+        functools.partial(attend_back_kernel, len(parts), len(cuts), head_count),
         outs,
         [ANY_SPEC] * len(cuts) + [VMEM_SPEC] * 7,
         ins,
-        [SMEM_SPEC] + [VMEM_SPEC] * 17 + [ANY_SPEC] * (len(out_parts) + len(first_parts)),
+        [SMEM_SPEC] + [VMEM_SPEC] * 17 + [ANY_SPEC] * len(parts),
         [
-            pltpu.VMEM((width, heads_width), BF16),
-            pltpu.VMEM((width, first_parts[0].shape[1]), BF16),
+            pltpu.VMEM((width, parts[0].shape[1]), BF16),
             pltpu.VMEM((width, 2 * heads_width), BF16),
             pltpu.VMEM((rows, heads_width), BF16),
             pltpu.VMEM((3 * rows, 2 * head_dim), F32),
-            pltpu.SemaphoreType.DMA((len(out_parts) + len(first_parts) + count,)),
+            pltpu.SemaphoreType.DMA((len(parts) + count,)),
         ],
         flops=8 * rows * width * heads_width + 30 * rows * rows * heads_width,
         moved=12 * width * heads_width + 30 * rows * width,
@@ -837,7 +853,8 @@
     rows, width = tokens_ref.shape
     head_dim = key_lin_ref.shape[1]
     seq = place_ref[0]
-    copies = start_placing(first_parts, first_w, sems, 0, seq)
+    heads_width = parts_width(first_parts[0], key_lin_ref.shape[1])
+    copies = start_placing(first_parts, first_w, sems, 0, seq, heads_width, 2 * key_lin_ref.shape[1])
     d_keys = near_ref[...] + back_ref[...].astype(F32) + far_ref[...].astype(F32)
     key_lin = key_lin_ref[...]
     scale = inverse_rms(key_lin)
@@ -847,10 +864,7 @@
     d_low[:, head_dim:] = d_keys[:, head_dim:].astype(BF16)
     whole[:, : 2 * head_dim] = dot_tn(attn_in_ref[...], d_low[...]).astype(BF16)
     wait_all(copies)
-    heads_width = first_w.shape[1] - 2 * head_dim - LANES
-    d_attn_in = d_in_ref[...] + dot_t(
-        d_low[...], first_w[:, heads_width : heads_width + 2 * head_dim]
-    )
+    d_attn_in = d_in_ref[...] + dot_t(d_low[...], first_w[...])
     inputs = tokens_ref[...].astype(F32)
     scale = inverse_rms(inputs)
     back, grad_an = norm_back(inputs * scale, scale, gains_ref[0:1, :], d_attn_in)
@@ -882,7 +896,7 @@
         [place] + list(ins) + first_parts,
         [SMEM_SPEC] + [VMEM_SPEC] * len(ins) + [ANY_SPEC] * len(parts),
         [
-            pltpu.VMEM((width, first_parts[0].shape[1]), BF16),
+            pltpu.VMEM((width, 2 * head_dim), BF16),
             pltpu.VMEM((width, pack), BF16),
             pltpu.VMEM((rows, 2 * head_dim), BF16),
             pltpu.SemaphoreType.DMA((len(parts) + count,)),
@@ -933,20 +947,24 @@
     inputs, upstream = tokens[0], cotangent[0]
     wide_rows, narrow_rows = attn_norm_gain.shape[0], query_gain.shape[0]
 
-    first_pack = pack_first(
+    pack = pack_attn(
         w_query,
         w_key,
         w_value,
+        w_out,
         [attn_norm_gain, attn_post_gain, ffn_norm_gain, ffn_post_gain],
         [query_gain, key_gain],
     )
-    first_parts = gather_attn(gather_planes(first_pack, place))
-    out_parts = gather_attn(gather_planes(w_out, place))
-    gate_parts = gather_ffn(w_gate)
-    up_parts = gather_ffn(w_up)
-    down_parts = gather_ffn(w_down)
-
-    tokens3 = [from_behind(inputs, 2), from_behind(inputs, 1), inputs]
+    behind = after(inputs, pack)
+    tokens3 = [inputs, from_behind(behind, 1), from_behind(behind, 2)]
+    hidden = w_gate.shape[1]
+    spare = jnp.zeros((w_gate.shape[0], -hidden % LANES), BF16)
+    gate_up_own = jnp.concatenate([w_gate, spare, w_up], axis=1)
+    pack_rows = gather_planes(pack, place)
+    pack_far = gather_far(pack_rows)
+    gate_up_other = swap(after(gate_up_own, pack_rows), "fsdp", 2)
+    parts = gather_core(pack_far)
+
     first_slot = seq_index * row_count
     position, padded = layout(
         doc_lengths[0], true_counts[0], first_slot - WINDOW, row_count + WINDOW
@@ -957,37 +975,64 @@
     reach = jnp.clip(position[WINDOW:] - padded[WINDOW:], 0, WINDOW - 1)
     lowest = (WINDOW + jnp.arange(row_count, dtype=jnp.int32) - reach)[:, None]
 
-    attn_in, query_lin, key_lin, query, keys, probs, attended, gains, small_gains = attend(
-        place,
-        [tokens3[2], tokens3[1], tokens3[0]],
+    gate_up_mine, gate_up_theirs = pick_slices(gate_up_own, gate_up_other)
+    attend_place = after(place, gate_up_mine, gate_up_theirs)
+    gate_up_near = spread_far({0: gate_up_mine})
+    gate_up_crossed = swap(gate_up_theirs, "seq", 2)
+    down_other = swap(after(w_down, gate_up_other), "fsdp", 2)
+    (
+        attn_in,
+        query_lin,
+        key_lin,
+        query,
+        keys,
+        probs,
+        attended,
+        gains,
+        small_gains,
+        attn_out,
+        middle,
+        ffn_in,
+    ) = attend(
+        attend_place,
+        tokens3,
         cosine,
         sine,
         lowest,
-        first_parts,
+        parts,
         head_count,
         head_dim,
         narrow_rows,
         wide_rows,
     )
-    attn_out, middle, ffn_in = post_attention(place, inputs, attended, gains, out_parts)
     blocks = group_blocks(ffn_in)
-    act, gate_slope, up_slope = gate_up(place, blocks, gate_parts, up_parts)
-    (far,) = down(place, act, 0, 1, down_parts)
-    far = diagonal(far)
-    across, along = down(place, act, 1, 2, down_parts)
-    across, along = swap(across, "seq", 2), swap(along, "fsdp", 1)
-    (own,) = down(place, act, 3, 1, down_parts)
+    gate_up_far = gate_up_near | spread_far({2: after(gate_up_crossed, ffn_in)})
+    gate_up_parts = gather_core({rel: after(part, ffn_in) for rel, part in gate_up_far.items()})
+    down_mine, down_theirs = pick_slices(w_down, after(down_other, ffn_in))
+    down_near = spread_far({0: down_mine})
+    down_crossed = swap(down_theirs, "seq", 2)
+    act, gate_slope, up_slope = gate_up(
+        after(place, down_crossed), blocks, gate_up_parts, hidden
+    )
+    down_far = down_near | spread_far({2: down_crossed})
+    down_parts = gather_core({rel: after(part, act) for rel, part in down_far.items()})
+    far, across, along, own = down(place, act, down_parts)
+    far, across, along = diagonal(far), swap(across, "seq", 2), swap(along, "fsdp", 1)
     output, d_ffn_low, grad_fp = turn([own, far, across, along], middle, upstream, gains)
+
     backs = group_blocks(d_ffn_low)
-    slopes = (gate_slope, up_slope, down_parts, gate_parts, up_parts)
-    far, far_gate, far_up = ffn_back(place, backs[:1], 0, *slopes)
-    far = diagonal(far)
-    across, along, side_gate, side_up = ffn_back(place, backs[1:3], 1, *slopes)
-    across, along = swap(across, "seq", 2), swap(along, "fsdp", 1)
+    slopes = (gate_slope, up_slope, down_parts, gate_up_parts)
     own, own_gate, own_up = ffn_back(place, backs[3:], 3, *slopes)
-    grad_down = scatter_ffn(weight_grad(place, backs, [act]))
-    grad_gate = scatter_ffn(weight_grad(place, blocks, [far_gate, side_gate, own_gate]))
-    grad_up = scatter_ffn(weight_grad(place, blocks, [far_up, side_up, own_up]))
+    far, across, along, side_gate, side_up = ffn_back(
+        after(place, own), backs[:3], 0, *slopes
+    )
+    far, across, along = diagonal(far), swap(across, "seq", 2), swap(along, "fsdp", 1)
+    down_pair = weight_grad(after(place, side_up), backs, [act])
+    gate_pair = weight_grad(after(place, down_pair[0]), blocks, [side_gate, own_gate])
+    down_merged = merge_cores(down_pair)
+    up_pair = weight_grad(after(place, gate_pair[0], down_merged), blocks, [side_up, own_up])
+    gate_merged = merge_cores(gate_pair)
+    down_cross, got = merge_column(down_merged, 1)
     saved = (
         middle,
         upstream,
@@ -1002,9 +1047,17 @@
         probs,
     )
     *head_grads, d_middle, d_in, far_halo, back_halo, near, gain_rows, query_gain_grad = attend_back(
-        place, [own, far, across, along], saved, cosine, sine, out_parts, first_parts, head_count
-    )
-    head_rows = scatter_attn(head_grads)
+        after(place, up_pair[0], gate_merged, down_cross),
+        [own, far, across, along],
+        saved,
+        cosine,
+        sine,
+        parts,
+        head_count,
+    )
+    down_near, got = merge_column(down_merged, 0, got)
+    up_merged = merge_cores(up_pair)
+    down_crossed = swap(down_cross, "seq", 2)
     ins = [
         near,
         from_behind(back_halo, -1),
@@ -1022,7 +1075,18 @@
         grad_fp,
         query_gain_grad,
     ]
-    *last_grads, input_grad = finish(place, ins, first_parts, narrow_rows, wide_rows)
+    *last_grads, input_grad = finish(
+        after(place, down_crossed, down_near, up_merged), ins, parts, narrow_rows, wide_rows
+    )
+    gate_cross, got = merge_column(gate_merged, 1, got)
+    gate_near, got = merge_column(gate_merged, 0, got)
+    up_cross, got = merge_column(up_merged, 1, got)
+    up_near, got = merge_column(up_merged, 0, got)
+    gate_crossed, up_crossed = swap(gate_cross, "seq", 2), swap(up_cross, "seq", 2)
+    grad_down, got = merge_planes(down_near, down_crossed)
+    grad_gate, got = merge_planes(gate_near, gate_crossed, got)
+    grad_up, got = merge_planes(up_near, up_crossed, got)
+    head_rows = scatter_attn(head_grads)
     last_rows = scatter_attn(last_grads)
     gain_cols = last_rows[:, 2 * head_dim :]
     return (

time: 642 us -> 509 us (0.79)
  the two profiles are of different devices: /device:TPU:0 before, /device:TPU:9 now
where the time goes in v3:
time: 509 us; the launch traced here: 499 us
  waiting for transfers between devices  227 us (45%)
  Pallas kernels  139 us (27%)
  starting transfers between devices  82.7 us (16%)
  other arithmetic  28.2 us (6%)
  local copies, waits for them, and re-layouts  20.6 us (4%)
    ppermute x52, waiting for transfers between devices, swap(): lax.ppermute(value, axis, [(source, source ^ mask) for source in range(co...  183 us
    pallas_call x12, Pallas kernels, call(): pl.pallas_call(kernel, out_shape=tuple(outs), in_specs=list(in_specs), ou...  121 us
    ppermute x52, starting transfers between devices, swap(): lax.ppermute(value, axis, [(source, source ^ mask) for source in range(co...  56.4 us
    ppermute x9, waiting for transfers between devices, shift(): lax.ppermute(value, axis, [(source, (source + steps) % count) for source...  29.8 us
    pallas_call x1, Pallas kernels, gate_up(): pl.pallas_call(functools.partial(gate_up_kernel, count), out_shape=(out,)...  18.2 us
    ppermute x4, waiting for transfers between devices, diagonal(): return lax.ppermute(value, ('seq', 'fsdp'), pairs)  14.3 us
    ppermute x4, starting transfers between devices, from_behind(): lax.ppermute(value, 'seq', [(source, source + steps) for source in range(...  12.9 us
    convert_element_type x9, other arithmetic, add_rounded(): return (first.astype(F32) + second.astype(F32)).astype(BF16)  11.4 us
  transfers between devices with their start and end apart: 69, of which 32 were waited for; matrix products, arithmetic and copies ran while one was open for 7% of the time, Pallas kernels for 18%

profile of v3, /device:TPU:9, one launch (start us, length us, event | category | flops | bytes accessed | tf_op | source)
XLA Modules:
  0.0 498.7 jit_solution(6198705256201896932)
XLA Ops:
  9.3 12.7 %collective-permute-done.1.refs_2_ = bf16[36,2688]{1,0:T(8,128)(2,1)S(1)} collective-permute-done((bf16[36,2688]{1,0:T(8,128)(2,1)}, bf16[36,2688]{1,0:T(8,128)(2,1)S(1)}, u32[]{:S(2)}, u32[]{:S(2)}) %collective-permute-start.1) | collective-permute-done | bytes 193568 | tf_op jit(solution)/shard_map/ppermute | solution.py:37
  29.6 4.8 collective-permute-start.5
  34.4 3.9 collective-permute-start.6
  39.3 32.4 %collective-permute-done.10.refs_4_ = bf16[144,2688]{1,0:T(8,128)(2,1)S(1)} collective-permute-done((bf16[144,2688]{1,0:T(8,128)(2,1)}, bf16[144,2688]{1,0:T(8,128)(2,1)S(1)}, u32[]{:S(2)}, u32[]{:S(2)}) %collective-permute-start.10) | collective-permute-done | bytes 774176 | tf_op jit(solution)/shard_map/ppermute | solution.py:32
  78.6 13.4 %collective-permute-done.12.refs_6_ = bf16[144,2688]{1,0:T(8,128)(2,1)} collective-permute-done((bf16[144,2688]{1,0:T(8,128)(2,1)S(1)}, bf16[144,2688]{1,0:T(8,128)(2,1)}, u32[]{:S(2)}, u32[]{:S(2)}) %collective-permute-start.12) | collective-permute-done | bytes 774176 | tf_op jit(solution)/shard_map/ppermute | solution.py:32
  94.3 3.3 collective-permute-start.4
  102.2 12.0 %shard_map.282 = (bf16[256,1152]{1,0:T(8,128)(2,1)}, f32[256,1024]{1,0:T(8,128)}, f32[256,256]{1,0:T(8,128)}, bf16[256,1024]{1,0:T(8,128)(2,1)}, bf16[768,512]{1...) custom-call(s32[2]{0:T(128)} %pad_add_fusion.place_ref, ...), custom_call_target="tpu_custom_call" | custom-call | flops 2315255808 | bytes 10911744 | tf_op jit(solution)/shard_map/pallas_call | solution.py:257
  121.0 4.0 collective-permute-done.21.refs_8_.refs_15_.refs_17_
  126.9 20.3 %collective-permute-done.23.refs_10_.refs_17_.refs_19_ = bf16[144,3520]{1,0:T(8,128)(2,1)S(1)} collective-permute-done((bf16[144,3520]{1,0:T(8,128)(2,1)}, bf16[144,3520]{1,0:T(8,128)(2,1)S(1)}, u32[]{:S(2)}, u32[]{:S(2)}) %collective-permute-start.23) | collective-permute-done | bytes 1013792 | tf_op jit(solution)/shard_map/ppermute | solution.py:32
  148.8 6.6 %collective-permute-done.16.refs_1_ = bf16[256,1152]{1,0:T(8,128)(2,1)S(1)} collective-permute-done((bf16[256,1152]{1,0:T(8,128)(2,1)S(1)}, bf16[256,1152]{1,0:T(8,128)(2,1)S(1)}, u32[]{:S(2)}, u32[]{:S(2)}) %collective-permute-start.16) | collective-permute-done | bytes 589856 | tf_op jit(solution)/shard_map/ppermute | solution.py:32
  158.7 13.3 %collective-permute-done.17.refs_2_ = bf16[256,1152]{1,0:T(8,128)(2,1)S(1)} collective-permute-done((bf16[256,1152]{1,0:T(8,128)(2,1)S(1)}, bf16[256,1152]{1,0:T(8,128)(2,1)S(1)}, u32[]{:S(2)}, u32[]{:S(2)}) %collective-permute-start.17) | collective-permute-done | bytes 589856 | tf_op jit(solution)/shard_map/ppermute | solution.py:32
  175.8 18.2 %shard_map.283 = (bf16[1024,1728]{1,0:T(8,128)(2,1)}, bf16[1024,1728]{1,0:T(8,128)(2,1)}, bf16[1024,1728]{1,0:T(8,128)(2,1)}) custom-call(s32[2]{0:T(128)} %pad_add_fusion.place_ref, bf16[256,1152]{1,0:T(8,128)(2,1)} %copy-done.37, bf16[256,1152]{1,0:T(8,128)(2,1)} %copy-done.38, bf16[256,1152]{1,0:T(8,128)(2,1)} %copy-done.39, ...), custom_call_target="tpu_custom_call" | custom-call | flops 8153726976 | bytes 18579456 | tf_op jit(solution)/shard_map/pallas_call | solution.py:496
  202.9 10.4 %shard_map.284 = (bf16[256,1152]{1,0:T(8,128)(2,1)}, bf16[256,1152]{1,0:T(8,128)(2,1)}, bf16[256,1152]{1,0:T(8,128)(2,1)}, bf16[256,1152]{1,0:T(8,128)(2,1)}) custom-call(s32[2]{0:T(128)} %pad_add_fusion.place_ref, bf16[1024,1728]{1,0:T(8,128)(2,1)} %get-tuple-element.103.act_ref.refs_4_, bf16[144,1728]{1,0:T(8,128)(2,1)} %copy-done.11, ...), custom_call_target="tpu_custom_call" | custom-call | flops 4076863488 | bytes 9879552 | tf_op jit(solution)/shard_map/pallas_call | solution.py:257
  216.0 13.0 %collective-permute-done.31.far_ref = bf16[256,1152]{1,0:T(8,128)(2,1)S(1)} collective-permute-done((bf16[256,1152]{1,0:T(8,128)(2,1)}, bf16[256,1152]{1,0:T(8,128)(2,1)S(1)}, u32[]{:S(2)}, u32[]{:S(2)}) %collective-permute-start.31) | collective-permute-done | bytes 589856 | tf_op jit(solution)/shard_map/ppermute | solution.py:47
  229.0 13.3 %collective-permute-done.32.across_ref = bf16[256,1152]{1,0:T(8,128)(2,1)S(1)} collective-permute-done((bf16[256,1152]{1,0:T(8,128)(2,1)}, bf16[256,1152]{1,0:T(8,128)(2,1)S(1)}, u32[]{:S(2)}, u32[]{:S(2)}) %collective-permute-start.32) | collective-permute-done | bytes 589856 | tf_op jit(solution)/shard_map/ppermute | solution.py:32
  243.4 3.9 shard_map.285
  250.0 11.7 %shard_map.286 = (bf16[256,1152]{1,0:T(8,128)(2,1)}, bf16[256,1728]{1,0:T(8,128)(2,1)}, bf16[256,1728]{1,0:T(8,128)(2,1)}) custom-call(s32[2]{0:T(128)} %pad_add_fusion.place_ref, bf16[256,1152]{1,0:T(8,128)(2,1)} %get-tuple-element.115.refs_0_.refs_3_, bf16[1024,1728]{1,0:T(8,128)(2,1)} %get-tuple-element.116.refs_1_.refs_3_, ...), custom_call_target="tpu_custom_call" | custom-call | flops 3057647616 | bytes 17252352 | tf_op jit(solution)/shard_map/pallas_call | solution.py:257
  262.9 13.4 %collective-permute-done.35.refs_1_ = bf16[256,1152]{1,0:T(8,128)(2,1)S(1)} collective-permute-done((bf16[256,1152]{1,0:T(8,128)(2,1)}, bf16[256,1152]{1,0:T(8,128)(2,1)S(1)}, u32[]{:S(2)}, u32[]{:S(2)}) %collective-permute-start.35) | collective-permute-done | bytes 589856 | tf_op jit(solution)/shard_map/ppermute | solution.py:32
  278.0 20.4 %shard_map.287 = (bf16[256,1152]{1,0:T(8,128)(2,1)}, bf16[256,1152]{1,0:T(8,128)(2,1)}, bf16[256,1152]{1,0:T(8,128)(2,1)}, bf16[768,1728]{1,0:T(8,128)(2,1)}, bf16[768,1728]{1,0:T(8,128)(2,1)}) custom-call(s32[2]{0:T(128)} %pad_add_fusion.place_ref, bf16[256,1152]{1,0:T(8,128)(2,1)} %copy-done.40, bf16[256,1152]{1,0:T(8,128)(2,1)} %copy-done.41, ...), custom_call_target="tpu_custom_call" | custom-call | flops 9172942848 | bytes 27869184 | tf_op jit(solution)/shard_map/pallas_call | solution.py:257
  298.4 11.0 %shard_map.288 = (bf16[4,144,1728]{2,1,0:T(8,128)(2,1)}, bf16[4,144,1728]{2,1,0:T(8,128)(2,1)}) custom-call(s32[2]{0:T(128)} %pad_add_fusion.place_ref, bf16[256,1152]{1,0:T(8,128)(2,1)} %copy-done.40, bf16[256,1152]{1,0:T(8,128)(2,1)} %copy-done.41, bf16[256,1152]{1,0:T(8,128)(2,1)} %copy-done.42, bf16[256,1152]{1,0:T(8,128)(2,1)} %get-tuple-element.115.refs_0_.refs_3_, ...), custom_call_target="tpu_custom_call" | custom-call | flops 4076863488 | bytes 9879552 | tf_op jit(solution)/shard_map/pallas_call | solution.py:257
  309.9 11.3 %shard_map.289 = (bf16[4,144,1728]{2,1,0:T(8,128)(2,1)}, bf16[4,144,1728]{2,1,0:T(8,128)(2,1)}) custom-call(s32[2]{0:T(128)} %pad_add_fusion.place_ref, bf16[256,1152]{1,0:T(8,128)(2,1)} %copy-done.37, bf16[256,1152]{1,0:T(8,128)(2,1)} %copy-done.38, bf16[256,1152]{1,0:T(8,128)(2,1)} %copy-done.39, bf16[256,1152]{1,0:T(8,128)(2,1)} %get-tuple-element.95.refs_3_, ...), custom_call_target="tpu_custom_call" | custom-call | flops 4076863488 | bytes 9879552 | tf_op jit(solution)/shard_map/pallas_call | solution.py:257
  329.8 8.6 %collective-permute-done.38 = bf16[1,144,1728]{2,1,0:T(8,128)(2,1)S(1)} collective-permute-done((bf16[1,144,1728]{2,1,0:T(8,128)(2,1)S(1)}, bf16[1,144,1728]{2,1,0:T(8,128)(2,1)S(1)}, u32[]{:S(2)}, u32[]{:S(2)}) %collective-permute-start.38) | collective-permute-done | bytes 497696 | tf_op jit(solution)/shard_map/ppermute | solution.py:32
  340.1 11.0 %shard_map.290 = (bf16[4,144,1728]{2,1,0:T(8,128)(2,1)}, bf16[4,144,1728]{2,1,0:T(8,128)(2,1)}) custom-call(s32[2]{0:T(128)} %pad_add_fusion.place_ref, bf16[256,1152]{1,0:T(8,128)(2,1)} %copy-done.37, bf16[256,1152]{1,0:T(8,128)(2,1)} %copy-done.38, bf16[256,1152]{1,0:T(8,128)(2,1)} %copy-done.39, bf16[256,1152]{1,0:T(8,128)(2,1)} %get-tuple-element.95.refs_3_, ...), custom_call_target="tpu_custom_call" | custom-call | flops 4076863488 | bytes 9879552 | tf_op jit(solution)/shard_map/pallas_call | solution.py:257
  355.5 6.0 %collective-permute-done.39 = bf16[144,1728]{1,0:T(8,128)(2,1)S(1)} collective-permute-done((bf16[144,1728]{1,0:T(8,128)(2,1)S(1)}, bf16[144,1728]{1,0:T(8,128)(2,1)S(1)}, u32[]{:S(2)}, u32[]{:S(2)}) %collective-permute-start.39) | collective-permute-done | bytes 497696 | tf_op jit(solution)/shard_map/ppermute | solution.py:32
  363.7 16.4 %shard_map.291 = (bf16[4,144,2048]{2,1,0:T(8,128)(2,1)}, bf16[4,144,2048]{2,1,0:T(8,128)(2,1)}, f32[256,1152]{1,0:T(8,128)}, f32[256,1152]{1,0:T(8,128)}, bf16[2...) custom-call(s32[2]{0:T(128)} %pad_add_fusion.place_ref, ...), custom_call_target="tpu_custom_call" | custom-call | flops 4429185024 | bytes 23003136 | tf_op jit(solution)/shard_map/pallas_call | solution.py:257
  396.6 4.3 collective-permute-done.61
  402.8 7.3 %shard_map.292 = (bf16[4,144,640]{2,1,0:T(8,128)(2,1)}, bf16[4,144,640]{2,1,0:T(8,128)(2,1)}, f32[256,1152]{1,0:T(8,128)}) custom-call(s32[2]{0:T(128)} %pad_add_fusion.place_ref, f32[256,512]{1,0:T(8,128)} %get-tuple-element.147.near_ref, bf16[256,512]{1,0:T(8,128)(2,1)} %copy-done.30, bf16[256,512]{1,0:T(8,128)(2,1)} %collective-permute-done.47.far_ref, ...), custom_call_target="tpu_custom_call" | custom-call | flops 603979776 | bytes 8847360 | tf_op jit(solution)/shard_map/pallas_call | solution.py:257
  414.5 6.1 %collective-permute-start.67 = (bf16[144,1728]{1,0:T(8,128)(2,1)S(1)}, bf16[144,1728]{1,0:T(8,128)(2,1)S(1)}, u32[]{:S(2)}, u32[]{:S(2)}) collective-permute-start(bf16[144,1728]{1,0:T(8,128)(2,1)S(1)} %fusion.13), channel_id=1, source_target_pairs={{0,8},{4,12},{8,0},{12,4},{16,24},{20,28},{24,16},{28,20},{1,9},{5... | collective-permute-start | bytes 1493000 | tf_op jit(solution)/shard_map/ppermute | solution.py:32
  426.4 9.8 %collective-permute-done.64 = bf16[144,1728]{1,0:T(8,128)(2,1)S(1)} collective-permute-done((bf16[144,1728]{1,0:T(8,128)(2,1)S(1)}, bf16[144,1728]{1,0:T(8,128)(2,1)S(1)}, u32[]{:S(2)}, u32[]{:S(2)}) %collective-permute-start.64) | collective-permute-done | bytes 497696 | tf_op jit(solution)/shard_map/ppermute | solution.py:32
  447.1 17.6 %collective-permute-done.49 = bf16[2,144,2048]{2,1,0:T(8,128)(2,1)} collective-permute-done((bf16[2,144,2048]{2,1,0:T(8,128)(2,1)}, bf16[2,144,2048]{2,1,0:T(8,128)(2,1)}, u32[]{:S(2)}, u32[]{:S(2)}) %collective-permute-start.49) | collective-permute-done | bytes 1179680 | tf_op jit(solution)/shard_map/ppermute | solution.py:32
  472.0 7.9 %collective-permute-done.50 = bf16[1,144,2048]{2,1,0:T(8,128)(2,1)S(1)} collective-permute-done((bf16[1,144,2048]{2,1,0:T(8,128)(2,1)S(1)}, bf16[1,144,2048]{2,1,0:T(8,128)(2,1)S(1)}, u32[]{:S(2)}, u32[]{:S(2)}) %collective-permute-start.50) | collective-permute-done | bytes 589856 | tf_op jit(solution)/shard_map/ppermute | solution.py:32
  485.3 9.1 %collective-permute-done.52 = bf16[36,2048]{1,0:T(8,128)(2,1)S(1)} collective-permute-done((bf16[36,2048]{1,0:T(8,128)(2,1)S(1)}, bf16[36,2048]{1,0:T(8,128)(2,1)S(1)}, u32[]{:S(2)}, u32[]{:S(2)}) %collective-permute-start.52) | collective-permute-done | bytes 147488 | tf_op jit(solution)/shard_map/ppermute | solution.py:37
  (256 shorter events, 139.4 us)
Async XLA Ops:
  28.7 44.9 %collective-permute-start.3 = (bf16[144,3520]{1,0:T(8,128)(2,1)S(1)}, bf16[144,3520]{1,0:T(8,128)(2,1)}, u32[]{:S(2)}, u32[]{:S(2)}) collective-permute-start(bf16[144,3520]{1,0:T(8,128)(2,1)S(1)} %concatenate.3), channel_id=1, source_target_pairs={{0,2},{1,3},{2,0},{3,1},{4,6},{5,7},{6,4},{7,5},{8,10},{9,11},{10,... | collective-permute-start | bytes 3041288 | tf_op jit(solution)/shard_map/ppermute | solution.py:32
  29.6 47.8 %collective-permute-start.5 = (bf16[256,1152]{1,0:T(8,128)(2,1)}, bf16[256,1152]{1,0:T(8,128)(2,1)}, u32[]{:S(2)}, u32[]{:S(2)}) collective-permute-start(bf16[256,1152]{1,0:T(8,128)(2,1)} %bitcast.8.near_ref.tokens_ref), channel_id=1, source_target_pairs={{0,4},{4,8},{8,12},{12,16},{16,20},{20,24},{24,28},{1,5},{5,9},{9,... | collective-permute-start | bytes 1769480 | tf_op jit(solution)/shard_map/ppermute | solution.py:23
  34.4 43.9 %collective-permute-start.6 = (bf16[256,1152]{1,0:T(8,128)(2,1)}, bf16[256,1152]{1,0:T(8,128)(2,1)}, u32[]{:S(2)}, u32[]{:S(2)}) collective-permute-start(bf16[256,1152]{1,0:T(8,128)(2,1)} %bitcast.8.near_ref.tokens_ref), channel_id=1, source_target_pairs={{0,8},{4,12},{8,16},{12,20},{16,24},{20,28},{1,9},{5,13},{9,17},{1... | collective-permute-start | bytes 1769480 | tf_op jit(solution)/shard_map/ppermute | solution.py:23
  38.5 33.2 %collective-permute-start.10 = (bf16[144,2688]{1,0:T(8,128)(2,1)}, bf16[144,2688]{1,0:T(8,128)(2,1)S(1)}, u32[]{:S(2)}, u32[]{:S(2)}) collective-permute-start(bf16[144,2688]{1,0:T(8,128)(2,1)} %shard_map.281.refs_0_), channel_id=1, source_target_pairs={{0,16},{4,20},{8,24},{12,28},{16,0},{20,4},{24,8},{28,12},{1,17},{... | collective-permute-start | bytes 2322440 | tf_op jit(solution)/shard_map/ppermute | solution.py:32
  38.7 39.5 %collective-permute-start.8 = (bf16[144,2688]{1,0:T(8,128)(2,1)}, bf16[144,2688]{1,0:T(8,128)(2,1)S(1)}, u32[]{:S(2)}, u32[]{:S(2)}) collective-permute-start(bf16[144,2688]{1,0:T(8,128)(2,1)} %shard_map.281.refs_0_), channel_id=1, source_target_pairs={{0,8},{4,12},{8,0},{12,4},{16,24},{20,28},{24,16},{28,20},{1,9},{5... | collective-permute-start | bytes 2322440 | tf_op jit(solution)/shard_map/ppermute | solution.py:32
  78.3 23.9 %collective-permute-start.9 = (bf16[144,2688]{1,0:T(8,128)(2,1)S(1)}, bf16[144,2688]{1,0:T(8,128)(2,1)}, u32[]{:S(2)}, u32[]{:S(2)}) collective-permute-start(bf16[144,2688]{1,0:T(8,128)(2,1)S(1)} %collective-permute-done.8.refs_2_), channel_id=1, source_target_pairs={{0,4},{4,0},{8,12},{12,8},{16,20},{20,16},{24,28},{28,24},{1,5},{5... | collective-permute-start | bytes 2322440 | tf_op jit(solution)/shard_map/ppermute | solution.py:32
  78.4 35.9 %collective-permute-start.19 = (bf16[144,3520]{1,0:T(8,128)(2,1)}, bf16[144,3520]{1,0:T(8,128)(2,1)}, u32[]{:S(2)}, u32[]{:S(2)}) collective-permute-start(bf16[144,3520]{1,0:T(8,128)(2,1)} %get-tuple-element.185), channel_id=1, source_target_pairs={{0,8},{4,12},{8,0},{12,4},{16,24},{20,28},{24,16},{28,20},{1,9},{5... | collective-permute-start | bytes 3041288 | tf_op jit(solution)/shard_map/ppermute | solution.py:32
  94.3 23.9 %collective-permute-start.4 = (bf16[144,1728]{1,0:T(8,128)(2,1)}, bf16[144,1728]{1,0:T(8,128)(2,1)}, u32[]{:S(2)}, u32[]{:S(2)}) collective-permute-start(bf16[144,1728]{1,0:T(8,128)(2,1)} %param.27), channel_id=1, source_target_pairs={{0,2},{1,3},{2,0},{3,1},{4,6},{5,7},{6,4},{7,5},{8,10},{9,11},{10,... | collective-permute-start | bytes 1493000 | tf_op jit(solution)/shard_map/ppermute | solution.py:32
  100.9 24.1 %collective-permute-start.21 = (bf16[144,3520]{1,0:T(8,128)(2,1)S(1)}, bf16[144,3520]{1,0:T(8,128)(2,1)S(1)}, u32[]{:S(2)}, u32[]{:S(2)}) collective-permute-start(bf16[144,3520]{1,0:T(8,128)(2,1)S(1)} %get-tuple-element.98.refs_4_.refs_11_.refs_13_), channel_id=1, source_target_pairs={{0,16},{4,20},{8,24},{12,28},{16,0},{20,4},{24,8},{28,12},{1,17},{... | collective-permute-start | bytes 3041288 | tf_op jit(solution)/shard_map/ppermute | solution.py:32
  114.3 32.9 %collective-permute-start.23 = (bf16[144,3520]{1,0:T(8,128)(2,1)}, bf16[144,3520]{1,0:T(8,128)(2,1)S(1)}, u32[]{:S(2)}, u32[]{:S(2)}) collective-permute-start(bf16[144,3520]{1,0:T(8,128)(2,1)} %collective-permute-done.19.refs_6_.refs_13_.refs_15_), channel_id=1, source_target_pairs={{0,16},{4,20},{8,24},{12,28},{16,0},{20,4},{24,8},{28,12},{1,17},{... | collective-permute-start | bytes 3041288 | tf_op jit(solution)/shard_map/ppermute | solution.py:32
  115.4 33.0 %collective-permute-start.15 = (bf16[256,1152]{1,0:T(8,128)(2,1)}, bf16[256,1152]{1,0:T(8,128)(2,1)S(1)}, u32[]{:S(2)}, u32[]{:S(2)}) collective-permute-start(bf16[256,1152]{1,0:T(8,128)(2,1)} %get-tuple-element.95.refs_3_), channel_id=1, source_target_pairs={{0,9},{1,8},{2,11},{3,10},{4,13},{5,12},{6,15},{7,14},{8,1},{9,0},... | collective-permute-start | bytes 1769480 | tf_op jit(solution)/shard_map/ppermute | solution.py:47
  119.5 28.8 %collective-permute-start.14 = (bf16[144,1728]{1,0:T(8,128)(2,1)S(1)}, bf16[144,1728]{1,0:T(8,128)(2,1)}, u32[]{:S(2)}, u32[]{:S(2)}) collective-permute-start(bf16[144,1728]{1,0:T(8,128)(2,1)S(1)} %get-tuple-element.188), channel_id=1, source_target_pairs={{0,8},{4,12},{8,0},{12,4},{16,24},{20,28},{24,16},{28,20},{1,9},{5... | collective-permute-start | bytes 1493000 | tf_op jit(solution)/shard_map/ppermute | solution.py:32
  120.8 34.7 %collective-permute-start.16 = (bf16[256,1152]{1,0:T(8,128)(2,1)S(1)}, bf16[256,1152]{1,0:T(8,128)(2,1)S(1)}, u32[]{:S(2)}, u32[]{:S(2)}) collective-permute-start(bf16[256,1152]{1,0:T(8,128)(2,1)S(1)} %copy-done.36), channel_id=1, source_target_pairs={{0,8},{4,12},{8,0},{12,4},{16,24},{20,28},{24,16},{28,20},{1,9},{5... | collective-permute-start | bytes 1769480 | tf_op jit(solution)/shard_map/ppermute | solution.py:32
  125.1 48.1 %collective-permute-start.22 = (bf16[144,3520]{1,0:T(8,128)(2,1)S(1)}, bf16[144,3520]{1,0:T(8,128)(2,1)S(1)}, u32[]{:S(2)}, u32[]{:S(2)}) collective-permute-start(bf16[144,3520]{1,0:T(8,128)(2,1)S(1)} %collective-permute-done.21.refs_8_.refs_15_.refs_17_), channel_id=1, source_target_pairs={{0,4},{4,0},{8,12},{12,8},{16,20},{20,16},{24,28},{28,24},{1,5},{5... | collective-permute-start | bytes 3041288 | tf_op jit(solution)/shard_map/ppermute | solution.py:32
  147.2 26.3 %collective-permute-start.20 = (bf16[144,3520]{1,0:T(8,128)(2,1)}, bf16[144,3520]{1,0:T(8,128)(2,1)S(1)}, u32[]{:S(2)}, u32[]{:S(2)}) collective-permute-start(bf16[144,3520]{1,0:T(8,128)(2,1)} %collective-permute-done.19.refs_6_.refs_13_.refs_15_), channel_id=1, source_target_pairs={{0,4},{4,0},{8,12},{12,8},{16,20},{20,16},{24,28},{28,24},{1,5},{5... | collective-permute-start | bytes 3041288 | tf_op jit(solution)/shard_map/ppermute | solution.py:32
  148.3 25.2 %collective-permute-start.18 = (bf16[144,3520]{1,0:T(8,128)(2,1)S(1)}, bf16[144,3520]{1,0:T(8,128)(2,1)S(1)}, u32[]{:S(2)}, u32[]{:S(2)}) collective-permute-start(bf16[144,3520]{1,0:T(8,128)(2,1)S(1)} %get-tuple-element.98.refs_4_.refs_11_.refs_13_), channel_id=1, source_target_pairs={{0,4},{4,0},{8,12},{12,8},{16,20},{20,16},{24,28},{28,24},{1,5},{5... | collective-permute-start | bytes 3041288 | tf_op jit(solution)/shard_map/ppermute | solution.py:32
  148.4 25.1 %collective-permute-start.24 = (bf16[144,3520]{1,0:T(8,128)(2,1)S(1)}, bf16[144,3520]{1,0:T(8,128)(2,1)S(1)}, u32[]{:S(2)}, u32[]{:S(2)}) collective-permute-start(bf16[144,3520]{1,0:T(8,128)(2,1)S(1)} %collective-permute-done.23.refs_10_.refs_17_.refs_19_), channel_id=1, source_target_pairs={{0,4},{4,0},{8,12},{12,8},{16,20},{20,16},{24,28},{28,24},{1,5},{5... | collective-permute-start | bytes 3041288 | tf_op jit(solution)/shard_map/ppermute | solution.py:32
  172.0 25.3 %collective-permute-start.27 = (bf16[144,1728]{1,0:T(8,128)(2,1)S(1)}, bf16[144,1728]{1,0:T(8,128)(2,1)}, u32[]{:S(2)}, u32[]{:S(2)}) collective-permute-start(bf16[144,1728]{1,0:T(8,128)(2,1)S(1)} %get-tuple-element.104.refs_0_.refs_3_.refs_5_), channel_id=1, source_target_pairs={{0,16},{4,20},{8,24},{12,28},{16,0},{20,4},{24,8},{28,12},{1,17},{... | collective-permute-start | bytes 1493000 | tf_op jit(solution)/shard_map/ppermute | solution.py:32
  214.4 27.9 %collective-permute-start.32 = (bf16[256,1152]{1,0:T(8,128)(2,1)}, bf16[256,1152]{1,0:T(8,128)(2,1)S(1)}, u32[]{:S(2)}, u32[]{:S(2)}) collective-permute-start(bf16[256,1152]{1,0:T(8,128)(2,1)} %get-tuple-element.110), channel_id=1, source_target_pairs={{0,8},{4,12},{8,0},{12,4},{16,24},{20,28},{24,16},{28,20},{1,9},{5... | collective-permute-start | bytes 1769480 | tf_op jit(solution)/shard_map/ppermute | solution.py:32
  215.7 26.7 %collective-permute-start.33 = (bf16[256,1152]{1,0:T(8,128)(2,1)}, bf16[256,1152]{1,0:T(8,128)(2,1)S(1)}, u32[]{:S(2)}, u32[]{:S(2)}) collective-permute-start(bf16[256,1152]{1,0:T(8,128)(2,1)} %get-tuple-element.111), channel_id=1, source_target_pairs={{0,1},{1,0},{2,3},{3,2},{4,5},{5,4},{6,7},{7,6},{8,9},{9,8},{10,11... | collective-permute-start | bytes 1769480 | tf_op jit(solution)/shard_map/ppermute | solution.py:32
  248.4 27.9 %collective-permute-start.35 = (bf16[256,1152]{1,0:T(8,128)(2,1)}, bf16[256,1152]{1,0:T(8,128)(2,1)S(1)}, u32[]{:S(2)}, u32[]{:S(2)}) collective-permute-start(bf16[256,1152]{1,0:T(8,128)(2,1)} %get-tuple-element.115.refs_0_.refs_3_), channel_id=1, source_target_pairs={{0,8},{4,12},{8,0},{12,4},{16,24},{20,28},{24,16},{28,20},{1,9},{5... | collective-permute-start | bytes 1769480 | tf_op jit(solution)/shard_map/ppermute | solution.py:32
  248.4 27.9 %collective-permute-start.36 = (bf16[256,1152]{1,0:T(8,128)(2,1)}, bf16[256,1152]{1,0:T(8,128)(2,1)S(1)}, u32[]{:S(2)}, u32[]{:S(2)}) collective-permute-start(bf16[256,1152]{1,0:T(8,128)(2,1)} %get-tuple-element.115.refs_0_.refs_3_), channel_id=1, source_target_pairs={{0,1},{1,0},{2,3},{3,2},{4,5},{5,4},{6,7},{7,6},{8,9},{9,8},{10,11... | collective-permute-start | bytes 1769480 | tf_op jit(solution)/shard_map/ppermute | solution.py:32
  321.4 42.4 %collective-permute-start.43 = (bf16[256,1152]{1,0:T(8,128)(2,1)}, bf16[256,1152]{1,0:T(8,128)(2,1)}, u32[]{:S(2)}, u32[]{:S(2)}) collective-permute-start(bf16[256,1152]{1,0:T(8,128)(2,1)} %get-tuple-element.136), channel_id=1, source_target_pairs={{0,9},{1,8},{2,11},{3,10},{4,13},{5,12},{6,15},{7,14},{8,1},{9,0},... | collective-permute-start | bytes 1769480 | tf_op jit(solution)/shard_map/ppermute | solution.py:47
  322.5 41.2 %collective-permute-start.44 = (bf16[256,1152]{1,0:T(8,128)(2,1)}, bf16[256,1152]{1,0:T(8,128)(2,1)}, u32[]{:S(2)}, u32[]{:S(2)}) collective-permute-start(bf16[256,1152]{1,0:T(8,128)(2,1)} %get-tuple-element.137), channel_id=1, source_target_pairs={{0,8},{4,12},{8,0},{12,4},{16,24},{20,28},{24,16},{28,20},{1,9},{5... | collective-permute-start | bytes 1769480 | tf_op jit(solution)/shard_map/ppermute | solution.py:32
  322.5 41.2 %collective-permute-start.45 = (bf16[256,1152]{1,0:T(8,128)(2,1)}, bf16[256,1152]{1,0:T(8,128)(2,1)}, u32[]{:S(2)}, u32[]{:S(2)}) collective-permute-start(bf16[256,1152]{1,0:T(8,128)(2,1)} %get-tuple-element.138), channel_id=1, source_target_pairs={{0,1},{1,0},{2,3},{3,2},{4,5},{5,4},{6,7},{7,6},{8,9},{9,8},{10,11... | collective-permute-start | bytes 1769480 | tf_op jit(solution)/shard_map/ppermute | solution.py:32
  351.9 39.0 %collective-permute-start.41 = (bf16[4,144,1728]{2,1,0:T(8,128)(2,1)}, bf16[4,144,1728]{2,1,0:T(8,128)(2,1)S(1)}, u32[]{:S(2)}, u32[]{:S(2)}) collective-permute-start(bf16[4,144,1728]{2,1,0:T(8,128)(2,1)} %get-tuple-element.132), channel_id=1, source_target_pairs={{0,4},{4,0},{8,12},{12,8},{16,20},{20,16},{24,28},{28,24},{1,5},{5... | collective-permute-start | bytes 5971976 | tf_op jit(solution)/shard_map/ppermute | solution.py:32
  384.3 36.6 %collective-permute-start.48 = (bf16[4,144,2048]{2,1,0:T(8,128)(2,1)}, bf16[4,144,2048]{2,1,0:T(8,128)(2,1)}, u32[]{:S(2)}, u32[]{:S(2)}) collective-permute-start(bf16[4,144,2048]{2,1,0:T(8,128)(2,1)} %get-tuple-element.158), channel_id=1, source_target_pairs={{0,4},{4,0},{8,12},{12,8},{16,20},{20,16},{24,28},{28,24},{1,5},{5... | collective-permute-start | bytes 7077896 | tf_op jit(solution)/shard_map/ppermute | solution.py:32
  411.7 24.4 %collective-permute-start.64 = (bf16[144,1728]{1,0:T(8,128)(2,1)S(1)}, bf16[144,1728]{1,0:T(8,128)(2,1)S(1)}, u32[]{:S(2)}, u32[]{:S(2)}) collective-permute-start(bf16[144,1728]{1,0:T(8,128)(2,1)S(1)} %broadcast_select_fusion.4), channel_id=1, source_target_pairs={{0,2},{1,3},{2,0},{3,1},{4,6},{5,7},{6,4},{7,5},{8,10},{9,11},{10,... | collective-permute-start | bytes 1493000 | tf_op jit(solution)/shard_map/ppermute | solution.py:32
  413.8 26.5 %collective-permute-start.66 = (bf16[1,144,1728]{2,1,0:T(8,128)(2,1)}, bf16[1,144,1728]{2,1,0:T(8,128)(2,1)S(1)}, u32[]{:S(2)}, u32[]{:S(2)}) collective-permute-start(bf16[1,144,1728]{2,1,0:T(8,128)(2,1)} %get-tuple-element.165), channel_id=1, source_target_pairs={{0,16},{4,20},{8,24},{12,28},{16,0},{20,4},{24,8},{28,12},{1,17},{... | collective-permute-start | bytes 1493000 | tf_op jit(solution)/shard_map/ppermute | solution.py:32
  414.5 25.9 %collective-permute-start.67 = (bf16[144,1728]{1,0:T(8,128)(2,1)S(1)}, bf16[144,1728]{1,0:T(8,128)(2,1)S(1)}, u32[]{:S(2)}, u32[]{:S(2)}) collective-permute-start(bf16[144,1728]{1,0:T(8,128)(2,1)S(1)} %fusion.13), channel_id=1, source_target_pairs={{0,8},{4,12},{8,0},{12,4},{16,24},{20,28},{24,16},{28,20},{1,9},{5... | collective-permute-start | bytes 1493000 | tf_op jit(solution)/shard_map/ppermute | solution.py:32
  424.9 39.8 %collective-permute-start.49 = (bf16[2,144,2048]{2,1,0:T(8,128)(2,1)}, bf16[2,144,2048]{2,1,0:T(8,128)(2,1)}, u32[]{:S(2)}, u32[]{:S(2)}) collective-permute-start(bf16[2,144,2048]{2,1,0:T(8,128)(2,1)} %slice_bitcast_fusion), channel_id=1, source_target_pairs={{0,8},{4,12},{8,0},{12,4},{16,24},{20,28},{24,16},{28,20},{1,9},{5... | collective-permute-start | bytes 3538952 | tf_op jit(solution)/shard_map/ppermute | solution.py:32
  442.1 40.7 %collective-permute-start.68 = (bf16[144,1728]{1,0:T(8,128)(2,1)}, bf16[144,1728]{1,0:T(8,128)(2,1)}, u32[]{:S(2)}, u32[]{:S(2)}) collective-permute-start(bf16[144,1728]{1,0:T(8,128)(2,1)} %broadcast_select_fusion.2), channel_id=1, source_target_pairs={{0,2},{1,3},{2,0},{3,1},{4,6},{5,7},{6,4},{7,5},{8,10},{9,11},{10,... | collective-permute-start | bytes 1493000 | tf_op jit(solution)/shard_map/ppermute | solution.py:32
  (80 other events, 1162.3 us)

commit v4 on v3

v4 whole, which is shorter than its diff:
```python
import functools

import jax
import jax.numpy as jnp
from jax import lax
from jax.experimental import pallas as pl
from jax.experimental.pallas import tpu as pltpu
from jax.sharding import PartitionSpec as P

WINDOW = 512
NORM_EPS = 1e-06
ROPE_BASE = 10000.0
NEGATIVE = -1e30
LANES = 128
VMEM_LIMIT = 56 * 2**20
PIECES = 8
BF16 = jnp.bfloat16
F32 = jnp.float32


def from_behind(value, steps):
    count = lax.axis_size("seq")
    first, last = (max(0, -steps), min(count, count - steps))
    return lax.ppermute(value, "seq", [(source, source + steps) for source in range(first, last)])


def seq_masks():
    return [1 << bit for bit in range(lax.axis_size("seq").bit_length() - 1)]


def swap(value, axis, mask):
    count = lax.axis_size(axis)
    return lax.ppermute(value, axis, [(source, source ^ mask) for source in range(count)])


def shift(value, axis, steps):
    count = lax.axis_size(axis)
    return lax.ppermute(value, axis, [(source, (source + steps) % count) for source in range(count)])


def sync(state):
    return lax.optimization_barrier(state)


class Parts:
    def __init__(self, arrays, where):
        self.arrays, self.where = list(arrays), tuple(where)
        self.width = arrays[0].shape[-1]
        self.rows = arrays[0].shape[-2] * len(where)


def core_stack(parts):
    stack = jnp.stack(list(parts.values())) if len(parts) > 1 else list(parts.values())[0][None]
    return tuple(parts), swap(stack, "seq", 1)


def all_parts(parts, cores, *which):
    arrays, where = [], {}
    for rel, part in parts.items():
        where[rel] = (len(arrays), which)
        arrays.append(part)
    for rels, stack in cores:
        for index, rel in enumerate(rels):
            where[rel ^ 1] = (len(arrays), (index,) + which)
        arrays.append(stack)
    places = [where[rel] for rel in range(len(where))]
    if arrays[0].shape[-2] % 16 == 0:
        return Parts(arrays, places)
    index = jnp.arange(len(places), dtype=jnp.int32) ^ lax.axis_index("seq")
    blocks = [arrays[number][block] for number, block in places]
    whole = jnp.take(jnp.stack(blocks), index, axis=0, mode="clip")
    return Parts([whole.reshape(-1, whole.shape[-1])], [(0, ())])


def add_rounded(first, second):
    return (first.astype(F32) + second.astype(F32)).astype(BF16)


def cut(pair, count):
    if len(pair) == 2:
        return pair
    whole = pair[0]
    index = jnp.arange(count, dtype=jnp.int32) ^ lax.axis_index("seq")
    blocks = whole.reshape(whole.shape[:-2] + (count, -1, whole.shape[-1]))
    blocks = jnp.take(blocks, index, axis=blocks.ndim - 3, mode="clip")
    return blocks[..., 0::2, :, :], blocks[..., 1::2, :, :]


def cores_send(pair):
    keep, send = cut(pair, lax.axis_size("seq"))
    return keep, swap(send, "seq", 1)


def far_step(part):
    masks = [mask for mask in seq_masks() if mask > 2][::-1]
    for mask in masks[:-1]:
        half = part.shape[0] // 2
        part = add_rounded(part[:half], swap(part[half:], "seq", mask))
    half = part.shape[0] // 2
    return part[:half], swap(part[half:], "seq", masks[-1])


def across_step(part):
    part = part.reshape((-1, 2) + part.shape[1:])
    return part[:, 0], swap(part[:, 1], "seq", 2)


def straight(part, *steps):
    return [swap(part[step], "seq", 2 * step) for step in steps]


def planes_send(rows):
    planes = lax.axis_size("fsdp")
    blocks = rows.reshape((planes, -1) + rows.shape[1:])
    mine = lax.axis_index("fsdp")
    sent = [lax.dynamic_index_in_dim(blocks, mine, 0, keepdims=False)]
    for steps in range(1, planes):
        send = lax.dynamic_index_in_dim(blocks, (mine + steps) % planes, 0, keepdims=False)
        sent.append(shift(send, "fsdp", steps))
    return sent


def add_up(terms):
    total = terms[0].astype(F32)
    for term in terms[1:]:
        total = total + term.astype(F32)
    return total


def dot(left, right):
    return jnp.dot(left, right, preferred_element_type=F32)


def dot_t(left, right):
    return lax.dot_general(left, right, (((1,), (1,)), ((), ())), preferred_element_type=F32)


def dot_tn(left, right):
    return lax.dot_general(left, right, (((0,), (0,)), ((), ())), preferred_element_type=F32)


def inverse_rms(values):
    return lax.rsqrt(jnp.mean(values * values, axis=-1, keepdims=True) + NORM_EPS)


def norm_back(normed, scale, gain, upstream):
    scaled = upstream * gain
    back = scale * (scaled - normed * jnp.mean(scaled * normed, axis=-1, keepdims=True))
    return back, jnp.sum(upstream * normed, axis=0, keepdims=True)


def rotate(values, cosine, sine):
    half = values.shape[-1] // 2
    first, second = values[:, :half], values[:, half:]
    return jnp.concatenate(
        [first * cosine - second * sine, second * cosine + first * sine], axis=-1
    )


def iota(shape, dim):
    return lax.broadcasted_iota(jnp.int32, shape, dim)


def unit(shape, hits):
    return jnp.where(hits, 1.0, 0.0).astype(BF16)


def spread_matrix(narrow, wide, narrow_rows, wide_rows):
    row, col = iota((narrow, wide), 0), iota((narrow, wide), 1)
    return unit((narrow, wide), col == (row // narrow_rows) * wide_rows + row % narrow_rows)


def tiles_of(width, step):
    return [(start, min(step, width - start)) for start in range(0, width, step)]


def slots(where):
    return max(PIECES, len(where))


def start_placing(where, refs, dest, sems, base, seq, lane=0, lanes=None):
    copies = []
    if len(where) == 1:
        whole = refs[0] if lanes is None else refs[0].at[:, pl.ds(lane, lanes)]
        count = PIECES if whole.shape[0] % (16 * PIECES) == 0 else 1
        rows = whole.shape[0] // count
        pieces = [(index * rows, whole.at[pl.ds(index * rows, rows), :]) for index in range(count)]
        copies = [
            pltpu.make_async_copy(part, dest.at[pl.ds(start, rows), :], sems.at[base + index])
            for index, (start, part) in enumerate(pieces)
        ]
        for copy in copies:
            copy.start()
        return copies
    for rel, (number, block) in enumerate(where):
        part = refs[number].at[block] if block else refs[number]
        rows = part.shape[0]
        start = pl.multiple_of((seq ^ rel) * rows, 16) if len(where) > 1 else 0
        if lanes is not None:
            part = part.at[:, pl.ds(lane, lanes)]
        copies.append(
            pltpu.make_async_copy(part, dest.at[pl.ds(start, rows), :], sems.at[base + rel])
        )
    for copy in copies:
        copy.start()
    return copies


def start_cutting(whole, outs, sems, base, seq, which=None):
    if which is not None:
        outs = [out.at[which] for out in outs]
    if len(outs) == 1:
        copies = [pltpu.make_async_copy(whole, outs[0], sems.at[base])]
    else:
        half, rows = outs[0].shape[0], outs[0].shape[1]
        copies = []
        for rel in range(2 * half):
            start = pl.multiple_of((seq ^ rel) * rows, 16)
            copies.append(
                pltpu.make_async_copy(
                    whole.at[pl.ds(start, rows), :], outs[rel % 2].at[rel // 2], sems.at[base + rel]
                )
            )
    for copy in copies:
        copy.start()
    return copies


def cut_shapes(height, width, count):
    rows = height // count
    if rows % 16:
        return [jax.ShapeDtypeStruct((height, width), BF16)]
    return [jax.ShapeDtypeStruct((count // 2, rows, width), BF16)] * 2


def wait_all(copies):
    for copy in copies:
        copy.wait()


SMEM_SPEC = pl.BlockSpec(memory_space=pltpu.SMEM)
VMEM_SPEC = pl.BlockSpec(memory_space=pltpu.VMEM)
ANY_SPEC = pl.BlockSpec(memory_space=pl.ANY)


def call(kernel, outs, out_specs, ins, in_specs, scratch=(), flops=0, moved=0, exps=0):
    return pl.pallas_call(
        kernel,
        out_shape=tuple(outs),
        in_specs=list(in_specs),
        out_specs=tuple(out_specs),
        scratch_shapes=list(scratch),
        compiler_params=pltpu.CompilerParams(vmem_limit_bytes=VMEM_LIMIT),
        cost_estimate=pl.CostEstimate(flops=flops, bytes_accessed=moved, transcendentals=exps),
    )(*ins)


def shape_of(dims, dtype):
    return jax.ShapeDtypeStruct(dims, dtype)


def pack_kernel(wq_ref, wk_ref, wv_ref, wo_ref, *refs):
    wide, narrow, out_ref = refs[:4], refs[4:6], refs[6]
    rows, heads_width, head_dim = wq_ref.shape[0], wq_ref.shape[1], wk_ref.shape[1]
    out_ref[:, :heads_width] = wq_ref[...]
    out_ref[:, heads_width : heads_width + head_dim] = wk_ref[...]
    out_ref[:, heads_width + head_dim : heads_width + 2 * head_dim] = wv_ref[...]
    row = iota((16, rows), 0)
    held = jnp.zeros((16, rows), F32)
    for index, ref in enumerate(wide):
        held = held + jnp.where(row == index, ref[...].astype(F32), 0.0)
    small = narrow[0].shape[1]
    fit = unit((small, rows), iota((small, rows), 0) == iota((small, rows), 1))
    for index, ref in enumerate(narrow):
        spread = dot(jnp.broadcast_to(ref[...].astype(F32), (16, small)).astype(BF16), fit)
        held = held + jnp.where(row == 4 + index, spread, 0.0)
    place = unit((16, LANES), iota((16, LANES), 0) == iota((16, LANES), 1))
    gain_start = heads_width + 2 * head_dim
    out_ref[:, gain_start : gain_start + LANES] = dot_tn(held.astype(BF16), place).astype(BF16)
    out_ref[:, gain_start + LANES :] = wo_ref[...]


def pack_attn(w_query, w_key, w_value, w_out, wide, narrow):
    rows = w_query.shape[0]
    width = 2 * w_query.shape[1] + 2 * w_key.shape[1] + LANES
    ins = [w_query, w_key, w_value, w_out] + [vec.reshape(1, -1) for vec in wide + narrow]
    return call(
        pack_kernel,
        [shape_of((rows, width), BF16)],
        [VMEM_SPEC],
        ins,
        [VMEM_SPEC] * len(ins),
    )[0]


def planes_kernel(place_ref, *refs):
    parts, out_ref = refs[:-1], refs[-1]
    count, rows = len(parts), parts[0].shape[0]
    total = None
    for steps, part in enumerate(parts):
        plane = lax.rem(place_ref[1] - steps + count, count)
        row, col = iota((count * rows, rows), 0), iota((count * rows, rows), 1)
        term = dot(unit((count * rows, rows), row == col + plane * rows), part[...])
        total = term if total is None else total + term
    out_ref[...] = total.astype(BF16)


def place_planes(parts, place):
    count = len(parts)
    rows, width = parts[0].shape
    return call(
        planes_kernel,
        [shape_of((count * rows, width), BF16)],
        [VMEM_SPEC],
        [place] + parts,
        [SMEM_SPEC] + [VMEM_SPEC] * count,
        flops=2 * count * count * rows * rows * width,
        moved=4 * count * rows * width,
    )[0]


def attend_kernel(
    where,
    ref_count,
    narrow_rows,
    wide_rows,
    head_count,
    place_ref,
    near_ref,
    back_ref,
    far_ref,
    cos_ref,
    sin_ref,
    low_ref,
    *refs,
):
    parts, refs = refs[:ref_count], refs[ref_count:]
    (
        attn_in_ref,
        query_lin_ref,
        key_lin_ref,
        query_ref,
        keys_ref,
        probs_ref,
        attended_ref,
        gains_ref,
        small_gains_ref,
        attn_out_ref,
        middle_ref,
        ffn_in_ref,
    ) = refs[:12]
    weights, inside, sems = refs[12:]
    copies = start_placing(where, parts, weights, sems, 0, place_ref[0])
    rows, width = near_ref.shape
    head_dim = key_lin_ref.shape[1]
    heads_width = head_count * head_dim
    score_scale = head_dim**-0.5
    blocks = [far_ref, back_ref, near_ref]
    scales = []
    for ref in blocks:
        scales.append(inverse_rms(ref[...].astype(F32)))
    wait_all(copies)
    gain_start = heads_width + 2 * head_dim
    gain_cols = weights[:, gain_start : gain_start + LANES]
    pick = unit((8, LANES), iota((8, LANES), 0) == iota((8, LANES), 1))
    gains = dot_t(pick, gain_cols)
    spread = spread_matrix(head_dim, width, narrow_rows, wide_rows)
    small_gains = dot_t(gains.astype(BF16), spread)
    gains_ref[...] = gains
    small_gains_ref[...] = small_gains
    gain_an, gain_q, gain_k = gains[0:1], small_gains[4:5], small_gains[5:6]
    for index, ref in enumerate(blocks):
        normed = ref[...].astype(F32) * scales[index] * gain_an
        inside[index * rows : (index + 1) * rows, :] = normed.astype(BF16)
    attn_in_ref[...] = inside[2 * rows :, :]
    for index in range(3):
        span = slice(index * rows, (index + 1) * rows)
        part_in = inside[span, :]
        key_lin = dot(part_in, weights[:, heads_width : heads_width + head_dim])
        value = dot(part_in, weights[:, heads_width + head_dim : heads_width + 2 * head_dim])
        key = rotate(key_lin * inverse_rms(key_lin) * gain_k, cos_ref[span, :], sin_ref[span, :])
        keys_ref[span, :head_dim] = key.astype(BF16)
        keys_ref[span, head_dim:] = value.astype(BF16)
        if index == 2:
            key_lin_ref[...] = key_lin
    cosine, sine = cos_ref[2 * rows :, :], sin_ref[2 * rows :, :]
    column = iota((rows, 3 * rows), 1)
    seen = (column >= low_ref[...]) & (column <= iota((rows, 3 * rows), 0) + 2 * rows)
    for head in range(head_count):
        lanes = slice(head * head_dim, (head + 1) * head_dim)
        query_lin = dot(inside[2 * rows :, :], weights[:, lanes])
        query_lin_ref[:, lanes] = query_lin
        query = rotate(query_lin * inverse_rms(query_lin) * gain_q, cosine, sine).astype(BF16)
        query_ref[:, lanes] = query
        scores = jnp.where(seen, dot_t(query, keys_ref[:, :head_dim]) * score_scale, NEGATIVE)
        raised = jnp.exp(scores - jnp.max(scores, axis=-1, keepdims=True))
        probs = (raised / jnp.sum(raised, axis=-1, keepdims=True)).astype(BF16)
        probs_ref[head * rows : (head + 1) * rows, :] = probs
        attended_ref[:, lanes] = dot(probs, keys_ref[:, head_dim:]).astype(BF16)
    for start, size in tiles_of(width, 384):
        attn_out_ref[:, start : start + size] = dot_t(
            attended_ref[...], weights[start : start + size, gain_start + LANES :]
        )
    attn_out = attn_out_ref[...]
    middle = near_ref[...].astype(F32) + attn_out * inverse_rms(attn_out) * gains[1:2]
    middle_ref[...] = middle
    ffn_in_ref[...] = (middle * inverse_rms(middle) * gains[2:3]).astype(BF16)


def attend(place, tokens3, cosine, sine, lowest, parts, head_count, head_dim, narrow_rows, wide_rows):
    rows, width = tokens3[0].shape
    heads_width = head_count * head_dim
    pack = parts.width
    outs = [
        shape_of((rows, width), BF16),
        shape_of((rows, heads_width), F32),
        shape_of((rows, head_dim), F32),
        shape_of((rows, heads_width), BF16),
        shape_of((3 * rows, 2 * head_dim), BF16),
        shape_of((head_count * rows, 3 * rows), BF16),
        shape_of((rows, heads_width), BF16),
        shape_of((8, width), F32),
        shape_of((8, head_dim), F32),
        shape_of((rows, width), F32),
        shape_of((rows, width), F32),
        shape_of((rows, width), BF16),
    ]
    return call(
        functools.partial(
            attend_kernel, parts.where, len(parts.arrays), narrow_rows, wide_rows, head_count
        ),
        outs,
        [VMEM_SPEC] * len(outs),
        [place] + list(tokens3) + [cosine, sine, lowest] + parts.arrays,
        [SMEM_SPEC] + [VMEM_SPEC] * 6 + [ANY_SPEC] * len(parts.arrays),
        [
            pltpu.VMEM((width, pack), BF16),
            pltpu.VMEM((3 * rows, width), BF16),
            pltpu.SemaphoreType.DMA((slots(parts.where),)),
        ],
        flops=2 * rows * width * (heads_width + 6 * head_dim) + 12 * rows * rows * heads_width,
        moved=2 * width * pack + 16 * rows * width,
        exps=3 * head_count * rows * rows,
    )


def gelu_pair(gate):
    square = gate * gate
    tanh = jnp.tanh(gate * (0.7978845608028654 + 0.035677408136300125 * square))
    half = 0.5 + 0.5 * tanh
    value = gate * half
    slope = half + value * (1.0 - tanh) * (0.7978845608028654 + 0.10703222440890037 * square)
    return value, slope


def take_parts(wheres, counts, refs):
    parts = []
    for count in counts:
        parts.append(refs[:count])
        refs = refs[count:]
    bases = [sum(slots(where) for where in wheres[:index]) for index in range(len(wheres))]
    return parts, bases, refs


def parts_of(weights):
    wheres = tuple(parts.where for parts in weights)
    counts = tuple(len(parts.arrays) for parts in weights)
    arrays = [array for parts in weights for array in parts.arrays]
    return wheres, counts, arrays, sum(slots(where) for where in wheres)


def gate_up_body(rows_ref, gate_w, up_w, act_ref, gate_slope_ref, up_slope_ref):
    rows_in = rows_ref[...]
    for start, size in tiles_of(gate_w.shape[1], 256):
        lanes = slice(start, start + size)
        gate = dot(rows_in, gate_w[:, lanes])
        up = dot(rows_in, up_w[:, lanes])
        value, slope = gelu_pair(gate)
        act_ref[:, lanes] = (value * up).astype(BF16)
        gate_slope_ref[:, lanes] = (slope * up).astype(BF16)
        up_slope_ref[:, lanes] = value.astype(BF16)


def down_body(act_ref, down_w, out_ref):
    for start, size in tiles_of(down_w.shape[0], 384):
        lanes = slice(start, start + size)
        out_ref[:, lanes] = dot_t(act_ref[...], down_w[lanes, :]).astype(BF16)


def ffn_kernel(wheres, counts, place_ref, rows_ref, *refs):
    parts, bases, refs = take_parts(wheres, counts, refs)
    act_ref, gate_slope_ref, up_slope_ref, out_ref, gate_w, up_w, down_w, sems = refs
    seq = place_ref[0]
    copies = start_placing(wheres[0], parts[0], gate_w, sems, bases[0], seq)
    copies += start_placing(wheres[1], parts[1], up_w, sems, bases[1], seq)
    later = start_placing(wheres[2], parts[2], down_w, sems, bases[2], seq)
    wait_all(copies)
    gate_up_body(rows_ref, gate_w, up_w, act_ref, gate_slope_ref, up_slope_ref)
    wait_all(later)
    down_body(act_ref, down_w, out_ref)


def gate_up_kernel(wheres, counts, place_ref, rows_ref, *refs):
    parts, bases, refs = take_parts(wheres, counts, refs)
    act_ref, gate_slope_ref, up_slope_ref, gate_w, up_w, sems = refs
    seq = place_ref[0]
    copies = start_placing(wheres[0], parts[0], gate_w, sems, bases[0], seq)
    copies += start_placing(wheres[1], parts[1], up_w, sems, bases[1], seq)
    wait_all(copies)
    gate_up_body(rows_ref, gate_w, up_w, act_ref, gate_slope_ref, up_slope_ref)


def gate_up(place, rows_in, weights):
    rows, width = rows_in.shape
    hidden = weights[0].width
    wheres, counts, arrays, sem_count = parts_of(weights)
    return call(
        functools.partial(gate_up_kernel, wheres, counts),
        [shape_of((rows, hidden), BF16)] * 3,
        [VMEM_SPEC] * 3,
        [place, rows_in] + arrays,
        [SMEM_SPEC, VMEM_SPEC] + [ANY_SPEC] * len(arrays),
        [pltpu.VMEM((width, hidden), BF16)] * 2 + [pltpu.SemaphoreType.DMA((sem_count,))],
        flops=4 * rows * hidden * width,
        moved=4 * width * hidden + 6 * rows * hidden,
    )


def down_kernel(wheres, counts, place_ref, act_ref, *refs):
    parts, bases, refs = take_parts(wheres, counts, refs)
    out_ref, down_w, sems = refs
    wait_all(start_placing(wheres[0], parts[0], down_w, sems, bases[0], place_ref[0]))
    down_body(act_ref, down_w, out_ref)


def down(place, act, weights):
    rows, hidden = act.shape
    width = weights[0].rows
    wheres, counts, arrays, sem_count = parts_of(weights)
    return call(
        functools.partial(down_kernel, wheres, counts),
        [shape_of((rows, width), BF16)],
        [VMEM_SPEC],
        [place, act] + arrays,
        [SMEM_SPEC, VMEM_SPEC] + [ANY_SPEC] * len(arrays),
        [pltpu.VMEM((width, hidden), BF16), pltpu.SemaphoreType.DMA((sem_count,))],
        flops=2 * rows * hidden * width,
        moved=2 * width * hidden + 2 * rows * hidden,
    )[0]


def ffn(place, rows_in, weights):
    rows, width = rows_in.shape
    hidden = weights[0].width
    wheres, counts, arrays, sem_count = parts_of(weights)
    return call(
        functools.partial(ffn_kernel, wheres, counts),
        [shape_of((rows, hidden), BF16)] * 3 + [shape_of((rows, width), BF16)],
        [VMEM_SPEC] * 4,
        [place, rows_in] + arrays,
        [SMEM_SPEC, VMEM_SPEC] + [ANY_SPEC] * len(arrays),
        [pltpu.VMEM((width, hidden), BF16)] * 3 + [pltpu.SemaphoreType.DMA((sem_count,))],
        flops=6 * rows * hidden * width,
        moved=6 * width * hidden + 8 * rows * hidden,
    )


def turn_kernel(own_ref, came_ref, middle_ref, upstream_ref, gains_ref, *outs):
    output_ref, back_ref, gain_grad_ref = outs
    total = own_ref[...].astype(F32) + came_ref[...].astype(F32)
    scale = inverse_rms(total)
    normed = total * scale
    gain = gains_ref[3:4, :]
    output_ref[...] = (middle_ref[...] + normed * gain).astype(BF16)
    back, gain_grad = norm_back(normed, scale, gain, upstream_ref[...].astype(F32))
    back_ref[...] = back.astype(BF16)
    gain_grad_ref[...] = gain_grad


def turn(sums, middle, upstream, gains):
    rows, width = middle.shape
    return call(
        turn_kernel,
        [shape_of((rows, width), BF16), shape_of((rows, width), BF16), shape_of((1, width), F32)],
        [VMEM_SPEC] * 3,
        list(sums) + [middle, upstream, gains],
        [VMEM_SPEC] * 5,
        moved=20 * rows * width,
    )


def ffn_back_kernel(
    wheres, counts, place_ref, back_ref, gate_slope_ref, up_slope_ref, *refs
):
    parts, bases, refs = take_parts(wheres, counts, refs)
    d_gate_ref, d_up_ref, out_ref, gate_w, up_w, down_w, sems = refs
    seq = place_ref[0]
    copies = start_placing(wheres[2], parts[2], down_w, sems, bases[2], seq)
    later = start_placing(wheres[0], parts[0], gate_w, sems, bases[0], seq)
    later += start_placing(wheres[1], parts[1], up_w, sems, bases[1], seq)
    wait_all(copies)
    back = back_ref[...]
    for start, size in tiles_of(down_w.shape[1], 256):
        lanes = slice(start, start + size)
        d_act = dot(back, down_w[:, lanes])
        d_gate_ref[:, lanes] = (d_act * gate_slope_ref[:, lanes].astype(F32)).astype(BF16)
        d_up_ref[:, lanes] = (d_act * up_slope_ref[:, lanes].astype(F32)).astype(BF16)
    wait_all(later)
    for start, size in tiles_of(gate_w.shape[0], 384):
        lanes = slice(start, start + size)
        total = dot_t(d_gate_ref[...], gate_w[lanes, :])
        out_ref[:, lanes] = (total + dot_t(d_up_ref[...], up_w[lanes, :])).astype(BF16)


def ffn_back(place, back, slopes, weights):
    rows, width = back.shape
    hidden = weights[0].width
    wheres, counts, arrays, sem_count = parts_of(weights)
    return call(
        functools.partial(ffn_back_kernel, wheres, counts),
        [shape_of((rows, hidden), BF16)] * 2 + [shape_of((rows, width), BF16)],
        [VMEM_SPEC] * 3,
        [place, back] + list(slopes) + arrays,
        [SMEM_SPEC] + [VMEM_SPEC] * 3 + [ANY_SPEC] * len(arrays),
        [pltpu.VMEM((width, hidden), BF16)] * 3 + [pltpu.SemaphoreType.DMA((sem_count,))],
        flops=6 * rows * hidden * width,
        moved=6 * width * hidden + 12 * rows * hidden,
    )


def ffn_back_and_grad_kernel(in_counts, out_count, back_kernel, grad_kernel, place_ref, *refs):
    back_ins, refs = refs[: in_counts[0]], refs[in_counts[0] :]
    grad_ins, refs = refs[: in_counts[1]], refs[in_counts[1] :]
    back_outs, refs = refs[:3], refs[3:]
    grad_outs, refs = refs[:out_count], refs[out_count:]
    back_kernel(place_ref, *back_ins, *back_outs, *refs[:4])
    grad_kernel(place_ref, *grad_ins, *grad_outs, *refs[4:])


def ffn_back_and_grad(place, back, slopes, weights, lefts, rights):
    rows, width = back.shape
    hidden = weights[0].width
    wheres, counts, arrays, sem_count = parts_of(weights)
    count = lax.axis_size("seq")
    cuts = cut_shapes(width, hidden, count)
    all_rows = sum(piece.shape[0] for piece in lefts)
    grad_ins = list(lefts) + list(rights)
    back_ins = [back] + list(slopes) + arrays
    outs = call(
        functools.partial(
            ffn_back_and_grad_kernel,
            (len(back_ins), len(grad_ins)),
            len(cuts),
            functools.partial(ffn_back_kernel, wheres, counts),
            functools.partial(weight_grad_kernel, len(lefts), (len(rights),), len(cuts)),
        ),
        [shape_of((rows, hidden), BF16)] * 2 + [shape_of((rows, width), BF16)] + cuts,
        [VMEM_SPEC] * 3 + [ANY_SPEC] * len(cuts),
        [place] + back_ins + grad_ins,
        [SMEM_SPEC] + [VMEM_SPEC] * 3 + [ANY_SPEC] * (len(arrays) + len(grad_ins)),
        [pltpu.VMEM((width, hidden), BF16)] * 3
        + [pltpu.SemaphoreType.DMA((sem_count,))]
        + weight_grad_scratch(all_rows, width, hidden, len(lefts), [len(rights)], count),
        flops=2 * all_rows * width * hidden + 6 * rows * width * hidden,
        moved=8 * width * hidden,
    )
    return outs[0], outs[1], outs[2], outs[3:]


def weight_grad_scratch(rows, height, width, left_count, right_counts, count):
    sides, pieces = len(right_counts), sum(right_counts)
    tiles = len(tiles_of(width, 512))
    return [
        pltpu.VMEM((rows, height), BF16),
        pltpu.VMEM((sides, rows, width), BF16),
        pltpu.VMEM((sides, height, width), BF16),
        pltpu.SemaphoreType.DMA((left_count + tiles * pieces,)),
        pltpu.SemaphoreType.DMA((sides, count)),
    ]


def weight_grad_kernel(left_count, right_counts, out_count, place_ref, *refs):
    lefts, refs = refs[:left_count], refs[left_count:]
    rights = []
    for count in right_counts:
        rights.append(refs[:count])
        refs = refs[count:]
    outs, (left, right, whole, sems, out_sems) = refs[:-5], refs[-5:]
    number = 0

    def fetch(pieces, dest, *lanes):
        nonlocal number
        copies, start = [], 0
        for piece in pieces:
            rows = piece.shape[0]
            source = piece.at[:, lanes[0]] if lanes else piece
            target = dest.at[(pl.ds(start, rows),) + lanes]
            copies.append(pltpu.make_async_copy(source, target, sems.at[number]))
            number += 1
            start += rows
        for copy in copies:
            copy.start()
        return copies

    tiles = tiles_of(whole.shape[-1], 512)
    first = fetch(lefts, left)
    waits = [
        [fetch(pieces, right.at[index], pl.ds(lane, size)) for lane, size in tiles]
        for index, pieces in enumerate(rights)
    ]
    wait_all(first)
    cuts = []
    for index, pieces in enumerate(rights):
        for copies, (lane, size) in zip(waits[index], tiles):
            wait_all(copies)
            lanes = slice(lane, lane + size)
            whole[index, :, lanes] = dot_tn(left[...], right[index, :, lanes]).astype(BF16)
        cuts += start_cutting(
            whole.at[index],
            outs[index * out_count : (index + 1) * out_count],
            out_sems.at[index],
            0,
            place_ref[0],
        )
    wait_all(cuts)


def weight_grad(place, lefts, *rights):
    height, width = lefts[0].shape[1], rights[0][0].shape[1]
    rows = sum(piece.shape[0] for piece in lefts)
    count = lax.axis_size("seq")
    cuts = cut_shapes(height, width, count)
    pieces = [piece for side in rights for piece in side]
    sides = [len(side) for side in rights]
    outs = call(
        functools.partial(
            weight_grad_kernel, len(lefts), tuple(len(side) for side in rights), len(cuts)
        ),
        cuts * len(rights),
        [ANY_SPEC] * (len(cuts) * len(rights)),
        [place] + list(lefts) + pieces,
        [SMEM_SPEC] + [ANY_SPEC] * (len(lefts) + len(pieces)),
        weight_grad_scratch(rows, height, width, len(lefts), sides, count),
        flops=2 * rows * height * width * len(rights),
        moved=2 * (rows * (height + width) + height * width) * len(rights),
    )
    return [outs[start : start + len(cuts)] for start in range(0, len(outs), len(cuts))]


def attend_back_kernel(
    where,
    ref_count,
    head_count,
    place_ref,
    own_ref,
    came_ref,
    middle_ref,
    upstream_ref,
    attn_out_ref,
    gains_ref,
    query_ref,
    keys_ref,
    probs_ref,
    *refs,
):
    parts, refs = refs[:ref_count], refs[ref_count:]
    d_middle_ref, d_attn_ref, d_rotated_ref, far_halo_ref, back_halo_ref, near_ref, rows_ref = refs[:7]
    weights, d_keys, sems = refs[7:]
    rows, width = middle_ref.shape
    head_dim = keys_ref.shape[1] // 2
    heads_width = head_count * head_dim
    score_scale = head_dim**-0.5
    out_start = parts[0].shape[-1] - heads_width
    copies = start_placing(where, parts, weights, sems, 0, place_ref[0], out_start, heads_width)
    total = own_ref[...].astype(F32) + came_ref[...].astype(F32)
    middle = middle_ref[...]
    scale = inverse_rms(middle)
    back, grad_fn = norm_back(middle * scale, scale, gains_ref[2:3, :], total)
    d_middle = upstream_ref[...].astype(F32) + back
    d_middle_ref[...] = d_middle
    attn_out = attn_out_ref[...]
    scale = inverse_rms(attn_out)
    d_attn_out, grad_ap = norm_back(attn_out * scale, scale, gains_ref[1:2, :], d_middle)
    row = iota((8, width), 0)
    rows_ref[...] = jnp.where(row == 1, grad_ap, 0.0) + jnp.where(row == 2, grad_fn, 0.0)
    d_attn_low = d_attn_out.astype(BF16)
    d_attn_ref[...] = d_attn_low
    wait_all(copies)
    for head in range(head_count):
        lanes = slice(head * head_dim, (head + 1) * head_dim)
        d_attended = dot(d_attn_low, weights[:, lanes]).astype(BF16)
        probs_low = probs_ref[head * rows : (head + 1) * rows, :]
        probs = probs_low.astype(F32)
        d_probs = dot_t(d_attended, keys_ref[:, head_dim:])
        delta = jnp.sum(probs * d_probs, axis=-1, keepdims=True)
        d_scores = (probs * (d_probs - delta) * score_scale).astype(BF16)
        d_rotated_ref[:, lanes] = dot(d_scores, keys_ref[:, :head_dim])
        d_key = dot_tn(d_scores, query_ref[:, lanes])
        d_value = dot_tn(probs_low, d_attended)
        if head == 0:
            d_keys[:, :head_dim] = d_key
            d_keys[:, head_dim:] = d_value
        else:
            d_keys[:, :head_dim] += d_key
            d_keys[:, head_dim:] += d_value
    far_halo_ref[...] = d_keys[:rows, :].astype(BF16)
    back_halo_ref[...] = d_keys[rows : 2 * rows, :].astype(BF16)
    near_ref[...] = d_keys[2 * rows :, :]


def attend_back(place, sums, saved, parts, head_count):
    middle, upstream, attn_out, gains, query, keys, probs = saved
    rows, width = middle.shape
    head_dim = keys.shape[1] // 2
    heads_width = head_count * head_dim
    outs = [
        shape_of((rows, width), F32),
        shape_of((rows, width), BF16),
        shape_of((rows, heads_width), F32),
        shape_of((rows, 2 * head_dim), BF16),
        shape_of((rows, 2 * head_dim), BF16),
        shape_of((rows, 2 * head_dim), F32),
        shape_of((8, width), F32),
    ]
    ins = [place] + list(sums) + list(saved) + parts.arrays
    return call(
        functools.partial(attend_back_kernel, parts.where, len(parts.arrays), head_count),
        outs,
        [VMEM_SPEC] * 7,
        ins,
        [SMEM_SPEC] + [VMEM_SPEC] * 9 + [ANY_SPEC] * len(parts.arrays),
        [
            pltpu.VMEM((width, heads_width), BF16),
            pltpu.VMEM((3 * rows, 2 * head_dim), F32),
            pltpu.SemaphoreType.DMA((slots(parts.where),)),
        ],
        flops=2 * rows * width * heads_width + 30 * rows * rows * heads_width,
        moved=2 * width * heads_width + 24 * rows * width,
    )


def heads_kernel(
    where,
    ref_count,
    out_count,
    head_count,
    place_ref,
    d_attn_ref,
    attended_ref,
    attn_in_ref,
    d_rotated_ref,
    query_lin_ref,
    small_gains_ref,
    cos_ref,
    sin_ref,
    *refs,
):
    parts, refs = refs[:ref_count], refs[ref_count:]
    grads, refs = refs[:out_count], refs[out_count:]
    d_in_ref, query_gain_ref, weights, whole, d_query, sems, out_sems = refs
    rows, width = attn_in_ref.shape
    heads_width = attended_ref.shape[1]
    head_dim = heads_width // head_count
    seq = place_ref[0]
    copies = start_placing(where, parts, weights, sems, 0, seq, 0, heads_width)
    for start, size in tiles_of(heads_width, 512):
        lanes = slice(start, start + size)
        whole[0, :, lanes] = dot_tn(d_attn_ref[...], attended_ref[:, lanes]).astype(BF16)
    cuts = start_cutting(whole.at[0], grads, out_sems.at[0], 0, seq, 0)
    cosine, sine = cos_ref[2 * rows :, :], sin_ref[2 * rows :, :]
    gain_q = small_gains_ref[4:5, :]
    query_gain = jnp.zeros((1, head_dim), F32)
    for head in range(head_count):
        lanes = slice(head * head_dim, (head + 1) * head_dim)
        query_lin = query_lin_ref[:, lanes]
        scale = inverse_rms(query_lin)
        d_normed = rotate(d_rotated_ref[:, lanes], cosine, -sine)
        back, gain_grad = norm_back(query_lin * scale, scale, gain_q, d_normed)
        query_gain = query_gain + gain_grad
        d_query[:, lanes] = back.astype(BF16)
    query_gain_ref[...] = query_gain
    for start, size in tiles_of(heads_width, 512):
        lanes = slice(start, start + size)
        whole[1, :, lanes] = dot_tn(attn_in_ref[...], d_query[:, lanes]).astype(BF16)
    cuts += start_cutting(whole.at[1], grads, out_sems.at[1], 0, seq, 1)
    wait_all(copies)
    for start, size in tiles_of(width, 384):
        lanes = slice(start, start + size)
        d_in_ref[:, lanes] = dot_t(d_query[...], weights[lanes, :])
    wait_all(cuts)


def heads_back(place, ins, parts, head_count):
    attn_in, attended, small_gains = ins[2], ins[1], ins[5]
    rows, width = attn_in.shape
    heads_width, head_dim = attended.shape[1], small_gains.shape[1]
    count = lax.axis_size("seq")
    cuts = [
        shape_of((2,) + part.shape, BF16) for part in cut_shapes(width, heads_width, count)
    ]
    return call(
        functools.partial(
            heads_kernel, parts.where, len(parts.arrays), len(cuts), head_count
        ),
        cuts + [shape_of((rows, width), F32), shape_of((1, head_dim), F32)],
        [ANY_SPEC] * len(cuts) + [VMEM_SPEC] * 2,
        [place] + list(ins) + parts.arrays,
        [SMEM_SPEC] + [VMEM_SPEC] * 8 + [ANY_SPEC] * len(parts.arrays),
        [
            pltpu.VMEM((width, heads_width), BF16),
            pltpu.VMEM((2, width, heads_width), BF16),
            pltpu.VMEM((rows, heads_width), BF16),
            pltpu.SemaphoreType.DMA((slots(parts.where),)),
            pltpu.SemaphoreType.DMA((2, count)),
        ],
        flops=6 * rows * width * heads_width,
        moved=8 * width * heads_width,
    )


def finish_kernel(
    where,
    ref_count,
    out_count,
    narrow_rows,
    wide_rows,
    place_ref,
    near_ref,
    back_ref,
    far_ref,
    key_lin_ref,
    small_gains_ref,
    gains_ref,
    cos_ref,
    sin_ref,
    attn_in_ref,
    tokens_ref,
    d_middle_ref,
    d_in_ref,
    rows_ref,
    ffn_post_ref,
    query_gain_ref,
    *refs,
):
    parts, refs = refs[:ref_count], refs[ref_count:]
    grads, (input_grad_ref, first_w, whole, d_low, sems) = refs[:out_count], refs[out_count:]
    rows, width = tokens_ref.shape
    head_dim = key_lin_ref.shape[1]
    seq = place_ref[0]
    heads_width = (parts[0].shape[-1] - 2 * head_dim - LANES) // 2
    copies = start_placing(where, parts, first_w, sems, 0, seq, heads_width, 2 * head_dim)
    d_keys = near_ref[...] + back_ref[...].astype(F32) + far_ref[...].astype(F32)
    key_lin = key_lin_ref[...]
    scale = inverse_rms(key_lin)
    d_normed = rotate(d_keys[:, :head_dim], cos_ref[2 * rows :, :], -sin_ref[2 * rows :, :])
    back, key_gain = norm_back(key_lin * scale, scale, small_gains_ref[5:6, :], d_normed)
    d_low[:, :head_dim] = back.astype(BF16)
    d_low[:, head_dim:] = d_keys[:, head_dim:].astype(BF16)
    whole[:, : 2 * head_dim] = dot_tn(attn_in_ref[...], d_low[...]).astype(BF16)
    wait_all(copies)
    d_attn_in = d_in_ref[...] + dot_t(d_low[...], first_w[...])
    inputs = tokens_ref[...].astype(F32)
    scale = inverse_rms(inputs)
    back, grad_an = norm_back(inputs * scale, scale, gains_ref[0:1, :], d_attn_in)
    input_grad_ref[...] = d_middle_ref[...] + back
    row = iota((8, width), 0)
    gain_rows = rows_ref[...] + jnp.where(row == 0, grad_an, 0.0)
    gain_rows = gain_rows + jnp.where(row == 3, ffn_post_ref[...], 0.0)
    small_row = iota((8, head_dim), 0)
    small = jnp.where(small_row == 4, query_gain_ref[...], 0.0)
    small = small + jnp.where(small_row == 5, key_gain, 0.0)
    spread = spread_matrix(head_dim, width, narrow_rows, wide_rows)
    gain_rows = gain_rows + dot(small.astype(BF16), spread)
    pick = unit((8, LANES), iota((8, LANES), 0) == iota((8, LANES), 1))
    whole[:, 2 * head_dim :] = dot_tn(gain_rows.astype(BF16), pick).astype(BF16)
    wait_all(start_cutting(whole, grads, sems, slots(where), seq))


def finish(place, ins, parts, narrow_rows, wide_rows):
    tokens, key_lin = ins[9], ins[3]
    rows, width = tokens.shape
    head_dim = key_lin.shape[1]
    count = lax.axis_size("seq")
    pack = 2 * head_dim + LANES
    cuts = cut_shapes(width, pack, count)
    return call(
        functools.partial(
            finish_kernel, parts.where, len(parts.arrays), len(cuts), narrow_rows, wide_rows
        ),
        cuts + [shape_of((rows, width), F32)],
        [ANY_SPEC] * len(cuts) + [VMEM_SPEC],
        [place] + list(ins) + parts.arrays,
        [SMEM_SPEC] + [VMEM_SPEC] * len(ins) + [ANY_SPEC] * len(parts.arrays),
        [
            pltpu.VMEM((width, 2 * head_dim), BF16),
            pltpu.VMEM((width, pack), BF16),
            pltpu.VMEM((rows, 2 * head_dim), BF16),
            pltpu.SemaphoreType.DMA((slots(parts.where) + count,)),
        ],
        flops=8 * rows * width * head_dim,
        moved=4 * width * pack + 20 * rows * width,
    )


def layout(lengths, counts, first_slot, row_count):
    starts = jnp.cumsum(lengths) - lengths
    slot_index = first_slot + jnp.arange(row_count, dtype=jnp.int32)
    member = (slot_index[:, None] >= starts[None, :]).astype(jnp.int32)
    document = jnp.sum(member, axis=1) - 1
    onehot = (document[:, None] == jnp.arange(lengths.shape[0], dtype=jnp.int32)[None, :]).astype(
        jnp.int32
    )
    position = slot_index - jnp.sum(onehot * starts[None, :], axis=1)
    padded = jnp.sum(onehot * (lengths - counts)[None, :], axis=1)
    return (position, padded)


def on_device(
    tokens,
    cotangent,
    doc_lengths,
    true_counts,
    w_query,
    w_key,
    w_value,
    w_out,
    w_gate,
    w_up,
    w_down,
    attn_norm_gain,
    query_gain,
    key_gain,
    attn_post_gain,
    ffn_norm_gain,
    ffn_post_gain,
):
    row_count = tokens.shape[1]
    head_dim = w_key.shape[1]
    heads_width = w_query.shape[1]
    head_count = heads_width // head_dim
    seq_index, plane_index = lax.axis_index("seq"), lax.axis_index("fsdp")
    place = jnp.stack([seq_index, plane_index]).astype(jnp.int32)
    inputs, upstream = tokens[0], cotangent[0]
    wide_rows, narrow_rows = attn_norm_gain.shape[0], query_gain.shape[0]

    planes_count = lax.axis_size("fsdp")
    far_masks = [mask for mask in seq_masks() if mask > 2]

    def swap_far(parts):
        parts = dict(parts)
        for mask in far_masks:
            parts.update({rel ^ mask: swap(part, "seq", mask) for rel, part in parts.items()})
        return parts

    def swap_both(parts, rel):
        if rel not in far_masks:
            return swap(parts[rel], "seq", 2)
        split = (parts[rel].shape[-2] // 2 + 15) // 16 * 16
        top = swap(parts[rel][..., :split, :], "seq", 2)
        bottom = swap(parts[2][..., split:, :], "seq", rel)
        return jnp.concatenate([top, bottom], axis=-2)

    pack = pack_attn(
        w_query,
        w_key,
        w_value,
        w_out,
        [attn_norm_gain, attn_post_gain, ffn_norm_gain, ffn_post_gain],
        [query_gain, key_gain],
    )
    gate_up_own = jnp.stack([w_gate, w_up])
    pack, gate_up_own, inputs, w_down = sync((pack, gate_up_own, inputs, w_down))

    planes = [pack] + [shift(pack, "fsdp", steps) for steps in range(1, planes_count)]
    gate_up_far = swap_far({0: gate_up_own})
    gate_up_half = gate_up_far | {2: swap(gate_up_own, "seq", 2)}
    first_slot = seq_index * row_count
    position, padded = layout(
        doc_lengths[0], true_counts[0], first_slot - WINDOW, row_count + WINDOW
    )
    frequency = ROPE_BASE ** (-2.0 * jnp.arange(head_dim // 2, dtype=F32) / head_dim)
    angles = position.astype(F32)[:, None] * frequency
    cosine, sine = jnp.cos(angles), jnp.sin(angles)
    reach = jnp.clip(position[WINDOW:] - padded[WINDOW:], 0, WINDOW - 1)
    lowest = (WINDOW + jnp.arange(row_count, dtype=jnp.int32) - reach)[:, None]
    state = (planes, gate_up_half, cosine, sine, lowest, inputs, w_down)
    planes, gate_up_half, cosine, sine, lowest, inputs, w_down = sync(state)
    pack_rows, gate_up_half, inputs, w_down = sync(
        (place_planes(planes, place), gate_up_half, inputs, w_down)
    )

    rows_far = swap_far({0: pack_rows})
    rows_half = rows_far | {2: swap(pack_rows, "seq", 2)}
    behind = from_behind(inputs, 1)
    gate_up_rels, gate_up_core = core_stack(gate_up_half)
    state = (rows_half, behind, gate_up_half, gate_up_core, w_down)
    rows_half, behind, gate_up_half, gate_up_core, w_down = sync(state)
    rows_rest = {rel ^ 2: swap_both(rows_half, rel) for rel in rows_far if rel}
    half_rels, half_core = core_stack(rows_half)
    tokens3 = [inputs, behind, from_behind(behind, 1)]
    state = (rows_half, rows_rest, half_core, tokens3, gate_up_half, w_down)
    rows_half, rows_rest, half_core, tokens3, gate_up_half, w_down = sync(state)
    rest_rels, rest_core = core_stack(rows_rest)
    rest_core, gate_up_half, w_down = sync((rest_core, gate_up_half, w_down))
    parts = all_parts(rows_half | rows_rest, [(half_rels, half_core), (rest_rels, rest_core)])

    gate_up_rest = {rel ^ 2: swap_both(gate_up_half, rel) for rel in gate_up_far if rel}
    (
        attn_in,
        query_lin,
        key_lin,
        query,
        keys,
        probs,
        attended,
        gains,
        small_gains,
        attn_out,
        middle,
        ffn_in,
    ) = attend(
        place,
        tokens3,
        cosine,
        sine,
        lowest,
        parts,
        head_count,
        head_dim,
        narrow_rows,
        wide_rows,
    )
    ffn_in, gate_up_rest, w_down = sync((ffn_in, gate_up_rest, w_down))

    rest_rels, rest_core = core_stack(gate_up_rest)
    down_far = swap_far({0: w_down})
    down_half = down_far | {2: swap(w_down, "seq", 2)}
    state = (shift(ffn_in, "fsdp", 1), rest_core, down_half)
    block, rest_core, down_half = sync(state)
    cores = [(gate_up_rels, gate_up_core), (rest_rels, rest_core)]
    weights = [all_parts(gate_up_half | gate_up_rest, cores, index) for index in range(2)]
    blocks = [ffn_in, block]
    down_rest = {rel ^ 2: swap_both(down_half, rel) for rel in down_far if rel}
    half_rels, half_core = core_stack(down_half)
    act, gate_slope, up_slope = gate_up(place, blocks[1], weights)
    state = (shift(blocks[1], "fsdp", 1), act, down_rest, half_core)
    block, act, down_rest, half_core = sync(state)
    blocks.append(block)
    rest_rels, rest_core = core_stack(down_rest)
    act, rest_core = sync((act, rest_core))
    weights.append(
        all_parts(down_half | down_rest, [(half_rels, half_core), (rest_rels, rest_core)])
    )
    acts, slopes = {1: act}, {1: (gate_slope, up_slope)}
    partials = {1: sync(down(place, act, weights[2:]))}
    carried = None
    for step in range(2, planes_count + 1):
        state = {}
        if step < planes_count - 1:
            state["block"] = shift(blocks[step], "fsdp", 1)
        leaving = partials[step - 1]
        if carried is not None:
            leaving = add_rounded(leaving, carried)
        index = step % planes_count
        acts[index], gate_slope, up_slope, partials[index] = ffn(place, blocks[index], weights)
        slopes[index] = (gate_slope, up_slope)
        state["carried"] = shift(leaving, "fsdp", 1)
        state, partials = sync((state, partials))
        carried = state["carried"]
        if "block" in state:
            blocks.append(state["block"])
    output, d_ffn_low, grad_fp = turn([partials[0], carried], middle, upstream, gains)

    backs, partials, d_gates, d_ups = [sync(d_ffn_low)], {}, [], []
    carried, down_pair, down_sent = None, None, None
    all_acts = [acts[index] for index in range(planes_count)]
    for step in range(planes_count):
        state = {}
        if step < planes_count - 2:
            state["block"] = shift(backs[step], "fsdp", 1)
        if step == planes_count - 3:
            state["last"] = shift(backs[0], "fsdp", -1)
        if step >= 2:
            leaving = partials[step - 1]
            if carried is not None:
                leaving = add_rounded(leaving, carried)
            state["carried"] = shift(leaving, "fsdp", 1)
        if step == planes_count - 2:
            d_gate, d_up, partials[step], down_pair = ffn_back_and_grad(
                place, backs[step], slopes[step], weights, backs, all_acts
            )
        else:
            d_gate, d_up, partials[step] = ffn_back(place, backs[step], slopes[step], weights)
        if step == planes_count - 1:
            state["down"] = cores_send(down_pair)
        d_gates.append(d_gate)
        d_ups.append(d_up)
        state, partials, d_gates, d_ups, down_pair = sync(
            (state, partials, d_gates, d_ups, down_pair)
        )
        carried = state.get("carried", carried)
        backs += [state[name] for name in ("block", "last") if name in state]
        down_sent = state.get("down")
    carried = shift(add_rounded(partials[planes_count - 1], carried), "fsdp", 1)
    down_part = add_rounded(*down_sent)
    down_terms = [down_part[0]] + straight(down_part, 1, 2)
    gate_pair, up_pair = weight_grad(place, blocks, d_gates, d_ups)
    carried, gate_pair, up_pair, down_terms, down_part = sync(
        (carried, gate_pair, up_pair, down_terms, down_part)
    )

    gate_sent, up_sent = cores_send(gate_pair), cores_send(up_pair)
    down_terms += straight(down_part, *range(3, down_part.shape[0]))
    saved = (middle, upstream, attn_out, gains, query, keys, probs)
    d_middle, d_attn, d_rotated, far_halo, back_halo, near, gain_rows = attend_back(
        place, [partials[0], carried], saved, parts, head_count
    )
    state = (far_halo, back_halo, d_attn, d_rotated, gate_sent, up_sent, down_terms)
    far_halo, back_halo, d_attn, d_rotated, gate_sent, up_sent, down_terms = sync(state)
    halos = [from_behind(back_halo, -1), from_behind(far_halo, -2)]
    gate_part, up_part = add_rounded(*gate_sent), add_rounded(*up_sent)
    quarter = up_part.shape[0] // 2
    gate_columns = gate_part.reshape((-1, 2) + gate_part.shape[1:])
    gate_second = far_step(gate_columns[:, 1])
    up_second = across_step(up_part[quarter:])
    ins = [d_attn, attended, attn_in, d_rotated, query_lin, small_gains, cosine, sine]
    *head_grads, d_in, query_gain_grad = heads_back(place, ins, parts, head_count)
    state = (halos, head_grads, gate_columns, gate_second, up_part, up_second)
    halos, head_grads, gate_columns, gate_second, up_part, up_second = sync(state)
    head_sent = cores_send(head_grads)
    gate_first = far_step(gate_columns[:, 0])
    up_first = across_step(up_part[:quarter])
    ins = [
        near,
        *halos,
        key_lin,
        small_gains,
        gains,
        cosine,
        sine,
        attn_in,
        inputs,
        d_middle,
        d_in,
        gain_rows,
        grad_fp,
        query_gain_grad,
    ]
    *last_grads, input_grad = finish(place, ins, parts, narrow_rows, wide_rows)
    state = (last_grads, head_sent, gate_first, gate_second, up_first, up_second)
    last_grads, head_sent, gate_first, gate_second, up_first, up_second = sync(state)
    last_sent = cores_send(last_grads)
    head_part = add_rounded(*head_sent)
    out_sides = far_step(head_part[0])
    query_sides = across_step(head_part[1])
    gate_came = swap(add_rounded(*gate_second)[0], "seq", 2)
    up_sides = far_step(jnp.concatenate([add_rounded(*up_first), add_rounded(*up_second)], axis=0))
    state = (last_sent, out_sides, query_sides, gate_came, gate_first, up_sides)
    last_sent, out_sides, query_sides, gate_came, gate_first, up_sides = sync(state)
    out_part = add_rounded(*out_sides)
    out_came = swap(out_part[1], "seq", 2)
    query_sides = far_step(add_rounded(*query_sides))
    last_part = add_rounded(*last_sent)
    last_terms = [last_part[0]] + straight(last_part, *range(1, last_part.shape[0]))
    state = (out_part, out_came, query_sides, last_terms)
    out_part, out_came, query_sides, last_terms = sync(state)
    grad_gate = add_up([add_up(gate_first)[0], gate_came])
    grad_up = add_up(up_sides)[0]
    reduced = jnp.concatenate(
        [
            add_rounded(out_part[0], out_came),
            add_rounded(*query_sides)[0],
            add_up(last_terms).astype(BF16),
        ],
        axis=1,
    )
    rows = add_up(planes_send(reduced))
    last_start = 2 * heads_width
    gain_cols = rows[:, last_start + 2 * head_dim :]
    return (
        output[None],
        input_grad[None],
        rows[:, heads_width:last_start],
        rows[:, last_start : last_start + head_dim],
        rows[:, last_start + head_dim : last_start + 2 * head_dim],
        rows[:, :heads_width],
        grad_gate,
        grad_up,
        add_up(down_terms),
        gain_cols[:, 0],
        gain_cols[:narrow_rows, 4],
        gain_cols[:narrow_rows, 5],
        gain_cols[:, 1],
        gain_cols[:, 2],
        gain_cols[:, 3],
    )


def solution(mesh):
    rows = P("fsdp", "seq", None)
    shard, tile, vector = P(("seq", "fsdp"), None), P("seq", "fsdp"), P(("seq", "fsdp"))
    groups = P("fsdp", None)
    return jax.shard_map(
        on_device,
        mesh=mesh,
        in_specs=(rows, rows, groups, groups) + (shard,) * 4 + (tile,) * 3 + (vector,) * 6,
        out_specs=(rows, rows) + (shard,) * 4 + (tile,) * 3 + (vector,) * 6,
        check_vma=False,
    )
```

time: 509 us -> 455 us (0.89)
  the two profiles are of different devices: /device:TPU:9 before, /device:TPU:0 now
where the time goes in v4:
time: 455 us; the launch traced here: 446 us
  waiting for transfers between devices  171 us (38%)
  Pallas kernels  158 us (35%)
  starting transfers between devices  69.3 us (15%)
  other arithmetic  23.3 us (5%)
  local copies, waits for them, and re-layouts  22.4 us (5%)
    pallas_call x17, Pallas kernels, call(): pl.pallas_call(kernel, out_shape=tuple(outs), in_specs=list(in_specs), ou...  158 us
    ppermute x39, waiting for transfers between devices, swap(): lax.ppermute(value, axis, [(source, source ^ mask) for source in range(co...  83.6 us
    ppermute x18, waiting for transfers between devices, shift(): lax.ppermute(value, axis, [(source, (source + steps) % count) for source...  80.1 us
    ppermute x39, starting transfers between devices, swap(): lax.ppermute(value, axis, [(source, source ^ mask) for source in range(co...  44.6 us
    ppermute x18, starting transfers between devices, shift(): lax.ppermute(value, axis, [(source, (source + steps) % count) for source...  19.1 us
    unnamed x130, local copies, waits for them, and re-layouts  10.4 us
    convert_element_type x15, other arithmetic, add_rounded(): return (first.astype(F32) + second.astype(F32)).astype(BF16)  9.4 us
  transfers between devices with their start and end apart: 61, of which 31 were waited for; matrix products, arithmetic and copies ran while one was open for 5% of the time, Pallas kernels for 33%

profile of v4, /device:TPU:0, one launch (start us, length us, event | category | flops | bytes accessed | tf_op | source)
XLA Modules:
  0.0 446.4 jit_solution(9585657696458174868)
XLA Ops:
  4.3 5.0 %collective-permute-start.2 = (bf16[36,2688]{1,0:T(8,128)(2,1)}, bf16[36,2688]{1,0:T(8,128)(2,1)S(1)}, u32[]{:S(2)}, u32[]{:S(2)}) collective-permute-start(bf16[36,2688]{1,0:T(8,128)(2,1)} %shard_map.280.refs_0_), channel_id=1, source_target_pairs={{0,3},{1,0},{2,1},{3,2},{4,7},{5,4},{6,5},{7,6},{8,11},{9,8},{10,9... | collective-permute-start | bytes 580616 | tf_op jit(solution)/shard_map/ppermute | solution.py:38
  16.9 10.9 %collective-permute-done.1.refs_2_ = bf16[36,2688]{1,0:T(8,128)(2,1)S(1)} collective-permute-done((bf16[36,2688]{1,0:T(8,128)(2,1)}, bf16[36,2688]{1,0:T(8,128)(2,1)S(1)}, u32[]{:S(2)}, u32[]{:S(2)}) %collective-permute-start.1) | collective-permute-done | bytes 193568 | tf_op jit(solution)/shard_map/ppermute | solution.py:38
  27.8 6.2 %collective-permute-done.4.refs_2_.refs_8_.refs_5_.refs_11_ = bf16[2,144,1728]{2,1,0:T(8,128)(2,1)S(1)} collective-permute-done((bf16[2,144,1728]{2,1,0:T(8,128)(2,1)S(1)}, bf16[2,144,1728]{2,1,0:T(8,128)(2,1)S(1)}, u32[]{:S(2)}, u32[]{:S(2)}) %collective-permute-start.4) | collective-permute-done | bytes 995360 | tf_op jit(solution)/shard_map/ppermute | solution.py:33
  45.3 13.6 %collective-permute-done.6.refs_2_ = bf16[144,2688]{1,0:T(8,128)(2,1)S(1)} collective-permute-done((bf16[144,2688]{1,0:T(8,128)(2,1)S(1)}, bf16[144,2688]{1,0:T(8,128)(2,1)S(1)}, u32[]{:S(2)}, u32[]{:S(2)}) %collective-permute-start.6) | collective-permute-done | bytes 774176 | tf_op jit(solution)/shard_map/ppermute | solution.py:33
  72.3 6.9 %collective-permute-done.10 = bf16[64,2688]{1,0:T(8,128)(2,1)S(1)} collective-permute-done((bf16[64,2688]{1,0:T(8,128)(2,1)S(1)}, bf16[64,2688]{1,0:T(8,128)(2,1)S(1)}, u32[]{:S(2)}, u32[]{:S(2)}) %collective-permute-start.10) | collective-permute-done | bytes 344096 | tf_op jit(solution)/shard_map/ppermute | solution.py:33
  79.9 5.3 %collective-permute-start.13 = (bf16[1,144,2688]{2,1,0:T(8,128)(2,1)S(1)}, bf16[1,144,2688]{2,1,0:T(8,128)(2,1)S(1)}, u32[]{:S(2)}, u32[]{:S(2)}) collective-permute-start(bf16[1,144,2688]{2,1,0:T(8,128)(2,1)S(1)} %bitcast.112), channel_id=1, source_target_pairs={{0,4},{4,0},{8,12},{12,8},{16,20},{20,16},{24,28},{28,24},{1,5},{5... | collective-permute-start | bytes 2322440 | tf_op jit(solution)/shard_map/ppermute | solution.py:33
  94.0 12.0 %shard_map.282 = (bf16[256,1152]{1,0:T(8,128)(2,1)}, f32[256,1024]{1,0:T(8,128)}, f32[256,256]{1,0:T(8,128)}, bf16[256,1024]{1,0:T(8,128)(2,1)}, bf16[768,512]{1...) custom-call(s32[2]{0:T(128)} %pad_add_fusion.place_ref, ...), custom_call_target="tpu_custom_call" | custom-call | flops 2315255808 | bytes 10911744 | tf_op jit(solution)/shard_map/pallas_call | solution.py:247
  110.9 13.0 %collective-permute-done.19.refs_2_.refs_14_.refs_17_ = bf16[144,1728]{1,0:T(8,128)(2,1)S(1)} collective-permute-done((bf16[144,1728]{1,0:T(8,128)(2,1)S(1)}, bf16[144,1728]{1,0:T(8,128)(2,1)S(1)}, u32[]{:S(2)}, u32[]{:S(2)}) %collective-permute-start.19) | collective-permute-done | bytes 497696 | tf_op jit(solution)/shard_map/ppermute | solution.py:33
  127.3 8.8 %shard_map.283 = (bf16[256,1728]{1,0:T(8,128)(2,1)}, bf16[256,1728]{1,0:T(8,128)(2,1)}, bf16[256,1728]{1,0:T(8,128)(2,1)}) custom-call(s32[2]{0:T(128)} %pad_add_fusion.place_ref, bf16[256,1152]{1,0:T(8,128)(2,1)} %copy-done.33, bf16[2,144,1728]{2,1,0:T(8,128)(2,1)} %copy-done.1, bf16[2,144,1728]{2,1,0:T(8,128)(2,1)} %copy-done.4, ...), custom_call_target="tpu_custom_call" | custom-call | flops 2038431744 | bytes 10616832 | tf_op jit(solution)/shard_map/pallas_call | solution.py:247
  137.2 5.9 %collective-permute-done.20.rows_ref.refs_2_ = bf16[256,1152]{1,0:T(8,128)(2,1)S(1)} collective-permute-done((bf16[256,1152]{1,0:T(8,128)(2,1)S(1)}, bf16[256,1152]{1,0:T(8,128)(2,1)S(1)}, u32[]{:S(2)}, u32[]{:S(2)}) %collective-permute-start.20) | collective-permute-done | bytes 589856 | tf_op jit(solution)/shard_map/ppermute | solution.py:38
  145.9 5.8 %shard_map.284 = bf16[256,1152]{1,0:T(8,128)(2,1)} custom-call(s32[2]{0:T(128)} %pad_add_fusion.place_ref, bf16[256,1728]{1,0:T(8,128)(2,1)} %get-tuple-element.305.act_ref.refs_26_, bf16[144,1728]{1,0:T(8,128)(2,1)} %refs_12_.5, bf16[144,1728]{1,0:T(8,128)(2,1)} %copy-done.9, bf16[144,1728]{1,0:T(8,128)(2,1)} %copy-done.8, bf16[144,1728]{1,0:T(8,128)(2,1)} %copy-done.10, ...), custom_call_target="tpu_custom_call" | custom-call | flops 1019215872 | bytes 4866048 | tf_op jit(solution)/shard_map/pallas_call | solution.py:247
  151.7 9.8 %shard_map.285 = (bf16[256,1728]{1,0:T(8,128)(2,1)}, bf16[256,1728]{1,0:T(8,128)(2,1)}, bf16[256,1728]{1,0:T(8,128)(2,1)}, bf16[256,1152]{1,0:T(8,128)(2,1)}) custom-call(s32[2]{0:T(128)} %pad_add_fusion.place_ref, bf16[256,1152]{1,0:T(8,128)(2,1)} %copy-done.34, bf16[2,144,1728]{2,1,0:T(8,128)(2,1)} %copy-done.1, bf16[2,144,1728]{2,1,0:T(8,128)(2,1)} %copy-done.4, ...), custom_call_target="tpu_custom_call" | custom-call | flops 3057647616 | bytes 15482880 | tf_op jit(solution)/shard_map/pallas_call | solution.py:247
  161.6 11.8 %collective-permute-done.26 = bf16[256,1152]{1,0:T(8,128)(2,1)S(1)} collective-permute-done((bf16[256,1152]{1,0:T(8,128)(2,1)}, bf16[256,1152]{1,0:T(8,128)(2,1)S(1)}, u32[]{:S(2)}, u32[]{:S(2)}) %collective-permute-start.26) | collective-permute-done | bytes 589856 | tf_op jit(solution)/shard_map/ppermute | solution.py:38
  174.6 9.8 %shard_map.286 = (bf16[256,1728]{1,0:T(8,128)(2,1)}, bf16[256,1728]{1,0:T(8,128)(2,1)}, bf16[256,1728]{1,0:T(8,128)(2,1)}, bf16[256,1152]{1,0:T(8,128)(2,1)}) custom-call(s32[2]{0:T(128)} %pad_add_fusion.place_ref, bf16[256,1152]{1,0:T(8,128)(2,1)} %copy-done.35, bf16[2,144,1728]{2,1,0:T(8,128)(2,1)} %copy-done.1, bf16[2,144,1728]{2,1,0:T(8,128)(2,1)} %copy-done.4, ...), custom_call_target="tpu_custom_call" | custom-call | flops 3057647616 | bytes 15482880 | tf_op jit(solution)/shard_map/pallas_call | solution.py:247
  184.4 6.9 %collective-permute-done.27 = bf16[256,1152]{1,0:T(8,128)(2,1)S(1)} collective-permute-done((bf16[256,1152]{1,0:T(8,128)(2,1)S(1)}, bf16[256,1152]{1,0:T(8,128)(2,1)S(1)}, u32[]{:S(2)}, u32[]{:S(2)}) %collective-permute-start.27) | collective-permute-done | bytes 589856 | tf_op jit(solution)/shard_map/ppermute | solution.py:38
  193.0 9.8 %shard_map.287 = (bf16[256,1728]{1,0:T(8,128)(2,1)}, bf16[256,1728]{1,0:T(8,128)(2,1)}, bf16[256,1728]{1,0:T(8,128)(2,1)}, bf16[256,1152]{1,0:T(8,128)(2,1)}) custom-call(s32[2]{0:T(128)} %pad_add_fusion.place_ref, bf16[256,1152]{1,0:T(8,128)(2,1)} %get-tuple-element.291.rows_ref.refs_0_, bf16[2,144,1728]{2,1,0:T(8,128)(2,1)} %copy-done.1, ...), custom_call_target="tpu_custom_call" | custom-call | flops 3057647616 | bytes 15482880 | tf_op jit(solution)/shard_map/pallas_call | solution.py:247
  202.8 6.0 %collective-permute-done.28.came_ref = bf16[256,1152]{1,0:T(8,128)(2,1)S(1)} collective-permute-done((bf16[256,1152]{1,0:T(8,128)(2,1)S(1)}, bf16[256,1152]{1,0:T(8,128)(2,1)S(1)}, u32[]{:S(2)}, u32[]{:S(2)}) %collective-permute-start.28) | collective-permute-done | bytes 589856 | tf_op jit(solution)/shard_map/ppermute | solution.py:38
  216.8 10.2 %shard_map.289 = (bf16[256,1728]{1,0:T(8,128)(2,1)}, bf16[256,1728]{1,0:T(8,128)(2,1)}, bf16[256,1152]{1,0:T(8,128)(2,1)}) custom-call(s32[2]{0:T(128)} %pad_add_fusion.place_ref, bf16[256,1152]{1,0:T(8,128)(2,1)} %get-tuple-element.321.back_ref.refs_21_, bf16[256,1728]{1,0:T(8,128)(2,1)} %get-tuple-element.322.gate_slope_ref, ...), custom_call_target="tpu_custom_call" | custom-call | flops 3057647616 | bytes 17252352 | tf_op jit(solution)/shard_map/pallas_call | solution.py:247
  232.1 10.2 %shard_map.290 = (bf16[256,1728]{1,0:T(8,128)(2,1)}, bf16[256,1728]{1,0:T(8,128)(2,1)}, bf16[256,1152]{1,0:T(8,128)(2,1)}) custom-call(s32[2]{0:T(128)} %pad_add_fusion.place_ref, bf16[256,1152]{1,0:T(8,128)(2,1)} %copy-done.23, bf16[256,1728]{1,0:T(8,128)(2,1)} %get-tuple-element.329.gate_slope_ref, bf16[256,1728]{1,0:T(8,128)(2,1)} %get-tuple-element.330.up_slope_ref, ...), custom_call_target="tpu_custom_call" | custom-call | flops 3057647616 | bytes 17252352 | tf_op jit(solution)/shard_map/pallas_call | solution.py:247
  242.3 11.1 %collective-permute-done.30.refs_0_.refs_23_ = bf16[256,1152]{1,0:T(8,128)(2,1)S(1)} collective-permute-done((bf16[256,1152]{1,0:T(8,128)(2,1)S(1)}, bf16[256,1152]{1,0:T(8,128)(2,1)S(1)}, u32[]{:S(2)}, u32[]{:S(2)}) %collective-permute-start.30) | collective-permute-done | bytes 589856 | tf_op jit(solution)/shard_map/ppermute | solution.py:38
  254.3 19.1 %shard_map.291 = (bf16[256,1728]{1,0:T(8,128)(2,1)}, bf16[256,1728]{1,0:T(8,128)(2,1)}, bf16[256,1152]{1,0:T(8,128)(2,1)}, bf16[4,144,1728]{2,1,0:T(8,128)(2,1)}, bf16[4,144,1728]{2,1,0:T(8,128)(2,1)}) custom-call(s32[2]{0:T(128)} %pad_add_fusion.place_ref, bf16[256,1152]{1,0:T(8,128)(2,1)} %copy-done.24, bf16[256,1728]{1,0:T(8,128)(2,1)} %get-tuple-element.339.refs_1_, ...), custom_call_target="tpu_custom_call" | custom-call | flops 7134511104 | bytes 15925248 | tf_op jit(solution)/shard_map/pallas_call | solution.py:247
  274.7 10.4 %shard_map.292 = (bf16[256,1728]{1,0:T(8,128)(2,1)}, bf16[256,1728]{1,0:T(8,128)(2,1)}, bf16[256,1152]{1,0:T(8,128)(2,1)}) custom-call(s32[2]{0:T(128)} %pad_add_fusion.place_ref, bf16[256,1152]{1,0:T(8,128)(2,1)} %copy-done.22, bf16[256,1728]{1,0:T(8,128)(2,1)} %get-tuple-element.359.gate_slope_ref, bf16[256,1728]{1,0:T(8,128)(2,1)} %get-tuple-element.360.up_slope_ref, ...), custom_call_target="tpu_custom_call" | custom-call | flops 3057647616 | bytes 17252352 | tf_op jit(solution)/shard_map/pallas_call | solution.py:247
  285.1 7.1 %collective-permute-done.33 = bf16[256,1152]{1,0:T(8,128)(2,1)S(1)} collective-permute-done((bf16[256,1152]{1,0:T(8,128)(2,1)S(1)}, bf16[256,1152]{1,0:T(8,128)(2,1)S(1)}, u32[]{:S(2)}, u32[]{:S(2)}) %collective-permute-start.33) | collective-permute-done | bytes 589856 | tf_op jit(solution)/shard_map/ppermute | solution.py:38
  296.3 16.4 %shard_map.293 = (bf16[4,144,1728]{2,1,0:T(8,128)(2,1)}, bf16[4,144,1728]{2,1,0:T(8,128)(2,1)}, bf16[4,144,1728]{2,1,0:T(8,128)(2,1)}, bf16[4,144,1728]{2,1,0:T(8,128)(2,1)}) custom-call(s32[2]{0:T(128)} %pad_add_fusion.place_ref, bf16[256,1152]{1,0:T(8,128)(2,1)} %get-tuple-element.291.rows_ref.refs_0_, bf16[256,1152]{1,0:T(8,128)(2,1)} %copy-done.33, ...), custom_call_target="tpu_custom_call" | custom-call | flops 8153726976 | bytes 19759104 | tf_op jit(solution)/shard_map/pallas_call | solution.py:247
  317.5 10.6 %shard_map.294 = (f32[256,1152]{1,0:T(8,128)}, bf16[256,1152]{1,0:T(8,128)(2,1)}, f32[256,1024]{1,0:T(8,128)}, bf16[256,512]{1,0:T(8,128)(2,1)}, bf16[256,512]{1...) custom-call(s32[2]{0:T(128)} %pad_add_fusion.place_ref, bf16[256,1152]{1,0:T(8,128)(2,1)} %get-tuple-element.370.own_ref, ...), custom_call_target="tpu_custom_call" | custom-call | flops 2617245696 | bytes 9437184 | tf_op jit(solution)/shard_map/pallas_call | solution.py:247
  339.0 8.8 %shard_map.295 = (bf16[2,4,144,1024]{3,2,1,0:T(8,128)(2,1)}, bf16[2,4,144,1024]{3,2,1,0:T(8,128)(2,1)}, f32[256,1152]{1,0:T(8,128)}, f32[1,256]{1,0:T(1,128)}) custom-call(s32[2]{0:T(128)} %pad_add_fusion.place_ref, bf16[256,1152]{1,0:T(8,128)(2,1)} %get-tuple-element.407.d_attn_ref, bf16[256,1024]{1,0:T(8,128)(2,1)} %get-tuple-element.408.attended_ref, ...), custom_call_target="tpu_custom_call" | custom-call | flops 1811939328 | bytes 9437184 | tf_op jit(solution)/shard_map/pallas_call | solution.py:247
  347.8 5.5 %collective-permute-done.42.far_ref = bf16[256,512]{1,0:T(8,128)(2,1)S(1)} collective-permute-done((bf16[256,512]{1,0:T(8,128)(2,1)S(1)}, bf16[256,512]{1,0:T(8,128)(2,1)S(1)}, u32[]{:S(2)}, u32[]{:S(2)}) %collective-permute-start.42) | collective-permute-done | bytes 262176 | tf_op jit(solution)/shard_map/ppermute | solution.py:24
  359.8 7.5 %shard_map.296 = (bf16[4,144,640]{2,1,0:T(8,128)(2,1)}, bf16[4,144,640]{2,1,0:T(8,128)(2,1)}, f32[256,1152]{1,0:T(8,128)}) custom-call(s32[2]{0:T(128)} %pad_add_fusion.place_ref, f32[256,512]{1,0:T(8,128)} %get-tuple-element.392.near_ref, bf16[256,512]{1,0:T(8,128)(2,1)} %copy-done.52, bf16[256,512]{1,0:T(8,128)(2,1)} %copy-done.53, ...), custom_call_target="tpu_custom_call" | custom-call | flops 603979776 | bytes 8847360 | tf_op jit(solution)/shard_map/pallas_call | solution.py:247
  383.6 7.9 %collective-permute-done.52 = bf16[1,144,1728]{2,1,0:T(8,128)(2,1)S(1)} collective-permute-done((bf16[1,144,1728]{2,1,0:T(8,128)(2,1)S(1)}, bf16[1,144,1728]{2,1,0:T(8,128)(2,1)S(1)}, u32[]{:S(2)}, u32[]{:S(2)}) %collective-permute-start.52) | collective-permute-done | bytes 497696 | tf_op jit(solution)/shard_map/ppermute | solution.py:33
  392.2 11.0 %collective-permute-done.50 = bf16[2,144,1024]{2,1,0:T(8,128)(2,1)S(1)} collective-permute-done((bf16[2,144,1024]{2,1,0:T(8,128)(2,1)S(1)}, bf16[2,144,1024]{2,1,0:T(8,128)(2,1)S(1)}, u32[]{:S(2)}, u32[]{:S(2)}) %collective-permute-start.50) | collective-permute-done | bytes 589856 | tf_op jit(solution)/shard_map/ppermute | solution.py:33
  411.7 5.7 %collective-permute-done.57 = bf16[144,640]{1,0:T(8,128)(2,1)S(1)} collective-permute-done((bf16[144,640]{1,0:T(8,128)(2,1)S(1)}, bf16[144,640]{1,0:T(8,128)(2,1)S(1)}, u32[]{:S(2)}, u32[]{:S(2)}) %collective-permute-start.57) | collective-permute-done | bytes 184352 | tf_op jit(solution)/shard_map/ppermute | solution.py:33
  432.7 10.6 %collective-permute-done.59 = bf16[36,2688]{1,0:T(8,128)(2,1)S(1)} collective-permute-done((bf16[36,2688]{1,0:T(8,128)(2,1)S(1)}, bf16[36,2688]{1,0:T(8,128)(2,1)S(1)}, u32[]{:S(2)}, u32[]{:S(2)}) %collective-permute-start.59) | collective-permute-done | bytes 193568 | tf_op jit(solution)/shard_map/ppermute | solution.py:38
  (307 shorter events, 144.8 us)
Async XLA Ops:
  9.3 18.5 %collective-permute-start.1 = (bf16[36,2688]{1,0:T(8,128)(2,1)}, bf16[36,2688]{1,0:T(8,128)(2,1)S(1)}, u32[]{:S(2)}, u32[]{:S(2)}) collective-permute-start(bf16[36,2688]{1,0:T(8,128)(2,1)} %shard_map.280.refs_0_), channel_id=1, source_target_pairs={{0,2},{1,3},{2,0},{3,1},{4,6},{5,7},{6,4},{7,5},{8,10},{9,11},{10,... | collective-permute-start | bytes 580616 | tf_op jit(solution)/shard_map/ppermute | solution.py:38
  9.3 18.5 %collective-permute-start = (bf16[36,2688]{1,0:T(8,128)(2,1)}, bf16[36,2688]{1,0:T(8,128)(2,1)}, u32[]{:S(2)}, u32[]{:S(2)}) collective-permute-start(bf16[36,2688]{1,0:T(8,128)(2,1)} %shard_map.280.refs_0_), channel_id=1, source_target_pairs={{0,1},{1,2},{2,3},{3,0},{4,5},{5,6},{6,7},{7,4},{8,9},{9,10},{10,1... | collective-permute-start | bytes 580616 | tf_op jit(solution)/shard_map/ppermute | solution.py:38
  10.3 23.7 %collective-permute-start.4 = (bf16[2,144,1728]{2,1,0:T(8,128)(2,1)S(1)}, bf16[2,144,1728]{2,1,0:T(8,128)(2,1)S(1)}, u32[]{:S(2)}, u32[]{:S(2)}) collective-permute-start(bf16[2,144,1728]{2,1,0:T(8,128)(2,1)S(1)} %pad_maximum_fusion.3.refs_0_.refs_6_.refs_3_.refs_9_), channel_id=1, source_target_pairs={{0,16},{4,20},{8,24},{12,28},{16,0},{20,4},{24,8},{28,12},{1,17},{... | collective-permute-start | bytes 2985992 | tf_op jit(solution)/shard_map/ppermute | solution.py:33
  11.9 23.4 %collective-permute-start.3 = (bf16[2,144,1728]{2,1,0:T(8,128)(2,1)S(1)}, bf16[2,144,1728]{2,1,0:T(8,128)(2,1)S(1)}, u32[]{:S(2)}, u32[]{:S(2)}) collective-permute-start(bf16[2,144,1728]{2,1,0:T(8,128)(2,1)S(1)} %pad_maximum_fusion.3.refs_0_.refs_6_.refs_3_.refs_9_), channel_id=1, source_target_pairs={{0,8},{4,12},{8,0},{12,4},{16,24},{20,28},{24,16},{28,20},{1,9},{5... | collective-permute-start | bytes 2985992 | tf_op jit(solution)/shard_map/ppermute | solution.py:33
  39.2 21.6 %collective-permute-start.8 = (bf16[3,2,144,1728]{3,2,1,0:T(8,128)(2,1)S(1)}, bf16[3,2,144,1728]{3,2,1,0:T(8,128)(2,1)S(1)}, u32[]{:S(2)}, u32[]{:S(2)}) collective-permute-start(bf16[3,2,144,1728]{3,2,1,0:T(8,128)(2,1)S(1)} %pad_maximum_fusion), channel_id=1, source_target_pairs={{0,4},{4,0},{8,12},{12,8},{16,20},{20,16},{24,28},{28,24},{1,5},{5... | collective-permute-start | bytes 8957960 | tf_op jit(solution)/shard_map/ppermute | solution.py:33
  39.9 19.0 %collective-permute-start.6 = (bf16[144,2688]{1,0:T(8,128)(2,1)S(1)}, bf16[144,2688]{1,0:T(8,128)(2,1)S(1)}, u32[]{:S(2)}, u32[]{:S(2)}) collective-permute-start(bf16[144,2688]{1,0:T(8,128)(2,1)S(1)} %copy-done.14), channel_id=1, source_target_pairs={{0,16},{4,20},{8,24},{12,28},{16,0},{20,4},{24,8},{28,12},{1,17},{... | collective-permute-start | bytes 2322440 | tf_op jit(solution)/shard_map/ppermute | solution.py:33
  40.6 20.2 %collective-permute-start.5 = (bf16[144,2688]{1,0:T(8,128)(2,1)S(1)}, bf16[144,2688]{1,0:T(8,128)(2,1)S(1)}, u32[]{:S(2)}, u32[]{:S(2)}) collective-permute-start(bf16[144,2688]{1,0:T(8,128)(2,1)S(1)} %copy-done.14), channel_id=1, source_target_pairs={{0,8},{4,12},{8,0},{12,4},{16,24},{20,28},{24,16},{28,20},{1,9},{5... | collective-permute-start | bytes 2322440 | tf_op jit(solution)/shard_map/ppermute | solution.py:33
  62.4 17.4 %collective-permute-start.11 = (bf16[3,144,2688]{2,1,0:T(8,128)(2,1)S(1)}, bf16[3,144,2688]{2,1,0:T(8,128)(2,1)S(1)}, u32[]{:S(2)}, u32[]{:S(2)}) collective-permute-start(bf16[3,144,2688]{2,1,0:T(8,128)(2,1)S(1)} %pad_maximum_fusion.1), channel_id=1, source_target_pairs={{0,4},{4,0},{8,12},{12,8},{16,20},{20,16},{24,28},{28,24},{1,5},{5... | collective-permute-start | bytes 6967304 | tf_op jit(solution)/shard_map/ppermute | solution.py:33
  87.2 18.9 %collective-permute-start.14 = (bf16[2,80,1728]{2,1,0:T(8,128)(2,1)S(1)}, bf16[2,80,1728]{2,1,0:T(8,128)(2,1)}, u32[]{:S(2)}, u32[]{:S(2)}) collective-permute-start(bf16[2,80,1728]{2,1,0:T(8,128)(2,1)S(1)} %slice.173), channel_id=1, source_target_pairs={{0,8},{4,12},{8,0},{12,4},{16,24},{20,28},{24,16},{28,20},{1,9},{5... | collective-permute-start | bytes 1658888 | tf_op jit(solution)/shard_map/ppermute | solution.py:33
  107.5 17.6 %collective-permute-start.17 = (bf16[1,2,144,1728]{3,2,1,0:T(8,128)(2,1)S(1)}, bf16[1,2,144,1728]{3,2,1,0:T(8,128)(2,1)S(1)}, u32[]{:S(2)}, u32[]{:S(2)}) collective-permute-start(bf16[1,2,144,1728]{3,2,1,0:T(8,128)(2,1)S(1)} %bitcast.104), channel_id=1, source_target_pairs={{0,4},{4,0},{8,12},{12,8},{16,20},{20,16},{24,28},{28,24},{1,5},{5... | collective-permute-start | bytes 2985992 | tf_op jit(solution)/shard_map/ppermute | solution.py:33
  107.6 17.5 %collective-permute-start.16 = (bf16[256,1152]{1,0:T(8,128)(2,1)S(1)}, bf16[256,1152]{1,0:T(8,128)(2,1)S(1)}, u32[]{:S(2)}, u32[]{:S(2)}) collective-permute-start(bf16[256,1152]{1,0:T(8,128)(2,1)S(1)} %copy-done.32), channel_id=1, source_target_pairs={{0,1},{1,2},{2,3},{3,0},{4,5},{5,6},{6,7},{7,4},{8,9},{9,10},{10,1... | collective-permute-start | bytes 1769480 | tf_op jit(solution)/shard_map/ppermute | solution.py:38
  125.3 17.8 %collective-permute-start.23 = (bf16[3,144,1728]{2,1,0:T(8,128)(2,1)S(1)}, bf16[3,144,1728]{2,1,0:T(8,128)(2,1)S(1)}, u32[]{:S(2)}, u32[]{:S(2)}) collective-permute-start(bf16[3,144,1728]{2,1,0:T(8,128)(2,1)S(1)} %pad_maximum_fusion.2), channel_id=1, source_target_pairs={{0,4},{4,0},{8,12},{12,8},{16,20},{20,16},{24,28},{28,24},{1,5},{5... | collective-permute-start | bytes 4478984 | tf_op jit(solution)/shard_map/ppermute | solution.py:33
  125.4 17.7 %collective-permute-start.20 = (bf16[256,1152]{1,0:T(8,128)(2,1)S(1)}, bf16[256,1152]{1,0:T(8,128)(2,1)S(1)}, u32[]{:S(2)}, u32[]{:S(2)}) collective-permute-start(bf16[256,1152]{1,0:T(8,128)(2,1)S(1)} %collective-permute-done.16.rows_ref.refs_1_), channel_id=1, source_target_pairs={{0,1},{1,2},{2,3},{3,0},{4,5},{5,6},{6,7},{7,4},{8,9},{9,10},{10,1... | collective-permute-start | bytes 1769480 | tf_op jit(solution)/shard_map/ppermute | solution.py:38
  143.2 18.4 %collective-permute-start.24 = (bf16[256,1152]{1,0:T(8,128)(2,1)S(1)}, bf16[256,1152]{1,0:T(8,128)(2,1)S(1)}, u32[]{:S(2)}, u32[]{:S(2)}) collective-permute-start(bf16[256,1152]{1,0:T(8,128)(2,1)S(1)} %collective-permute-done.20.rows_ref.refs_2_), channel_id=1, source_target_pairs={{0,1},{1,2},{2,3},{3,0},{4,5},{5,6},{6,7},{7,4},{8,9},{9,10},{10,1... | collective-permute-start | bytes 1769480 | tf_op jit(solution)/shard_map/ppermute | solution.py:38
  151.7 21.7 %collective-permute-start.26 = (bf16[256,1152]{1,0:T(8,128)(2,1)}, bf16[256,1152]{1,0:T(8,128)(2,1)S(1)}, u32[]{:S(2)}, u32[]{:S(2)}) collective-permute-start(bf16[256,1152]{1,0:T(8,128)(2,1)} %shard_map.284), channel_id=1, source_target_pairs={{0,1},{1,2},{2,3},{3,0},{4,5},{5,6},{6,7},{7,4},{8,9},{9,10},{10,1... | collective-permute-start | bytes 1769480 | tf_op jit(solution)/shard_map/ppermute | solution.py:38
  174.6 16.7 %collective-permute-start.27 = (bf16[256,1152]{1,0:T(8,128)(2,1)S(1)}, bf16[256,1152]{1,0:T(8,128)(2,1)S(1)}, u32[]{:S(2)}, u32[]{:S(2)}) collective-permute-start(bf16[256,1152]{1,0:T(8,128)(2,1)S(1)} %add_convert_fusion.10), channel_id=1, source_target_pairs={{0,1},{1,2},{2,3},{3,0},{4,5},{5,6},{6,7},{7,4},{8,9},{9,10},{10,1... | collective-permute-start | bytes 1769480 | tf_op jit(solution)/shard_map/ppermute | solution.py:38
  213.0 18.3 %collective-permute-start.29 = (bf16[256,1152]{1,0:T(8,128)(2,1)}, bf16[256,1152]{1,0:T(8,128)(2,1)S(1)}, u32[]{:S(2)}, u32[]{:S(2)}) collective-permute-start(bf16[256,1152]{1,0:T(8,128)(2,1)} %get-tuple-element.321.back_ref.refs_21_), channel_id=1, source_target_pairs={{0,1},{1,2},{2,3},{3,0},{4,5},{5,6},{6,7},{7,4},{8,9},{9,10},{10,1... | collective-permute-start | bytes 1769480 | tf_op jit(solution)/shard_map/ppermute | solution.py:38
  213.0 29.3 %collective-permute-start.31 = (bf16[256,1152]{1,0:T(8,128)(2,1)}, bf16[256,1152]{1,0:T(8,128)(2,1)S(1)}, u32[]{:S(2)}, u32[]{:S(2)}) collective-permute-start(bf16[256,1152]{1,0:T(8,128)(2,1)} %get-tuple-element.321.back_ref.refs_21_), channel_id=1, source_target_pairs={{0,3},{1,0},{2,1},{3,2},{4,7},{5,4},{6,5},{7,6},{8,11},{9,8},{10,9... | collective-permute-start | bytes 1769480 | tf_op jit(solution)/shard_map/ppermute | solution.py:38
  231.3 22.1 %collective-permute-start.30 = (bf16[256,1152]{1,0:T(8,128)(2,1)S(1)}, bf16[256,1152]{1,0:T(8,128)(2,1)S(1)}, u32[]{:S(2)}, u32[]{:S(2)}) collective-permute-start(bf16[256,1152]{1,0:T(8,128)(2,1)S(1)} %collective-permute-done.29.back_ref.refs_22_), channel_id=1, source_target_pairs={{0,1},{1,2},{2,3},{3,0},{4,5},{5,6},{6,7},{7,4},{8,9},{9,10},{10,1... | collective-permute-start | bytes 1769480 | tf_op jit(solution)/shard_map/ppermute | solution.py:38
  253.4 19.9 %collective-permute-start.32 = (bf16[256,1152]{1,0:T(8,128)(2,1)}, bf16[256,1152]{1,0:T(8,128)(2,1)S(1)}, u32[]{:S(2)}, u32[]{:S(2)}) collective-permute-start(bf16[256,1152]{1,0:T(8,128)(2,1)} %get-tuple-element.336), channel_id=1, source_target_pairs={{0,1},{1,2},{2,3},{3,0},{4,5},{5,6},{6,7},{7,4},{8,9},{9,10},{10,1... | collective-permute-start | bytes 1769480 | tf_op jit(solution)/shard_map/ppermute | solution.py:38
  273.4 18.9 %collective-permute-start.34 = (bf16[4,144,1728]{2,1,0:T(8,128)(2,1)}, bf16[4,144,1728]{2,1,0:T(8,128)(2,1)S(1)}, u32[]{:S(2)}, u32[]{:S(2)}) collective-permute-start(bf16[4,144,1728]{2,1,0:T(8,128)(2,1)} %get-tuple-element.357), channel_id=1, source_target_pairs={{0,4},{4,0},{8,12},{12,8},{16,20},{20,16},{24,28},{28,24},{1,5},{5... | collective-permute-start | bytes 5971976 | tf_op jit(solution)/shard_map/ppermute | solution.py:33
  274.7 17.6 %collective-permute-start.33 = (bf16[256,1152]{1,0:T(8,128)(2,1)S(1)}, bf16[256,1152]{1,0:T(8,128)(2,1)S(1)}, u32[]{:S(2)}, u32[]{:S(2)}) collective-permute-start(bf16[256,1152]{1,0:T(8,128)(2,1)S(1)} %add_convert_fusion.8), channel_id=1, source_target_pairs={{0,1},{1,2},{2,3},{3,0},{4,5},{5,6},{6,7},{7,4},{8,9},{9,10},{10,1... | collective-permute-start | bytes 1769480 | tf_op jit(solution)/shard_map/ppermute | solution.py:38
  293.4 19.3 %collective-permute-start.35 = (bf16[256,1152]{1,0:T(8,128)(2,1)S(1)}, bf16[256,1152]{1,0:T(8,128)(2,1)S(1)}, u32[]{:S(2)}, u32[]{:S(2)}) collective-permute-start(bf16[256,1152]{1,0:T(8,128)(2,1)S(1)} %add_convert_fusion.7), channel_id=1, source_target_pairs={{0,1},{1,2},{2,3},{3,0},{4,5},{5,6},{6,7},{7,4},{8,9},{9,10},{10,1... | collective-permute-start | bytes 1769480 | tf_op jit(solution)/shard_map/ppermute | solution.py:38
  295.3 17.4 %collective-permute-start.37 = (bf16[144,1728]{1,0:T(8,128)(2,1)S(1)}, bf16[144,1728]{1,0:T(8,128)(2,1)S(1)}, u32[]{:S(2)}, u32[]{:S(2)}) collective-permute-start(bf16[144,1728]{1,0:T(8,128)(2,1)S(1)} %get-tuple-element.489), channel_id=1, source_target_pairs={{0,16},{4,20},{8,24},{12,28},{16,0},{20,4},{24,8},{28,12},{1,17},{... | collective-permute-start | bytes 1493000 | tf_op jit(solution)/shard_map/ppermute | solution.py:33
  296.0 16.7 %collective-permute-start.36 = (bf16[144,1728]{1,0:T(8,128)(2,1)S(1)}, bf16[144,1728]{1,0:T(8,128)(2,1)S(1)}, u32[]{:S(2)}, u32[]{:S(2)}) collective-permute-start(bf16[144,1728]{1,0:T(8,128)(2,1)S(1)} %get-tuple-element.490), channel_id=1, source_target_pairs={{0,8},{4,12},{8,0},{12,4},{16,24},{20,28},{24,16},{28,20},{1,9},{5... | collective-permute-start | bytes 1493000 | tf_op jit(solution)/shard_map/ppermute | solution.py:33
  331.9 21.4 %collective-permute-start.44 = (bf16[1,144,1728]{2,1,0:T(8,128)(2,1)}, bf16[1,144,1728]{2,1,0:T(8,128)(2,1)S(1)}, u32[]{:S(2)}, u32[]{:S(2)}) collective-permute-start(bf16[1,144,1728]{2,1,0:T(8,128)(2,1)} %get-tuple-element.496), channel_id=1, source_target_pairs={{0,8},{4,12},{8,0},{12,4},{16,24},{20,28},{24,16},{28,20},{1,9},{5... | collective-permute-start | bytes 1493000 | tf_op jit(solution)/shard_map/ppermute | solution.py:33
  335.0 18.4 %collective-permute-start.43 = (bf16[1,144,1728]{2,1,0:T(8,128)(2,1)S(1)}, bf16[1,144,1728]{2,1,0:T(8,128)(2,1)S(1)}, u32[]{:S(2)}, u32[]{:S(2)}) collective-permute-start(bf16[1,144,1728]{2,1,0:T(8,128)(2,1)S(1)} %get-tuple-element.487), channel_id=1, source_target_pairs={{0,16},{4,20},{8,24},{12,28},{16,0},{20,4},{24,8},{28,12},{1,17},{... | collective-permute-start | bytes 1493000 | tf_op jit(solution)/shard_map/ppermute | solution.py:33
  354.4 19.6 %collective-permute-start.45 = (bf16[2,4,144,1024]{3,2,1,0:T(8,128)(2,1)}, bf16[2,4,144,1024]{3,2,1,0:T(8,128)(2,1)S(1)}, u32[]{:S(2)}, u32[]{:S(2)}) collective-permute-start(bf16[2,4,144,1024]{3,2,1,0:T(8,128)(2,1)} %get-tuple-element.431), channel_id=1, source_target_pairs={{0,4},{4,0},{8,12},{12,8},{16,20},{20,16},{24,28},{28,24},{1,5},{5... | collective-permute-start | bytes 7077896 | tf_op jit(solution)/shard_map/ppermute | solution.py:33
  377.8 25.4 %collective-permute-start.48 = (bf16[4,144,640]{2,1,0:T(8,128)(2,1)S(1)}, bf16[4,144,640]{2,1,0:T(8,128)(2,1)S(1)}, u32[]{:S(2)}, u32[]{:S(2)}) collective-permute-start(bf16[4,144,640]{2,1,0:T(8,128)(2,1)S(1)} %copy-done.61), channel_id=1, source_target_pairs={{0,4},{4,0},{8,12},{12,8},{16,20},{20,16},{24,28},{28,24},{1,5},{5... | collective-permute-start | bytes 2211848 | tf_op jit(solution)/shard_map/ppermute | solution.py:33
  378.2 25.0 %collective-permute-start.50 = (bf16[2,144,1024]{2,1,0:T(8,128)(2,1)S(1)}, bf16[2,144,1024]{2,1,0:T(8,128)(2,1)S(1)}, u32[]{:S(2)}, u32[]{:S(2)}) collective-permute-start(bf16[2,144,1024]{2,1,0:T(8,128)(2,1)S(1)} %get-tuple-element.492), channel_id=1, source_target_pairs={{0,8},{4,12},{8,0},{12,4},{16,24},{20,28},{24,16},{28,20},{1,9},{5... | collective-permute-start | bytes 1769480 | tf_op jit(solution)/shard_map/ppermute | solution.py:33
  379.7 23.5 %collective-permute-start.49 = (bf16[2,144,1024]{2,1,0:T(8,128)(2,1)S(1)}, bf16[2,144,1024]{2,1,0:T(8,128)(2,1)S(1)}, u32[]{:S(2)}, u32[]{:S(2)}) collective-permute-start(bf16[2,144,1024]{2,1,0:T(8,128)(2,1)S(1)} %get-tuple-element.483), channel_id=1, source_target_pairs={{0,16},{4,20},{8,24},{12,28},{16,0},{20,4},{24,8},{28,12},{1,17},{... | collective-permute-start | bytes 1769480 | tf_op jit(solution)/shard_map/ppermute | solution.py:33
  426.4 16.9 %collective-permute-start.59 = (bf16[36,2688]{1,0:T(8,128)(2,1)S(1)}, bf16[36,2688]{1,0:T(8,128)(2,1)S(1)}, u32[]{:S(2)}, u32[]{:S(2)}) collective-permute-start(bf16[36,2688]{1,0:T(8,128)(2,1)S(1)} %get-tuple-element.500), channel_id=1, source_target_pairs={{0,2},{1,3},{2,0},{3,1},{4,6},{5,7},{6,4},{7,5},{8,10},{9,11},{10,... | collective-permute-start | bytes 580616 | tf_op jit(solution)/shard_map/ppermute | solution.py:38
  (94 other events, 784.2 us)
